TPU v7x, 256 devices: a whole 4x4x8 slice. The times are simulated.
256 devices in a mesh: resp: 2 (over core), ctx: 32 (over z_lo, y, x), tp: 4 (over z_hi).
Axes of the slice: x: 4, y: 4, z: 8 (z_hi: 4, z_lo: 2; z = z_hi * 2 + z_lo), core: 2. Of those that a mesh axis runs over, the one named last changes fastest.
Arguments:
- q_prompt: bfloat16 [4096, 4096], P(('resp', 'ctx'), 'tp'), may hold values from -4.5 to 4.5
- k_prompt: bfloat16 [4096, 512], P(('resp', 'ctx'), 'tp'), may hold values from -4.5 to 4.5
- v_prompt: bfloat16 [4096, 512], P(('resp', 'ctx'), 'tp'), may hold values from -4.5 to 4.5
- doc_ids: int32 [4096], P(('resp', 'ctx')), may hold values from 0 to 3, never falling along the last dimension, each value on 1 to 2048 neighbouring positions
- q_resp: bfloat16 [2, 2048, 4096], P('resp', 'ctx', 'tp'), may hold values from -4.5 to 4.5
- k_resp: bfloat16 [2, 2048, 512], P('resp', 'ctx', 'tp'), may hold values from -4.5 to 4.5
- v_resp: bfloat16 [2, 2048, 512], P('resp', 'ctx', 'tp'), may hold values from -4.5 to 4.5
- resp_len: int32 [2], replicated, may hold values from 512 to 2048, as said below
- out_weight: bfloat16 [4096, 5120], P('tp'), may hold values from -0.09375 to 0.09375
- grad_prompt: bfloat16 [4096, 5120], P(('resp', 'ctx'), 'tp'), may hold values from -6 to 6
- grad_resp: bfloat16 [2, 2048, 5120], P('resp', 'ctx', 'tp'), may hold values from -6 to 6
Outputs:
- out_prompt: bfloat16 [4096, 5120], P(('resp', 'ctx'), 'tp')
- out_resp: bfloat16 [2, 2048, 5120], P('resp', 'ctx', 'tp')
- grad_q_prompt: bfloat16 [4096, 4096], P(('resp', 'ctx'), 'tp')
- grad_k_prompt: bfloat16 [4096, 512], P(('resp', 'ctx'), 'tp')
- grad_v_prompt: bfloat16 [4096, 512], P(('resp', 'ctx'), 'tp')
- grad_q_resp: bfloat16 [2, 2048, 4096], P('resp', 'ctx', 'tp')
- grad_k_resp: bfloat16 [2, 2048, 512], P('resp', 'ctx', 'tp')
- grad_v_resp: bfloat16 [2, 2048, 512], P('resp', 'ctx', 'tp')
Inputs may be any that keep to these rules, and one draw needn't show every extreme that they name: `resp_len`: one of the two responses has all 2048 tokens live.
All inputs are finite; a program needn't handle non-finite values.
Results may differ from a plain program's by a relative error of at most 0.028.
Values may be sent and summed in bfloat16 or wider, within the bound.
No kernel may reach another device: no remote copies, remote signals or barrier semaphores. Data moves between devices by JAX's collectives and lax.ppermute only.
A program may use at most 128 MiB of HBM per device.

v0:
```python
import math

import jax
import jax.numpy as jnp
from jax import lax
from jax.sharding import PartitionSpec as P

HQ = 32
HK = 4
DH = 128


NEGATIVE = -1e30


def forward_keys(queries, keys, values, visible_fn, carry_state, score_scale):
    total_keys = keys.shape[0]
    heads_kv = queries.shape[1]
    block_width = math.gcd(512, total_keys)
    blocks = total_keys // block_width
    key_blocks = keys.reshape(blocks, block_width, heads_kv, -1)
    value_blocks = values.reshape(blocks, block_width, heads_kv, -1)

    def forward_block_step(current_state, block_item):
        block_index, key_block, value_block = block_item
        first_key = block_index * block_width
        running_max, total, accum = current_state
        scores = (
            jnp.einsum("nhgd,khd->nhgk", queries, key_block, preferred_element_type=jnp.float32)
            * score_scale
        )
        visible = visible_fn(first_key, block_width)[:, None, None, :]
        new_max = jnp.maximum(running_max, jnp.max(jnp.where(visible, scores, NEGATIVE), axis=-1))
        weights = jnp.where(visible, jnp.exp(scores - new_max[..., None]), 0.0)
        factor = jnp.exp(running_max - new_max)
        total = total * factor + jnp.sum(weights, axis=-1)
        accum = accum * factor[..., None] + jnp.einsum(
            "nhgk,khd->nhgd",
            weights.astype(jnp.bfloat16),
            value_block,
            preferred_element_type=jnp.float32,
        )
        current_state = (new_max, total, accum)
        return (current_state, None)

    carry_state, unused = lax.scan(
        forward_block_step,
        carry_state,
        (jnp.arange(blocks, dtype=jnp.int32), key_blocks, value_blocks),
    )
    return carry_state


def backward_keys(queries, d_attended, log_total, row_delta, keys, values, visible_fn, score_scale):
    total_keys = keys.shape[0]
    heads_kv = queries.shape[1]
    block_width = math.gcd(512, total_keys)
    blocks = total_keys // block_width
    key_blocks = keys.reshape(blocks, block_width, heads_kv, -1)
    value_blocks = values.reshape(blocks, block_width, heads_kv, -1)

    def backward_block_step(grad_queries, block_item):
        block_index, key_block, value_block = block_item
        first_key = block_index * block_width
        current = grad_queries
        scores = (
            jnp.einsum("nhgd,khd->nhgk", queries, key_block, preferred_element_type=jnp.float32)
            * score_scale
        )
        visible = visible_fn(first_key, block_width)[:, None, None, :]
        probs = jnp.where(visible, jnp.exp(scores - log_total[..., None]), 0.0)
        grad_values = jnp.einsum(
            "nhgk,nhgd->khd",
            probs.astype(jnp.bfloat16),
            d_attended,
            preferred_element_type=jnp.float32,
        )
        dprobs = jnp.einsum(
            "nhgd,khd->nhgk", d_attended, value_block, preferred_element_type=jnp.float32
        )
        score_grad = (probs * (dprobs - row_delta[..., None])).astype(jnp.bfloat16)
        current = current + score_scale * jnp.einsum(
            "nhgk,khd->nhgd", score_grad, key_block, preferred_element_type=jnp.float32
        )
        grad_keys = score_scale * jnp.einsum(
            "nhgk,nhgd->khd", score_grad, queries, preferred_element_type=jnp.float32
        )
        return (current, (grad_keys, grad_values))

    start_grads = jnp.zeros(queries.shape, jnp.float32)
    grad_queries, block_grads = lax.scan(
        backward_block_step,
        start_grads,
        (jnp.arange(blocks, dtype=jnp.int32), key_blocks, value_blocks),
    )
    return (
        grad_queries,
        block_grads[0].reshape(total_keys, -1),
        block_grads[1].reshape(total_keys, -1),
    )


def body(
    q_prompt,
    k_prompt,
    v_prompt,
    doc_ids,
    q_resp,
    k_resp,
    v_resp,
    resp_len,
    out_weight,
    grad_prompt,
    grad_resp,
):
    prompt_rows = q_prompt.shape[0]
    resp_rows = q_resp.shape[1]
    all_rows = prompt_rows + resp_rows
    heads_kv = k_prompt.shape[1] // DH
    group_size = HQ // HK
    score_scale = 1.0 / math.sqrt(DH)
    keys_prompt, values_prompt, docs_all = (
        lax.all_gather(k_prompt, ("resp", "ctx"), axis=0, tiled=True),
        lax.all_gather(v_prompt, ("resp", "ctx"), axis=0, tiled=True),
        lax.all_gather(doc_ids, ("resp", "ctx"), axis=0, tiled=True),
    )
    keys_resp, values_resp = (
        lax.all_gather(k_resp, "ctx", axis=1, tiled=True),
        lax.all_gather(v_resp, "ctx", axis=1, tiled=True),
    )
    keys_resp = keys_resp[0]
    values_resp = values_resp[0]
    prompt_first = lax.axis_index(("resp", "ctx")) * prompt_rows
    resp_first = lax.axis_index("ctx") * resp_rows
    live_len = lax.dynamic_index_in_dim(resp_len, lax.axis_index("resp"), 0, keepdims=False)
    prompt_pos = prompt_first + jnp.arange(prompt_rows, dtype=jnp.int32)
    resp_pos = resp_first + jnp.arange(resp_rows, dtype=jnp.int32)

    def upper_visible(first_key, block_width):
        key_pos = first_key + jnp.arange(block_width, dtype=jnp.int32)
        key_docs = lax.dynamic_slice_in_dim(docs_all, first_key, block_width)
        return (key_pos[None, :] <= prompt_pos[:, None]) & (key_docs[None, :] == doc_ids[:, None])

    def prompt_visible(first_key, block_width):
        return jnp.concatenate(
            [upper_visible(first_key, block_width), jnp.ones((resp_rows, block_width), bool)],
            axis=0,
        )

    def resp_visible(first_key, block_width):
        key_pos = first_key + jnp.arange(block_width, dtype=jnp.int32)
        return (key_pos[None, :] <= resp_pos[:, None]) & (key_pos[None, :] < live_len)

    queries = jnp.concatenate([q_prompt, q_resp[0]], axis=0).reshape(
        all_rows, heads_kv, group_size, DH
    )
    kp_heads = keys_prompt.reshape(-1, heads_kv, DH)
    vp_heads = values_prompt.reshape(-1, heads_kv, DH)
    kr_heads = keys_resp.reshape(-1, heads_kv, DH)
    vr_heads = values_resp.reshape(-1, heads_kv, DH)
    start_state = (
        jnp.full((all_rows, heads_kv, group_size), NEGATIVE, jnp.float32),
        jnp.zeros((all_rows, heads_kv, group_size), jnp.float32),
        jnp.zeros((all_rows, heads_kv, group_size, DH), jnp.float32),
    )
    after_prompt = forward_keys(
        queries, kp_heads, vp_heads, prompt_visible, start_state, score_scale
    )
    resp_state = (
        after_prompt[0][prompt_rows:],
        after_prompt[1][prompt_rows:],
        after_prompt[2][prompt_rows:],
    )
    after_resp = forward_keys(
        queries[prompt_rows:], kr_heads, vr_heads, resp_visible, resp_state, score_scale
    )
    running_max = jnp.concatenate([after_prompt[0][:prompt_rows], after_resp[0]], axis=0)
    total = jnp.concatenate([after_prompt[1][:prompt_rows], after_resp[1]], axis=0)
    accum = jnp.concatenate([after_prompt[2][:prompt_rows], after_resp[2]], axis=0)
    attended = (accum / total[..., None]).astype(jnp.bfloat16)
    log_total = running_max + jnp.log(total)
    partial_out = jnp.dot(
        attended.reshape(all_rows, -1), out_weight, preferred_element_type=jnp.float32
    )
    outputs = lax.psum_scatter(
        partial_out.astype(jnp.bfloat16), "tp", scatter_dimension=1, tiled=True
    )
    cotangent = jnp.concatenate([grad_prompt, grad_resp[0]], axis=0)
    whole_cotangent = lax.all_gather(cotangent, "tp", axis=1, tiled=True)
    d_attended = lax.dot_general(
        whole_cotangent, out_weight, (((1,), (1,)), ((), ())), preferred_element_type=jnp.float32
    ).astype(jnp.bfloat16)
    d_attended = d_attended.reshape(all_rows, heads_kv, group_size, DH)
    row_delta = jnp.sum(d_attended.astype(jnp.float32) * attended.astype(jnp.float32), axis=-1)
    gq_all, gk_prompt_terms, gv_prompt_terms = backward_keys(
        queries, d_attended, log_total, row_delta, kp_heads, vp_heads, prompt_visible, score_scale
    )
    gq_resp, gk_resp_terms, gv_resp_terms = backward_keys(
        queries[prompt_rows:],
        d_attended[prompt_rows:],
        log_total[prompt_rows:],
        row_delta[prompt_rows:],
        kr_heads,
        vr_heads,
        resp_visible,
        score_scale,
    )
    grad_queries = jnp.concatenate([gq_all[:prompt_rows], gq_all[prompt_rows:] + gq_resp], axis=0)
    grad_queries = grad_queries.reshape(all_rows, -1).astype(jnp.bfloat16)
    grad_k_prompt, grad_v_prompt = (
        lax.psum_scatter(gk_prompt_terms, ("resp", "ctx"), scatter_dimension=0, tiled=True),
        lax.psum_scatter(gv_prompt_terms, ("resp", "ctx"), scatter_dimension=0, tiled=True),
    )
    grad_k_resp, grad_v_resp = (
        lax.psum_scatter(
            gk_resp_terms.astype(jnp.bfloat16), "ctx", scatter_dimension=0, tiled=True
        ).astype(jnp.float32),
        lax.psum_scatter(
            gv_resp_terms.astype(jnp.bfloat16), "ctx", scatter_dimension=0, tiled=True
        ).astype(jnp.float32),
    )
    return (
        outputs[:prompt_rows],
        outputs[prompt_rows:][None],
        grad_queries[:prompt_rows],
        grad_k_prompt.astype(jnp.bfloat16),
        grad_v_prompt.astype(jnp.bfloat16),
        grad_queries[prompt_rows:][None],
        grad_k_resp.astype(jnp.bfloat16)[None],
        grad_v_resp.astype(jnp.bfloat16)[None],
    )


def solution(mesh):
    in_specs = (
        P(("resp", "ctx"), "tp"),
        P(("resp", "ctx"), "tp"),
        P(("resp", "ctx"), "tp"),
        P(("resp", "ctx")),
        P("resp", "ctx", "tp"),
        P("resp", "ctx", "tp"),
        P("resp", "ctx", "tp"),
        P(),
        P("tp", None),
        P(("resp", "ctx"), "tp"),
        P("resp", "ctx", "tp"),
    )
    out_specs = (
        P(("resp", "ctx"), "tp"),
        P("resp", "ctx", "tp"),
        P(("resp", "ctx"), "tp"),
        P(("resp", "ctx"), "tp"),
        P(("resp", "ctx"), "tp"),
        P("resp", "ctx", "tp"),
        P("resp", "ctx", "tp"),
        P("resp", "ctx", "tp"),
    )
    return jax.shard_map(body, mesh=mesh, in_specs=in_specs, out_specs=out_specs, check_vma=False)
```

profile of v0, /device:TPU:32, one launch (start us, length us, event | category | flops | bytes accessed | tf_op | source)
XLA Modules:
  0.0 1591.0 jit_solution(4853131537111025484)
XLA Ops:
  7.3 1.8 pad_maximum_fusion
  14.7 307.9 %all-reduce.2 = s32[4096]{0:T(1024)S(1)} all-reduce(s32[4096]{0:T(1024)S(1)} %dynamic-update-slice), channel_id=1, replica_groups=mesh['resp'=2,'ctx'=32,'tp'=4] {'resp','ctx'}, use_global_device_ids=true, to_apply=%add.2 | all-reduce | flops 4096 | bytes 32768
  322.6 78.2 %all_gather.21 = bf16[1,2048,128]{2,1,0:T(8,128)(2,1)S(1)} all-gather(bf16[1,64,128]{2,1,0:T(8,128)(2,1)S(1)} %copy-done.7), channel_id=1, replica_groups=mesh['resp'=2,'ctx'=32,'tp'=4] {'ctx'}, dimensions={1}, use_global_device_ids=true | all-gather | bytes 540672 | tf_op jit(solution)/shard_map/all_gather | solution.py:128
  400.8 80.0 %all_gather.22 = bf16[1,2048,128]{2,1,0:T(8,128)(2,1)S(1)} all-gather(bf16[1,64,128]{2,1,0:T(8,128)(2,1)S(1)} %copy-done.8), channel_id=1, replica_groups=mesh['resp'=2,'ctx'=32,'tp'=4] {'ctx'}, dimensions={1}, use_global_device_ids=true | all-gather | bytes 540672 | tf_op jit(solution)/shard_map/all_gather | solution.py:129
  480.8 8.0 convolution_convert_fusion.1
  489.8 40.0 %while.61 = (s32[]{:T(128)}, f32[128,1,8]{0,2,1:T(8,128)S(1)}, f32[128,1,8]{0,2,1:T(8,128)S(1)}, f32[128,1,8,128]{0,3,2,1:T(8,128)S(1)}, s32[8]{0:T(128)S(1)}, /...) while((s32[]{:T(128)}, f32[128,1,8]{0,2,1:T(8,128)S(1)}, ...), condition=%wide.region_3.4_spmd.clone, body=%wide.region_0.3_spmd.clone.sunk | while | flops 274700864 | bytes 8268792 | solution.py:46
  491.4 1.4 fusion.167
  493.2 1.5 fusion.170
  496.4 1.4 fusion.167
  498.2 1.5 fusion.170
  501.4 1.4 fusion.167
  503.2 1.5 fusion.170
  506.4 1.4 fusion.167
  508.2 1.5 fusion.170
  511.4 1.4 fusion.167
  513.2 1.5 fusion.170
  516.4 1.4 fusion.167
  518.2 1.5 fusion.170
  521.4 1.4 fusion.167
  523.2 1.5 fusion.170
  526.4 1.4 fusion.167
  528.2 1.5 fusion.170
  531.4 1.2 copy.37
  533.2 12.9 while.60
  547.3 1.4 maximum_add_fusion
  550.7 6.9 convolution_convert_fusion
  557.7 1.2 multiply_reduce_fusion
  558.9 69.9 %while.62 = (s32[]{:T(128)}, f32[128,1,8,128]{0,3,2,1:T(8,128)S(1)}, f32[8,512,1,128]{3,1,2,0:T(8,128)}, f32[8,512,1,128]{3,1,2,0:T(8,128)}, bf16[8,512,1,128]{3...) while((s32[]{:T(128)}, ...), condition=%wide.region_11.12_spmd.clone, body=%wide.region_10.11_spmd.clone.sunk | while | flops 675316288 | bytes 12667930 | solution.py:91
  561.2 1.5 bitcast_select_fusion.3
  562.7 1.3 fusion.181
  565.2 1.3 fusion.182
  569.9 1.5 bitcast_select_fusion.3
  571.4 1.3 fusion.181
  573.9 1.3 fusion.182
  578.6 1.5 bitcast_select_fusion.3
  580.1 1.3 fusion.181
  581.5 1.2 fusion.184
  582.7 1.3 fusion.182
  587.4 1.5 bitcast_select_fusion.3
  588.9 1.3 fusion.181
  590.2 1.2 fusion.184
  591.4 1.3 fusion.182
  596.1 1.5 bitcast_select_fusion.3
  597.6 1.3 fusion.181
  600.1 1.3 fusion.182
  601.4 1.2 fusion.183
  604.9 1.5 bitcast_select_fusion.3
  606.4 1.3 fusion.181
  608.9 1.3 fusion.182
  613.6 1.5 bitcast_select_fusion.3
  615.1 1.3 fusion.181
  617.6 1.3 fusion.182
  622.3 1.5 bitcast_select_fusion.3
  623.8 1.3 fusion.181
  626.3 1.3 fusion.182
  627.6 1.2 fusion.183
  629.5 18.8 %while.63 = (s32[]{:T(128)}, f32[64,1,8,128]{3,0,2,1:T(8,128)S(1)}, bf16[4,512,1,128]{3,1,2,0:T(8,128)(2,1)}, bf16[4,512,1,128]{3,1,2,0:T(8,128)(2,1)S(1)}, bf16...) while((s32[]{:T(128)}, f32[64,1,8,128]{3,0,2,1:T(8,128)S(1)}, ...), condition=%wide.region_15.16_spmd.clone, body=%wide.region_14.15_spmd.clone.sunk | while | flops 337708608 | bytes 10958619 | solution.py:91
  651.8 1.7 slice_bitcast_fusion
  653.5 290.0 %reduce-scatter.8.cloned.1.call-done = f32[64,128]{1,0:T(8,128)} async-done(((f32[4096,128]{1,0:T(8,128)}), f32[64,128]{1,0:T(8,128)}) %reduce-scatter.8.cloned.1.call-update) | async-done | bytes 32784 | tf_op jit(solution)/shard_map/reduce_scatter | solution.py:211
  943.5 1.4 convert_element_type.91
  944.9 315.0 %reduce-scatter.10.cloned.1.call-done = f32[64,128]{1,0:T(8,128)} async-done(((f32[4096,128]{1,0:T(8,128)}), f32[64,128]{1,0:T(8,128)}) %reduce-scatter.10.cloned.1.call-update) | async-done | bytes 32784 | tf_op jit(solution)/shard_map/reduce_scatter | solution.py:212
  1259.9 1.4 convert_element_type.92
  1261.3 160.8 %reduce-scatter.14.cloned.1.call-done = bf16[64,128]{1,0:T(8,128)(2,1)} async-done(((bf16[2048,128]{1,0:T(8,128)(2,1)}), bf16[64,128]{1,0:T(8,128)(2,1)}) %reduce-scatter.14.cloned.1.call-update) | async-done | bytes 16400 | tf_op jit(solution)/shard_map/reduce_scatter | solution.py:218
  1422.1 162.1 %reduce-scatter.12.cloned.1.call-done = bf16[64,128]{1,0:T(8,128)(2,1)} async-done(((bf16[2048,128]{1,0:T(8,128)(2,1)}), bf16[64,128]{1,0:T(8,128)(2,1)}) %reduce-scatter.12.cloned.1.call-update) | async-done | bytes 16400 | tf_op jit(solution)/shard_map/reduce_scatter | solution.py:215
  (326 shorter events, 79.0 us)
Async XLA Ops:
  7.2 5.5 copy-start.12
  7.2 6.7 copy-start.11
  7.2 7.3 copy-start.5
  7.2 315.4 %copy-start.7 = (bf16[1,64,128]{2,1,0:T(8,128)(2,1)S(1)}, bf16[1,64,128]{2,1,0:T(8,128)(2,1)}, u32[]{:S(2)}) copy-start(bf16[1,64,128]{2,1,0:T(8,128)(2,1)} %param.24) | copy-start | bytes 49156
  7.2 393.6 %copy-start.8 = (bf16[1,64,128]{2,1,0:T(8,128)(2,1)S(1)}, bf16[1,64,128]{2,1,0:T(8,128)(2,1)}, u32[]{:S(2)}) copy-start(bf16[1,64,128]{2,1,0:T(8,128)(2,1)} %param.25) | copy-start | bytes 49156
  7.2 473.5 %all-gather.8.cloned.1.call-start = ((), (), s32[]{:S(2)}) async-start(), calls=%async_computation.8 | async-start | bytes 1638400 | tf_op jit(solution)/shard_map/all_gather | solution.py:189
  9.1 480.7 %all-gather.4.cloned.1.call-start = ((), (), s32[]{:S(2)}) async-start(), calls=%async_computation.5 | async-start | bytes 1064960 | tf_op jit(solution)/shard_map/all_gather | solution.py:123
  9.8 480.0 %all-gather.6.cloned.1.call-start = ((), (), s32[]{:S(2)}) async-start(), calls=%async_computation.6 | async-start | bytes 1064960 | tf_op jit(solution)/shard_map/all_gather | solution.py:124
  10.5 641.2 %reduce-scatter.6.cloned.1.call-start = ((), (), s32[]{:S(2)}) async-start(), calls=%async_computation.7 | async-start | bytes 1638400 | tf_op jit(solution)/shard_map/reduce_scatter | solution.py:185
  529.8 0.6 copy-start.4
  533.2 14.1 copy-start.10
  550.7 7.0 copy-start
  557.6 1.3 copy-start.6
  557.6 1.3 copy-start.9
  557.6 385.9 %reduce-scatter.8.cloned.1.call-start = ((), (), s32[]{:S(2)}) async-start(), calls=%async_computation.9 | async-start | bytes 2129920 | tf_op jit(solution)/shard_map/reduce_scatter | solution.py:211
  628.8 631.1 %reduce-scatter.10.cloned.1.call-start = ((), (), s32[]{:S(2)}) async-start(), calls=%async_computation.10 | async-start | bytes 2129920 | tf_op jit(solution)/shard_map/reduce_scatter | solution.py:212
  629.4 792.7 %reduce-scatter.14.cloned.1.call-start = ((), (), s32[]{:S(2)}) async-start(), calls=%async_computation.12 | async-start | bytes 540672 | tf_op jit(solution)/shard_map/reduce_scatter | solution.py:218
  631.9 1.1 copy-start.2
  633.4 0.8 copy-start.3
  636.6 1.1 copy-start.2
  638.1 0.8 copy-start.3
  641.3 1.1 copy-start.2
  642.8 0.8 copy-start.3
  646.0 1.1 copy-start.2
  647.5 0.8 copy-start.3
  648.3 0.8 copy-start.1
  649.1 935.0 %reduce-scatter.12.cloned.1.call-start = ((), (), s32[]{:S(2)}) async-start(), calls=%async_computation.11 | async-start | bytes 540672 | tf_op jit(solution)/shard_map/reduce_scatter | solution.py:215
Sparse Core Ops, SparseCore 0:
  9.9 38.3 all-gather.7
  50.1 104.6 all-gather.3
  156.7 102.7 all-gather.5
  557.7 33.6 reduce-scatter.5
  629.0 314.5 reduce-scatter.7
  946.0 313.8 reduce-scatter.9
  1263.0 159.0 reduce-scatter.13
  1425.3 158.7 reduce-scatter.11
where the time goes:
time: 1590 us
  waiting for transfers between devices  930 us (58%)
  blocking collectives  466 us (29%)
  matrix products  99.8 us (6%)
  local copies, waits for them, and re-layouts  40.2 us (3%)
  other arithmetic  21.8 us (1%)
  loops' own time  17.3 us (1%)
    reduce_scatter x1, waiting for transfers between devices, body(): lax.psum_scatter(gv_prompt_terms, ('resp', 'ctx'), scatter_dimension=0, t...  315 us
    unnamed x1, blocking collectives  308 us
    reduce_scatter x1, waiting for transfers between devices, body(): lax.psum_scatter(gk_prompt_terms, ('resp', 'ctx'), scatter_dimension=0, t...  290 us
    reduce_scatter x1, waiting for transfers between devices, body(): lax.psum_scatter(gk_resp_terms.astype(jnp.bfloat16), 'ctx', scatter_dimen...  162 us
    reduce_scatter x1, waiting for transfers between devices, body(): lax.psum_scatter(gv_resp_terms.astype(jnp.bfloat16), 'ctx', scatter_dimen...  161 us
    all_gather x1, blocking collectives, body(): lax.all_gather(v_resp, 'ctx', axis=1, tiled=True)  80 us
    all_gather x1, blocking collectives, body(): lax.all_gather(k_resp, 'ctx', axis=1, tiled=True)  78.2 us
  transfers between devices with their start and end apart: 8, of which 4 were waited for; matrix products, arithmetic and copies ran while one was open for 6% of the time, Pallas kernels for 0%

commit v1 on v0

v1 whole, which is shorter than its diff:
```python
import math

import jax
import jax.numpy as jnp
from jax import lax
from jax.experimental import pallas as pl
from jax.experimental.pallas import tpu as pltpu
from jax.sharding import Mesh, PartitionSpec as P

HQ = 32
HK = 4
DH = 128
GROUP = HQ // HK
ROWS = 64
QROWS = GROUP * ROWS
HALF = 2048
NBLK = 32
KB = 512
PER = KB // ROWS
PACK = 2 * ROWS + 16
PLANE = 16
CTX = ("zl", "y", "x")
NEG = -1e30
SCALE = 1.0 / math.sqrt(DH)
EXP_SCALE = SCALE * math.log2(math.e)
MIB = 1 << 20
bf16 = jnp.bfloat16
f32 = jnp.float32
i32 = jnp.int32


def dot(a, b):
    return lax.dot_general(a, b, (((1,), (0,)), ((), ())), preferred_element_type=f32)


def dot_tn(a, b):
    return lax.dot_general(a, b, (((0,), (0,)), ((), ())), preferred_element_type=f32)


def dot_nt(a, b):
    return lax.dot_general(a, b, (((1,), (1,)), ((), ())), preferred_element_type=f32)


def stack_heads(ref):
    return jnp.concatenate([ref[:, h * DH : (h + 1) * DH] for h in range(GROUP)], axis=0)


def where_am_i():
    side = lax.axis_index("resp")
    place = (lax.axis_index("zl") * 4 + lax.axis_index("y")) * 4 + lax.axis_index("x")
    return side, place


def start_copies(pairs, sems):
    copies = [pltpu.make_async_copy(s, d, sems.at[n]) for n, (s, d) in enumerate(pairs)]
    for c in copies:
        c.start()
    return copies


def key_pairs(ref, first, row, kp, vp):
    level = lax.axis_index("zl")
    pairs = []
    for n, z in enumerate((level, 1 - level)):
        to = pl.ds(first + z * PLANE, PLANE)
        pairs.append((ref.at[:, n, row : row + 64, :], kp.at[to]))
        pairs.append((ref.at[:, n, row + 64 : row + 128, :], vp.at[to]))
    return pairs


def prompt_pairs(side, own, other, kp, vp):
    return key_pairs(own, side * NBLK, 0, kp, vp) + key_pairs(other, (1 - side) * NBLK, 0, kp, vp)


def take(ref, first, rows):
    return ref[pl.ds(first, rows // ROWS), :, :].reshape(rows, DH)


def pick_start(doc, starts):
    low = jnp.where(doc >= 1, starts[0], 0)
    low = jnp.where(doc >= 2, starts[1], low)
    return jnp.where(doc >= 3, starts[2], low)


def key_positions(first, rows):
    return first + lax.broadcasted_iota(i32, (rows, QROWS), 0)


def lane_rows():
    return lax.broadcasted_iota(i32, (1, QROWS), 1) % ROWS


def head_lanes(row):
    return jnp.concatenate([row] * GROUP, axis=1)


def resp_range(resp_len, side, place):
    pos0 = place * ROWS
    live = resp_len[side]
    high = jnp.minimum(pos0 + lane_rows(), live - 1)
    blocks = jnp.minimum(pos0 + ROWS - 1, live - 1) // KB + 1
    return high, blocks


def pack_kernel(kp, vp, docs, kr, vr, out, ids, in_sems):
    copies = start_copies(
        [
            (docs, ids),
            (kp, out.at[0:64]),
            (vp, out.at[64:128]),
            (kr, out.at[PACK : PACK + 64]),
            (vr, out.at[PACK + 64 : PACK + 128]),
        ],
        in_sems,
    )
    copies[0].wait()
    row = jnp.concatenate([ids[...].astype(f32), jnp.full((1, DH - ROWS), 100.0, f32)], axis=1)
    out[128:144, :] = jnp.broadcast_to(row, (16, DH)).astype(bf16)
    for c in copies[1:]:
        c.wait()


def copies_kernel(own, other, prompt_out, resp_out, both, in_sems, sems):
    for c in start_copies([(own, both.at[0]), (other, both.at[1])], in_sems):
        c.wait()
    outs = [(both.at[:, 0:PACK, :], prompt_out.at[n]) for n in range(PLANE)]
    outs += [(both.at[:, PACK : PACK + 2 * ROWS, :], resp_out.at[n]) for n in range(PLANE)]
    for c in start_copies(outs, sems):
        c.wait()


def fwd_block(q_t, key, value, m_ref, l_ref, acc_ref, mask):
    z = dot(key, q_t) * EXP_SCALE
    if mask is not None:
        z = jnp.where(mask, z, NEG)
    old = m_ref[...]
    new = jnp.maximum(old, jnp.max(z, axis=0, keepdims=True))
    p = jnp.exp2(z - new)
    factor = jnp.exp2(old - new)
    m_ref[...] = new
    l_ref[...] = l_ref[...] * factor + jnp.sum(p, axis=0, keepdims=True)
    acc_ref[...] = acc_ref[...] * factor + dot_tn(value, p.astype(bf16))


def close_rows(m_ref, l_ref, acc_ref, att):
    total = l_ref[...]
    out = (acc_ref[...] / total).astype(bf16)
    rows = out.T
    for h in range(GROUP):
        att[:, h * DH : (h + 1) * DH] = rows[h * ROWS : (h + 1) * ROWS, :]
    return m_ref[...] + jnp.log2(total), out


def project(att, w_buf, tp, outs):
    all_att = att[...]
    width = outs[0].shape[1]
    for n, out in enumerate(outs):
        cols = pl.ds(pl.multiple_of(lax.rem(tp + n, 4) * width, width), width)
        out[...] = dot(all_att, w_buf[:, cols]).astype(bf16)


def row_deltas(d_t, out_t):
    return jnp.sum(d_t.astype(f32) * out_t.astype(f32), axis=0, keepdims=True)


def fwd_prompt_kernel(
    doc_ids, own, other, qp_in, qr_in, weight,
    out0, out1, out2, out3, out_t, stats, acc_out, win,
    kp, vp, docs, qp, qr, w_buf, att, m_ref, l_ref, acc_ref, sems, q_sems, w_sem,
):
    side, place = where_am_i()
    tp = lax.axis_index("tp")
    level = lax.axis_index("zl")
    q_copies = start_copies([(qp_in, qp), (qr_in, qr)], q_sems)
    pairs = prompt_pairs(side, own, other, kp, vp)
    for ref, first in ((own, side * NBLK), (other, (1 - side) * NBLK)):
        for n, z in enumerate((level, 1 - level)):
            pairs.append((ref.at[:, n, 128:144, :], docs.at[pl.ds(first + z * PLANE, PLANE)]))
    copies = start_copies(pairs, sems)
    w_copy = pltpu.make_async_copy(weight, w_buf, w_sem)
    w_copy.start()
    for c in q_copies:
        c.wait()
    q_t = stack_heads(qp).T
    r_t = stack_heads(qr).T
    for c in copies:
        c.wait()
    all_docs = docs[...].astype(f32).reshape(2 * NBLK * 16, DH)
    starts = []
    for n, value in enumerate((1.0, 2.0, 3.0)):
        count = jnp.sum(jnp.where(all_docs < value, 1.0 / 16, 0.0)).astype(i32)
        starts.append(count)

    def begin():
        m_ref[...] = jnp.full((1, QROWS), NEG, f32)
        l_ref[...] = jnp.zeros((1, QROWS), f32)
        acc_ref[...] = jnp.zeros((DH, QROWS), f32)

    begin()
    block = side * NBLK + place
    pos0 = block * ROWS
    low = pick_start(head_lanes(docs[block].astype(f32)[0:1, 0:ROWS]), starts)
    high = pos0 + lane_rows()
    low0 = pick_start(doc_ids[0], starts)
    win[0] = low0

    @pl.loop(low0 // KB, pos0 // KB + 1)
    def _(j):
        pos = key_positions(j * KB, KB)
        fwd_block(
            q_t, take(kp, j * PER, KB), take(vp, j * PER, KB), m_ref, l_ref, acc_ref,
            (pos >= low) & (pos <= high),
        )

    stats[0:1, :], out_t[...] = close_rows(m_ref, l_ref, acc_ref, att)
    begin()
    for j in range(4096 // KB):
        fwd_block(r_t, take(kp, j * PER, KB), take(vp, j * PER, KB), m_ref, l_ref, acc_ref, None)

    stats[1:2, :] = m_ref[...]
    stats[2:3, :] = l_ref[...]
    stats[4:5, :] = low.astype(f32)
    acc_out[...] = acc_ref[...]
    w_copy.wait()
    project(att, w_buf, tp, (out0, out1, out2, out3))

def resp_kernel(
    resp_len, own, qr_in, stats_in, acc_in, out_t_in, weight, *refs,
):
    cot_in = refs[:8]
    out0, out1, out2, out3, stats, g_resp, gq_ref, d_out = refs[8:16]
    kr, vr, qr, w_buf, cot, out_t_p, m_ref, l_ref, acc_ref, att, sems, c_sems, w_sem = refs[16:]
    side, place = where_am_i()
    tp = lax.axis_index("tp")
    copies = start_copies(
        key_pairs(own, 0, 0, kr, vr)
        + [(qr_in, qr), (stats_in, stats), (acc_in, acc_ref), (out_t_in, out_t_p)],
        sems,
    )
    w_copy = pltpu.make_async_copy(weight, w_buf, w_sem)
    w_copy.start()
    width = cot_in[0].shape[1]
    pairs = []
    for n, ref in enumerate(cot_in):
        cols = pl.ds(pl.multiple_of(lax.rem(tp + n // 2, 4) * width, width), width)
        pairs.append((ref, cot.at[pl.ds((n % 2) * ROWS, ROWS), cols]))
    c_copies = start_copies(pairs, c_sems)
    for c in copies:
        c.wait()
    q_rows = stack_heads(qr)
    q_t = q_rows.T
    m_ref[...] = stats[1:2, :]
    l_ref[...] = stats[2:3, :]
    high, used = resp_range(resp_len, side, place)

    @pl.loop(0, used)
    def _(j):
        pos = key_positions(j * KB, KB)
        fwd_block(
            q_t, take(kr, j * PER, KB), take(vr, j * PER, KB), m_ref, l_ref, acc_ref, pos <= high
        )

    log_total, out_t = close_rows(m_ref, l_ref, acc_ref, att)
    for c in c_copies:
        c.wait()
    w_copy.wait()
    d_all = dot(w_buf[...], cot[...].T).astype(bf16)
    for n in range(2):
        for h in range(GROUP):
            d_out[n, :, h * ROWS : (h + 1) * ROWS] = d_all[
                h * DH : (h + 1) * DH, n * ROWS : (n + 1) * ROWS
            ]
    d_t = d_out[1]
    d_rows = d_t.T
    delta = row_deltas(d_t, out_t)
    stats[1:2, :] = log_total
    stats[2:3, :] = row_deltas(d_out[0], out_t_p[...])
    stats[3:4, :] = delta
    gq_ref[...] = jnp.zeros((DH, QROWS), f32)

    @pl.loop(0, used)
    def _(j):
        pos = key_positions(j * KB, KB)
        g_key, g_value = bwd_block(
            q_t, q_rows, d_t, d_rows, take(kr, j * PER, KB), take(vr, j * PER, KB),
            log_total, delta, gq_ref, pos <= high,
        )
        blocks = pl.ds(j * PER, PER)
        g_resp[blocks, 0:64, :] = (g_key * SCALE).astype(bf16).reshape(PER, ROWS, DH)
        g_resp[blocks, 64:128, :] = g_value.astype(bf16).reshape(PER, ROWS, DH)

    @pl.loop(used, HALF // KB)
    def _(j):
        g_resp[pl.ds(j * PER, PER), :, :] = jnp.zeros((PER, 2 * ROWS, DH), bf16)

    project(att, w_buf, tp, (out0, out1, out2, out3))


def bwd_block(q_t, q_rows, d_t, d_rows, key, value, log_total, delta, gq_ref, mask):
    z = dot(key, q_t) * EXP_SCALE
    if mask is not None:
        z = jnp.where(mask, z, NEG)
    p = jnp.exp2(z - log_total)
    g_value = dot(p.astype(bf16), d_rows)
    dp = dot(value, d_t)
    ds = (p * (dp - delta)).astype(bf16)
    g_key = dot(ds, q_rows)
    gq_ref[...] += dot_tn(key, ds)
    return g_key, g_value


def store_q(gq_ref, out):
    rows = (gq_ref[...] * SCALE).astype(bf16).T
    for h in range(GROUP):
        out[:, h * DH : (h + 1) * DH] = rows[h * ROWS : (h + 1) * ROWS, :]


def bwd_prompt_kernel(
    win, own, other, qp_in, qr_in, d_in, stats_in, gq_in,
    gq_p, gq_r, g_mine, g_other,
    kp, vp, qp, qr, d_att, stats, gk, gv, gq_ref, sems,
):
    side, place = where_am_i()
    copies = start_copies(
        [(qr_in, qr), (qp_in, qp), (d_in, d_att), (stats_in, stats), (gq_in, gq_ref)]
        + prompt_pairs(side, own, other, kp, vp),
        sems,
    )
    for c in copies:
        c.wait()
    d_t = d_att[1]
    d_rows = d_t.T
    q_rows = stack_heads(qr)
    q_t = q_rows.T
    log_total = stats[1:2, :]
    delta = stats[3:4, :]

    @pl.loop(0, 4096 // KB // 4)
    def _(t):
        for u in range(4):
            j = t * 4 + u
            at = pl.ds(pl.multiple_of(j * KB, KB), KB)
            g_key, g_value = bwd_block(
                q_t, q_rows, d_t, d_rows, take(kp, j * PER, KB), take(vp, j * PER, KB),
                log_total, delta, gq_ref, None,
            )
            gk[at, :] = g_key
            gv[at, :] = g_value

    store_q(gq_ref, gq_r)

    d_t = d_att[0]
    d_rows = d_t.T
    q_rows = stack_heads(qp)
    q_t = q_rows.T
    log_total = stats[0:1, :]
    delta = stats[2:3, :]
    gq_ref[...] = jnp.zeros((DH, QROWS), f32)
    pos0 = (side * NBLK + place) * ROWS
    low = stats[4:5, :].astype(i32)
    high = pos0 + lane_rows()

    @pl.loop(win[0] // KB, pos0 // KB + 1)
    def _(j):
        at = pl.ds(pl.multiple_of(j * KB, KB), KB)
        pos = key_positions(j * KB, KB)
        g_key, g_value = bwd_block(
            q_t, q_rows, d_t, d_rows, take(kp, j * PER, KB), take(vp, j * PER, KB),
            log_total, delta, gq_ref, (pos >= low) & (pos <= high),
        )
        gk[at, :] += g_key
        gv[at, :] += g_value

    store_q(gq_ref, gq_p)

    @pl.loop(0, HALF // KB)
    def _(j):
        blocks = pl.ds(j * PER, PER)
        for base, out in ((side * HALF, g_mine), ((1 - side) * HALF, g_other)):
            at = pl.ds(pl.multiple_of(base + j * KB, KB), KB)
            out[blocks, 0:64, :] = (gk[at, :] * SCALE).astype(bf16).reshape(PER, ROWS, DH)
            out[blocks, 64:128, :] = gv[at, :].astype(bf16).reshape(PER, ROWS, DH)


def sum_kernel(prompt, resp, gk_p, gv_p, gk_r, gv_r):
    for ref, gk, gv in ((prompt, gk_p, gv_p), (resp, gk_r, gv_r)):
        total = ref[0].astype(f32)
        for n in range(1, NBLK):
            total = total + ref[n].astype(f32)
        gk[...] = total[0:64, :].astype(bf16)
        gv[...] = total[64:128, :].astype(bf16)


VM = pl.BlockSpec(memory_space=pltpu.VMEM)
SM = pl.BlockSpec(memory_space=pltpu.SMEM)
HB = pl.BlockSpec(memory_space=pltpu.HBM)


def shape(*dims, dtype=bf16):
    return jax.ShapeDtypeStruct(dims, dtype)


def call(kernel, name, in_specs, outs, scratch, args, gflop, out_specs=None, limit=58):
    return pl.pallas_call(
        kernel,
        out_shape=outs,
        in_specs=in_specs,
        out_specs=out_specs or (VM,) * len(outs),
        scratch_shapes=scratch,
        compiler_params=pltpu.CompilerParams(vmem_limit_bytes=limit * MIB),
        cost_estimate=pl.CostEstimate(
            flops=int(gflop * 1e9), bytes_accessed=4 * 10**6, transcendentals=10**6
        ),
        name=name,
    )(*args)


def state_scratch():
    return [pltpu.VMEM((1, QROWS), f32), pltpu.VMEM((1, QROWS), f32), pltpu.VMEM((DH, QROWS), f32)]


def key_scratch(blocks):
    return [pltpu.VMEM((blocks, ROWS, DH), bf16), pltpu.VMEM((blocks, ROWS, DH), bf16)]


def sems(n):
    return pltpu.SemaphoreType.DMA((n,))


SWAP = [(0, 1), (1, 0)]


def shift(x, by):
    return lax.ppermute(x, "tp", [(n, (n + by) % 4) for n in range(4)])


def add(*terms):
    total = terms[0].astype(f32)
    for t in terms[1:]:
        total = total + t.astype(f32)
    return total.astype(bf16)


def body(q_prompt, k_prompt, v_prompt, doc_ids, q_resp, k_resp, v_resp, resp_len, out_weight,
         grad_prompt, grad_resp):
    q_resp, k_resp, v_resp, grad_resp = q_resp[0], k_resp[0], v_resp[0], grad_resp[0]
    part = grad_prompt.shape[1]
    cols = GROUP * DH
    row_vm = pltpu.VMEM((ROWS, cols), bf16)
    weight_vm = pltpu.VMEM(out_weight.shape, bf16)
    stats_vm = pltpu.VMEM((8, QROWS), f32)

    left_p, left_r = shift(grad_prompt, 1), shift(grad_resp, 1)
    right_p, right_r = shift(grad_prompt, -1), shift(grad_resp, -1)
    (pack,) = call(
        pack_kernel, "pack_keys", [HB] * 5, (shape(PACK + 2 * ROWS, DH),),
        [pltpu.VMEM((1, ROWS), i32), sems(5)],
        (k_prompt, v_prompt, doc_ids.reshape(1, ROWS), k_resp, v_resp), 0.1,
    )
    pack_z = lax.ppermute(pack, "zl", SWAP)
    pack_p, pack_r = call(
        copies_kernel, "copy_packs", [HB] * 2,
        (shape(PLANE, 2, PACK, DH), shape(PLANE, 2, 2 * ROWS, DH)),
        [pltpu.VMEM((2, PACK + 2 * ROWS, DH), bf16), sems(2), sems(2 * PLANE)],
        (pack, pack_z), 0.1,
        out_specs=(HB, HB),
    )
    own_p = lax.all_to_all(pack_p, ("y", "x"), 0, 0, tiled=True)
    own_p, pack_r, left_p, left_r, right_p, right_r = lax.optimization_barrier(
        (own_p, pack_r, left_p, left_r, right_p, right_r)
    )
    far_p, far_r = shift(left_p, 1), shift(right_r, -1)
    own_r = lax.all_to_all(pack_r, ("y", "x"), 0, 0, tiled=True)
    other_p = lax.ppermute(own_p, "resp", SWAP)

    p0, p1, p2, p3, out_t, stats_p, acc_r, win = call(
        fwd_prompt_kernel, "forward_prompt_keys", [SM] + [HB] * 5,
        (shape(ROWS, part),) * 4
        + (
            shape(DH, QROWS), shape(8, QROWS, dtype=f32),
            shape(DH, QROWS, dtype=f32), shape(4, dtype=i32),
        ),
        key_scratch(2 * NBLK)
        + [pltpu.VMEM((2 * NBLK, 16, DH), bf16), row_vm, row_vm, weight_vm, row_vm]
        + state_scratch()
        + [sems(12), sems(2), pltpu.SemaphoreType.DMA(())],
        (doc_ids, own_p, other_p, q_prompt, q_resp, out_weight), 4,
        out_specs=(VM,) * 7 + (SM,),
    )
    out_p = add(p0, shift(p1, 1), shift(p2, 2), shift(p3, -1))

    r0, r1, r2, r3, stats, g_resp, gq_acc, d_att = call(
        resp_kernel, "response_keys", [SM] + [HB] * 14,
        (shape(ROWS, part),) * 4
        + (
            shape(8, QROWS, dtype=f32), shape(NBLK, 2 * ROWS, DH),
            shape(DH, QROWS, dtype=f32), shape(2, DH, QROWS),
        ),
        key_scratch(NBLK)
        + [
            row_vm, weight_vm, pltpu.VMEM((2 * ROWS, 4 * part), bf16),
            pltpu.VMEM((DH, QROWS), bf16),
        ]
        + state_scratch()
        + [row_vm, sems(8), sems(8), pltpu.SemaphoreType.DMA(())],
        (
            resp_len, own_r, q_resp, stats_p, acc_r, out_t, out_weight,
            grad_prompt, grad_resp, right_p, right_r, far_p, far_r, left_p, left_r,
        ), 4,
    )
    sums_r = lax.all_to_all(g_resp, CTX, 0, 0, tiled=True)
    gq_acc, out_p = lax.optimization_barrier((gq_acc, out_p))
    out_r = add(r0, shift(r1, 1), shift(r2, 2), shift(r3, -1))
    gq_p, gq_r, g_mine, g_other = call(
        bwd_prompt_kernel, "backward_prompt_keys", [SM] + [HB] * 7,
        (shape(ROWS, cols),) * 2 + (shape(NBLK, 2 * ROWS, DH),) * 2,
        key_scratch(2 * NBLK)
        + [
            row_vm, row_vm, pltpu.VMEM((2, DH, QROWS), bf16), stats_vm,
            pltpu.VMEM((4096, DH), f32), pltpu.VMEM((4096, DH), f32),
            pltpu.VMEM((DH, QROWS), f32), sems(13),
        ],
        (win, own_p, other_p, q_prompt, q_resp, d_att, stats, gq_acc), 8,
    )
    g_in = lax.ppermute(g_other, "resp", SWAP)
    g_in, out_r = lax.optimization_barrier((g_in, out_r))
    sums_p = lax.all_to_all(add(g_mine, g_in), CTX, 0, 0, tiled=True)
    gk_p, gv_p, gk_r, gv_r = call(
        sum_kernel, "sum_parts", [VM, VM], (shape(ROWS, DH),) * 4, [], (sums_p, sums_r), 0.1,
        limit=16,
    )
    return (out_p, out_r[None], gq_p, gk_p, gv_p, gq_r[None], gk_r[None], gv_r[None])


def solution(mesh):
    fine = Mesh(mesh.devices.reshape(2, 2, 4, 4, 4), ("resp", "zl", "y", "x", "tp"))
    rows = P(("resp",) + CTX, "tp")
    resp_rows = P("resp", CTX, "tp")
    in_specs = (
        rows, rows, rows, P(("resp",) + CTX), resp_rows, resp_rows, resp_rows, P(),
        P("tp", None), rows, resp_rows,
    )
    out_specs = (rows, resp_rows, rows, rows, rows, resp_rows, resp_rows, resp_rows)
    return jax.shard_map(body, mesh=fine, in_specs=in_specs, out_specs=out_specs, check_vma=False)
```

time: 1590 us -> 157 us (0.10)
  waiting for transfers between devices: 930 us -> 28 us
  blocking collectives: 466 us -> 23.6 us
  matrix products: 99.8 us -> 0 us
  starting transfers between devices: 0.32 us -> 52 us
  Pallas kernels: 0 us -> 44.1 us
  local copies, waits for them, and re-layouts: 40.2 us -> 4.01 us
  other arithmetic: 21.8 us -> 3.1 us
  loops' own time: 17.3 us -> 0 us
    reduce_scatter x5 -> x0, waiting for transfers between devices: 928 us -> none  [the longest x1 315 us: body(): lax.psum_scatter(gv_prompt_terms, ('resp', 'ctx'), scatter_dimension=0, t...]
    unnamed x1 -> x0, blocking collectives: 308 us -> none
    all_gather x2 -> x0, blocking collectives: 158 us -> none  [the longest x1 80 us: body(): lax.all_gather(v_resp, 'ctx', axis=1, tiled=True)]
    dot_general x86 -> x0, matrix products: 99.8 us -> none  [the longest x12 13.7 us: forward_block_step(): jnp.einsum('nhgk,khd->nhgd', weights.astype(jnp.bfloat16), value_block, p...]
    pallas_call x0 -> x6, Pallas kernels: none -> 44.1 us  [call(): pl.pallas_call(kernel, out_shape=outs, in_specs=in_specs, out_specs=out_s...]
    ppermute x0 -> x15, starting transfers between devices: none -> 29.1 us  [the longest x12 27 us: shift(): return lax.ppermute(x, 'tp', [(n, (n + by) % 4) for n in range(4)])]
    ppermute x0 -> x15, waiting for transfers between devices: none -> 28 us  [the longest x12 25.3 us: shift(): return lax.ppermute(x, 'tp', [(n, (n + by) % 4) for n in range(4)])]
    all_to_all x0 -> x1, blocking collectives: none -> 23.6 us  [body(): sums_p = lax.all_to_all(add(g_mine, g_in), CTX, 0, 0, tiled=True)]
  transfers between devices with their start and end apart: 8 -> 18, of which waited for: 4 -> 7; matrix products, arithmetic and copies ran while one was open for 6% -> 2% of each run, Pallas kernels for 0% -> 25%
where the time goes in v1:
time: 157 us; the launch traced here: 156 us
  starting transfers between devices  52 us (33%)
  Pallas kernels  44.1 us (28%)
  waiting for transfers between devices  28 us (18%)
  blocking collectives  23.6 us (15%)
  local copies, waits for them, and re-layouts  4.01 us (3%)
  other arithmetic  3.1 us (2%)
    pallas_call x6, Pallas kernels, call(): pl.pallas_call(kernel, out_shape=outs, in_specs=in_specs, out_specs=out_s...  44.1 us
    ppermute x12, starting transfers between devices, shift(): return lax.ppermute(x, 'tp', [(n, (n + by) % 4) for n in range(4)])  27 us
    ppermute x12, waiting for transfers between devices, shift(): return lax.ppermute(x, 'tp', [(n, (n + by) % 4) for n in range(4)])  25.3 us
    all_to_all x1, blocking collectives, body(): sums_p = lax.all_to_all(add(g_mine, g_in), CTX, 0, 0, tiled=True)  23.6 us
    all_to_all x1, starting transfers between devices, body(): sums_r = lax.all_to_all(g_resp, CTX, 0, 0, tiled=True)  8.92 us
    all_to_all x1, starting transfers between devices, body(): own_p = lax.all_to_all(pack_p, ('y', 'x'), 0, 0, tiled=True)  7.05 us
    all_to_all x1, starting transfers between devices, body(): own_r = lax.all_to_all(pack_r, ('y', 'x'), 0, 0, tiled=True)  6.94 us
    unnamed x30, local copies, waits for them, and re-layouts  4.01 us
  transfers between devices with their start and end apart: 18, of which 7 were waited for; matrix products, arithmetic and copies ran while one was open for 2% of the time, Pallas kernels for 25%

profile of v1, /device:TPU:32, one launch (start us, length us, event | category | flops | bytes accessed | tf_op | source)
XLA Modules:
  0.0 155.7 jit_solution(8818891444962758340)
XLA Ops:
  0.6 1.5 pack_keys.1.own
  2.1 0.0 copy-start.6
  2.1 0.0 copy-start.5
  2.1 1.9 %collective-permute-start = (bf16[272,128]{1,0:T(8,128)(2,1)}, bf16[272,128]{1,0:T(8,128)(2,1)S(1)}, u32[]{:S(2)}, u32[]{:S(2)}) collective-permute-start(bf16[272,128]{1,0:T(8,128)(2,1)} %pack_keys.1.own), channel_id=1, source_target_pairs={{0,64},{64,0},{1,65},{65,1},{2,66},{66,2},{3,67},{67,3},{4,68},{68... | collective-permute-start | bytes 208904 | tf_op jit(solution)/shard_map/ppermute | solution.py:460
  4.1 2.7 %collective-permute-done.other = bf16[272,128]{1,0:T(8,128)(2,1)S(1)} collective-permute-done((bf16[272,128]{1,0:T(8,128)(2,1)}, bf16[272,128]{1,0:T(8,128)(2,1)S(1)}, u32[]{:S(2)}, u32[]{:S(2)}) %collective-permute-start) | collective-permute-done | bytes 69664 | tf_op jit(solution)/shard_map/ppermute | solution.py:460
  6.7 0.6 copy-done.14
  7.4 2.6 %copy_packs.1 = (bf16[16,2,144,128]{3,2,1,0:T(8,128)(2,1)}, bf16[16,2,128,128]{3,2,1,0:T(8,128)(2,1)}) custom-call(bf16[272,128]{1,0:T(8,128)(2,1)} %pack_keys.1.own, bf16[272,128]{1,0:T(8,128)(2,1)} %copy-done.14), custom_call_target="tpu_custom_call" | custom-call | flops 100000000 | bytes 4000000 | tf_op jit(solution)/shard_map/copy_packs/pallas_call | solution.py:404
  10.0 7.0 %all-to-all-start = ((bf16[16,2,144,128]{3,2,1,0:T(8,128)(2,1)}), bf16[16,2,144,128]{3,2,1,0:T(8,128)(2,1)S(1)}, u32[]{:S(2)}, u32[]{:S(2)}) async-start(bf16[16,2,144,128]{3,2,1,0:T(8,128)(2,1)} %get-tuple-element.44), calls=%async_computation | async-start | bytes 2359296 | tf_op jit(solution)/shard_map/all_to_all | solution.py:468
  17.0 0.0 copy-done.6
  17.0 5.5 %collective-permute-start.4 = (bf16[64,1280]{1,0:T(8,128)(2,1)S(1)}, bf16[64,1280]{1,0:T(8,128)(2,1)S(1)}, u32[]{:S(2)}, u32[]{:S(2)}) collective-permute-start(bf16[64,1280]{1,0:T(8,128)(2,1)S(1)} %bitcast.11), channel_id=1, source_target_pairs={{0,3},{1,0},{2,1},{3,2},{4,7},{5,4},{6,5},{7,6},{8,11},{9,8},{10,9... | collective-permute-start | bytes 491528 | tf_op jit(solution)/shard_map/ppermute | solution.py:434
  22.5 0.0 collective-permute-start.2
  22.5 0.0 copy-done.5
  22.5 2.0 %collective-permute-start.1 = (bf16[64,1280]{1,0:T(8,128)(2,1)S(1)}, bf16[64,1280]{1,0:T(8,128)(2,1)S(1)}, u32[]{:S(2)}, u32[]{:S(2)}) collective-permute-start(bf16[64,1280]{1,0:T(8,128)(2,1)S(1)} %copy-done.5), channel_id=1, source_target_pairs={{0,1},{1,2},{2,3},{3,0},{4,5},{5,6},{6,7},{7,4},{8,9},{9,10},{10,1... | collective-permute-start | bytes 491528 | tf_op jit(solution)/shard_map/ppermute | solution.py:434
  24.5 2.2 %collective-permute-start.3 = (bf16[64,1280]{1,0:T(8,128)(2,1)S(1)}, bf16[64,1280]{1,0:T(8,128)(2,1)}, u32[]{:S(2)}, u32[]{:S(2)}) collective-permute-start(bf16[64,1280]{1,0:T(8,128)(2,1)S(1)} %copy-done.5), channel_id=1, source_target_pairs={{0,3},{1,0},{2,1},{3,2},{4,7},{5,4},{6,5},{7,6},{8,11},{9,8},{10,9... | collective-permute-start | bytes 491528 | tf_op jit(solution)/shard_map/ppermute | solution.py:434
  26.7 4.4 %collective-permute-done.4.refs_3_ = bf16[64,1280]{1,0:T(8,128)(2,1)S(1)} collective-permute-done((bf16[64,1280]{1,0:T(8,128)(2,1)S(1)}, bf16[64,1280]{1,0:T(8,128)(2,1)S(1)}, u32[]{:S(2)}, u32[]{:S(2)}) %collective-permute-start.4) | collective-permute-done | bytes 163872 | tf_op jit(solution)/shard_map/ppermute | solution.py:434
  31.0 6.0 %collective-permute-done.2.refs_7_ = bf16[64,1280]{1,0:T(8,128)(2,1)S(1)} collective-permute-done((bf16[64,1280]{1,0:T(8,128)(2,1)S(1)}, bf16[64,1280]{1,0:T(8,128)(2,1)S(1)}, u32[]{:S(2)}, u32[]{:S(2)}) %collective-permute-start.2) | collective-permute-done | bytes 163872 | tf_op jit(solution)/shard_map/ppermute | solution.py:434
  37.1 2.2 %collective-permute-done.1.refs_6_ = bf16[64,1280]{1,0:T(8,128)(2,1)S(1)} collective-permute-done((bf16[64,1280]{1,0:T(8,128)(2,1)S(1)}, bf16[64,1280]{1,0:T(8,128)(2,1)S(1)}, u32[]{:S(2)}, u32[]{:S(2)}) %collective-permute-start.1) | collective-permute-done | bytes 163872 | tf_op jit(solution)/shard_map/ppermute | solution.py:434
  39.3 0.0 copy-done.7
  39.3 0.0 copy-done.8
  39.3 0.7 copy-done.9
  40.0 0.0 collective-permute-done.3.refs_2_
  40.0 0.0 all-to-all-done.own
  40.0 0.1 collective-permute-start.5
  40.1 6.9 %all-to-all-start.1 = ((bf16[16,2,128,128]{3,2,1,0:T(8,128)(2,1)}), bf16[16,2,128,128]{3,2,1,0:T(8,128)(2,1)S(1)}, u32[]{:S(2)}, u32[]{:S(2)}) async-start(bf16[16,2,128,128]{3,2,1,0:T(8,128)(2,1)} %get-tuple-element.46), calls=%async_computation.1 | async-start | bytes 2097152 | tf_op jit(solution)/shard_map/all_to_all | solution.py:473
  47.0 0.5 collective-permute-start.7
  47.5 2.5 %collective-permute-start.6 = (bf16[64,1280]{1,0:T(8,128)(2,1)}, bf16[64,1280]{1,0:T(8,128)(2,1)}, u32[]{:S(2)}, u32[]{:S(2)}) collective-permute-start(bf16[64,1280]{1,0:T(8,128)(2,1)} %copy-done.9), channel_id=1, source_target_pairs={{0,1},{1,2},{2,3},{3,0},{4,5},{5,6},{6,7},{7,4},{8,9},{9,10},{10,1... | collective-permute-start | bytes 491528 | tf_op jit(solution)/shard_map/ppermute | solution.py:434
  50.0 0.0 collective-permute-done.5.other
  50.0 0.0 copy-done
  50.0 1.0 copy-done.4
  51.0 12.2 %forward_prompt_keys.1 = (bf16[64,1280]{1,0:T(8,128)(2,1)}, bf16[64,1280]{1,0:T(8,128)(2,1)}, bf16[64,1280]{1,0:T(8,128)(2,1)}, bf16[64,1280]{1,0:T(8,128)(2,1)}...) custom-call(s32[64]{0:T(128)} %doc_ids.1, bf16[16,2,144,128]{3,2,1,0:T(8,128)(2,1)} %copy-done, ...), custom_call_target="tpu_custom_call" | custom-call | flops 4000000000 | bytes 4000000 | tf_op jit(solution)/shard_map/forward_prompt_keys/pallas_call | solution.py:404
  63.2 0.5 collective-permute-start.8
  63.7 3.6 %collective-permute-start.9 = (bf16[64,1280]{1,0:T(8,128)(2,1)}, bf16[64,1280]{1,0:T(8,128)(2,1)S(1)}, u32[]{:S(2)}, u32[]{:S(2)}) collective-permute-start(bf16[64,1280]{1,0:T(8,128)(2,1)} %get-tuple-element.58), channel_id=1, source_target_pairs={{0,2},{1,3},{2,0},{3,1},{4,6},{5,7},{6,4},{7,5},{8,10},{9,11},{10,... | collective-permute-start | bytes 491528 | tf_op jit(solution)/shard_map/ppermute | solution.py:434
  67.3 1.7 %collective-permute-start.10 = (bf16[64,1280]{1,0:T(8,128)(2,1)}, bf16[64,1280]{1,0:T(8,128)(2,1)S(1)}, u32[]{:S(2)}, u32[]{:S(2)}) collective-permute-start(bf16[64,1280]{1,0:T(8,128)(2,1)} %get-tuple-element.59), channel_id=1, source_target_pairs={{0,3},{1,0},{2,1},{3,2},{4,7},{5,4},{6,5},{7,6},{8,11},{9,8},{10,9... | collective-permute-start | bytes 491528 | tf_op jit(solution)/shard_map/ppermute | solution.py:434
  69.0 0.0 collective-permute-done.7.refs_5_
  69.0 0.7 copy-done.13
  69.6 0.0 collective-permute-done.6.refs_4_
  69.6 0.0 all-to-all-done.1.own
  69.6 1.0 copy-done.1
  70.6 13.9 %response_keys.1 = (bf16[64,1280]{1,0:T(8,128)(2,1)}, bf16[64,1280]{1,0:T(8,128)(2,1)}, bf16[64,1280]{1,0:T(8,128)(2,1)}, bf16[64,1280]{1,0:T(8,128)(2,1)}, f32[...) custom-call(s32[2]{0:T(128)} %resp_len.1, ...), custom_call_target="tpu_custom_call" | custom-call | flops 4000000000 | bytes 4000000 | tf_op jit(solution)/shard_map/response_keys/pallas_call | solution.py:404
  84.5 0.0 copy-start.3
  84.5 8.9 %all-to-all-start.3 = ((bf16[32,128,128]{2,1,0:T(8,128)(2,1)}), bf16[32,128,128]{2,1,0:T(8,128)(2,1)S(1)}, u32[]{:S(2)}, u32[]{:S(2)}) async-start(bf16[32,128,128]{2,1,0:T(8,128)(2,1)} %get-tuple-element.74), calls=%async_computation.3 | async-start | bytes 2097152 | tf_op jit(solution)/shard_map/all_to_all | solution.py:511
  93.4 0.0 collective-permute-done.8
  93.4 0.0 collective-permute-done.9
  93.5 0.0 collective-permute-done.10
  93.5 0.0 copy-done.3
  93.5 0.8 add_convert_fusion.2
  94.2 13.2 %backward_prompt_keys.1 = (bf16[64,1024]{1,0:T(8,128)(2,1)}, bf16[64,1024]{1,0:T(8,128)(2,1)}, bf16[32,128,128]{2,1,0:T(8,128)(2,1)}, bf16[32,128,128]{2,1,0:T(8,128)(2,1)}) custom-call(s32[4]{0:T(128)} %get-tuple-element.61.win, bf16[16,2,144,128]{3,2,1,0:T(8,128)(2,1)} %copy-done, bf16[16,2,144,128]{3,2,1,0:T(8,128)(2,1)} %copy-done.4, ...), custom_call_target="tpu_custom_call" | custom-call | flops 8000000000 | bytes 4000000 | tf_op jit(solution)/shard_map/backward_prompt_keys/pallas_call | solution.py:404
  107.4 0.1 collective-permute-start.11
  107.5 0.0 copy-done.12
  107.5 1.3 collective-permute-start.12
  108.8 0.0 copy-done.11
  108.8 3.2 %collective-permute-start.13 = (bf16[64,1280]{1,0:T(8,128)(2,1)S(1)}, bf16[64,1280]{1,0:T(8,128)(2,1)S(1)}, u32[]{:S(2)}, u32[]{:S(2)}) collective-permute-start(bf16[64,1280]{1,0:T(8,128)(2,1)S(1)} %copy-done.11), channel_id=1, source_target_pairs={{0,2},{1,3},{2,0},{3,1},{4,6},{5,7},{6,4},{7,5},{8,10},{9,11},{10,... | collective-permute-start | bytes 491528 | tf_op jit(solution)/shard_map/ppermute | solution.py:434
  112.1 0.0 copy-done.10
  112.1 4.0 %collective-permute-start.14 = (bf16[64,1280]{1,0:T(8,128)(2,1)S(1)}, bf16[64,1280]{1,0:T(8,128)(2,1)S(1)}, u32[]{:S(2)}, u32[]{:S(2)}) collective-permute-start(bf16[64,1280]{1,0:T(8,128)(2,1)S(1)} %copy-done.10), channel_id=1, source_target_pairs={{0,3},{1,0},{2,1},{3,2},{4,7},{5,4},{6,5},{7,6},{8,11},{9,8},{10,9... | collective-permute-start | bytes 491528 | tf_op jit(solution)/shard_map/ppermute | solution.py:434
  116.1 5.4 %collective-permute-done.12 = bf16[64,1280]{1,0:T(8,128)(2,1)S(1)} collective-permute-done((bf16[64,1280]{1,0:T(8,128)(2,1)S(1)}, bf16[64,1280]{1,0:T(8,128)(2,1)S(1)}, u32[]{:S(2)}, u32[]{:S(2)}) %collective-permute-start.12) | collective-permute-done | bytes 163872 | tf_op jit(solution)/shard_map/ppermute | solution.py:434
  121.6 2.5 %collective-permute-done.13 = bf16[64,1280]{1,0:T(8,128)(2,1)S(1)} collective-permute-done((bf16[64,1280]{1,0:T(8,128)(2,1)S(1)}, bf16[64,1280]{1,0:T(8,128)(2,1)S(1)}, u32[]{:S(2)}, u32[]{:S(2)}) %collective-permute-start.13) | collective-permute-done | bytes 163872 | tf_op jit(solution)/shard_map/ppermute | solution.py:434
  124.0 4.8 %collective-permute-done.14 = bf16[64,1280]{1,0:T(8,128)(2,1)S(1)} collective-permute-done((bf16[64,1280]{1,0:T(8,128)(2,1)S(1)}, bf16[64,1280]{1,0:T(8,128)(2,1)S(1)}, u32[]{:S(2)}, u32[]{:S(2)}) %collective-permute-start.14) | collective-permute-done | bytes 163872 | tf_op jit(solution)/shard_map/ppermute | solution.py:434
  128.8 0.0 copy-done.2
  128.8 0.7 add_convert_fusion.1
  129.6 0.0 collective-permute-done.11
  129.6 1.6 %add_convert_fusion = bf16[32,128,128]{2,1,0:T(8,128)(2,1)S(1)} fusion(bf16[32,128,128]{2,1,0:T(8,128)(2,1)S(1)} %collective-permute-done.11, bf16[32,128,128]{2,1,0:T(8,128)(2,1)} %get-tuple-element.72), kind=kLoop, calls=%fused_computation | loop fusion | flops 2097152 | bytes 3145728 | tf_op jit(solution)/shard_map/convert_element_type | solution.py:441
  131.2 0.0 all-to-all-done.3.resp
  131.2 23.6 %all_to_all.20.prompt = bf16[32,128,128]{2,1,0:T(8,128)(2,1)S(1)} all-to-all(bf16[32,128,128]{2,1,0:T(8,128)(2,1)S(1)} %add_convert_fusion), channel_id=1, replica_groups=mesh['resp'=2,'zl'=2,'y'=4,'x'=4,'tp'=4] {'zl','y','x'}, dimensions={0} | all-to-all | bytes 2097152 | tf_op jit(solution)/shard_map/all_to_all | solution.py:527
  154.8 0.9 sum_parts.1
  (12 shorter events, 0.0 us)
Async XLA Ops:
  2.1 14.9 %copy-start.6 = (bf16[1,64,1280]{2,1,0:T(8,128)(2,1)S(1)}, bf16[1,64,1280]{2,1,0:T(8,128)(2,1)}, u32[]{:S(2)}) copy-start(bf16[1,64,1280]{2,1,0:T(8,128)(2,1)} %param.21) | copy-start | bytes 491524
  2.1 20.4 %copy-start.5 = (bf16[64,1280]{1,0:T(8,128)(2,1)S(1)}, bf16[64,1280]{1,0:T(8,128)(2,1)}, u32[]{:S(2)}) copy-start(bf16[64,1280]{1,0:T(8,128)(2,1)} %refs_0_.1) | copy-start | bytes 491524
  2.1 4.6 %collective-permute-start = (bf16[272,128]{1,0:T(8,128)(2,1)}, bf16[272,128]{1,0:T(8,128)(2,1)S(1)}, u32[]{:S(2)}, u32[]{:S(2)}) collective-permute-start(bf16[272,128]{1,0:T(8,128)(2,1)} %pack_keys.1.own), channel_id=1, source_target_pairs={{0,64},{64,0},{1,65},{65,1},{2,66},{66,2},{3,67},{67,3},{4,68},{68... | collective-permute-start | bytes 208904 | tf_op jit(solution)/shard_map/ppermute | solution.py:460
  6.7 0.6 copy-start.14
  10.0 30.0 %all-to-all-start = ((bf16[16,2,144,128]{3,2,1,0:T(8,128)(2,1)}), bf16[16,2,144,128]{3,2,1,0:T(8,128)(2,1)S(1)}, u32[]{:S(2)}, u32[]{:S(2)}) async-start(bf16[16,2,144,128]{3,2,1,0:T(8,128)(2,1)} %get-tuple-element.44), calls=%async_computation | async-start | bytes 2359296 | tf_op jit(solution)/shard_map/all_to_all | solution.py:468
  17.0 14.0 %collective-permute-start.4 = (bf16[64,1280]{1,0:T(8,128)(2,1)S(1)}, bf16[64,1280]{1,0:T(8,128)(2,1)S(1)}, u32[]{:S(2)}, u32[]{:S(2)}) collective-permute-start(bf16[64,1280]{1,0:T(8,128)(2,1)S(1)} %bitcast.11), channel_id=1, source_target_pairs={{0,3},{1,0},{2,1},{3,2},{4,7},{5,4},{6,5},{7,6},{8,11},{9,8},{10,9... | collective-permute-start | bytes 491528 | tf_op jit(solution)/shard_map/ppermute | solution.py:434
  22.5 14.6 %collective-permute-start.2 = (bf16[64,1280]{1,0:T(8,128)(2,1)S(1)}, bf16[64,1280]{1,0:T(8,128)(2,1)S(1)}, u32[]{:S(2)}, u32[]{:S(2)}) collective-permute-start(bf16[64,1280]{1,0:T(8,128)(2,1)S(1)} %bitcast.12), channel_id=1, source_target_pairs={{0,1},{1,2},{2,3},{3,0},{4,5},{5,6},{6,7},{7,4},{8,9},{9,10},{10,1... | collective-permute-start | bytes 491528 | tf_op jit(solution)/shard_map/ppermute | solution.py:434
  22.5 16.8 %collective-permute-start.1 = (bf16[64,1280]{1,0:T(8,128)(2,1)S(1)}, bf16[64,1280]{1,0:T(8,128)(2,1)S(1)}, u32[]{:S(2)}, u32[]{:S(2)}) collective-permute-start(bf16[64,1280]{1,0:T(8,128)(2,1)S(1)} %copy-done.5), channel_id=1, source_target_pairs={{0,1},{1,2},{2,3},{3,0},{4,5},{5,6},{6,7},{7,4},{8,9},{9,10},{10,1... | collective-permute-start | bytes 491528 | tf_op jit(solution)/shard_map/ppermute | solution.py:434
  24.5 15.4 %collective-permute-start.3 = (bf16[64,1280]{1,0:T(8,128)(2,1)S(1)}, bf16[64,1280]{1,0:T(8,128)(2,1)}, u32[]{:S(2)}, u32[]{:S(2)}) collective-permute-start(bf16[64,1280]{1,0:T(8,128)(2,1)S(1)} %copy-done.5), channel_id=1, source_target_pairs={{0,3},{1,0},{2,1},{3,2},{4,7},{5,4},{6,5},{7,6},{8,11},{9,8},{10,9... | collective-permute-start | bytes 491528 | tf_op jit(solution)/shard_map/ppermute | solution.py:434
  31.0 8.2 %copy-start.7 = (bf16[64,1280]{1,0:T(8,128)(2,1)}, bf16[64,1280]{1,0:T(8,128)(2,1)S(1)}, u32[]{:S(2)}) copy-start(bf16[64,1280]{1,0:T(8,128)(2,1)S(1)} %collective-permute-done.4.refs_3_) | copy-start | bytes 491524
  37.1 2.2 %copy-start.8 = (bf16[64,1280]{1,0:T(8,128)(2,1)}, bf16[64,1280]{1,0:T(8,128)(2,1)S(1)}, u32[]{:S(2)}) copy-start(bf16[64,1280]{1,0:T(8,128)(2,1)S(1)} %collective-permute-done.2.refs_7_) | copy-start | bytes 491524
  39.3 0.7 copy-start.9
  40.0 10.1 %copy-start = (bf16[16,2,144,128]{3,2,1,0:T(8,128)(2,1)}, bf16[16,2,144,128]{3,2,1,0:T(8,128)(2,1)S(1)}, u32[]{:S(2)}) copy-start(bf16[16,2,144,128]{3,2,1,0:T(8,128)(2,1)S(1)} %all-to-all-done.own) | copy-start | bytes 3538948
  40.0 10.1 %collective-permute-start.5 = (bf16[16,2,144,128]{3,2,1,0:T(8,128)(2,1)S(1)}, bf16[16,2,144,128]{3,2,1,0:T(8,128)(2,1)S(1)}, u32[]{:S(2)}, u32[]{:S(2)}) collective-permute-start(bf16[16,2,144,128]{3,2,1,0:T(8,128)(2,1)S(1)} %all-to-all-done.own), channel_id=1, source_target_pairs={{0,128},{128,0},{1,129},{129,1},{2,130},{130,2},{3,131},{131,3},{4... | collective-permute-start | bytes 3538952 | tf_op jit(solution)/shard_map/ppermute | solution.py:474
  40.1 29.6 %all-to-all-start.1 = ((bf16[16,2,128,128]{3,2,1,0:T(8,128)(2,1)}), bf16[16,2,128,128]{3,2,1,0:T(8,128)(2,1)S(1)}, u32[]{:S(2)}, u32[]{:S(2)}) async-start(bf16[16,2,128,128]{3,2,1,0:T(8,128)(2,1)} %get-tuple-element.46), calls=%async_computation.1 | async-start | bytes 2097152 | tf_op jit(solution)/shard_map/all_to_all | solution.py:473
  47.0 22.0 %collective-permute-start.7 = (bf16[64,1280]{1,0:T(8,128)(2,1)}, bf16[64,1280]{1,0:T(8,128)(2,1)S(1)}, u32[]{:S(2)}, u32[]{:S(2)}) collective-permute-start(bf16[64,1280]{1,0:T(8,128)(2,1)} %copy-done.7), channel_id=1, source_target_pairs={{0,3},{1,0},{2,1},{3,2},{4,7},{5,4},{6,5},{7,6},{8,11},{9,8},{10,9... | collective-permute-start | bytes 491528 | tf_op jit(solution)/shard_map/ppermute | solution.py:434
  47.5 22.1 %collective-permute-start.6 = (bf16[64,1280]{1,0:T(8,128)(2,1)}, bf16[64,1280]{1,0:T(8,128)(2,1)}, u32[]{:S(2)}, u32[]{:S(2)}) collective-permute-start(bf16[64,1280]{1,0:T(8,128)(2,1)} %copy-done.9), channel_id=1, source_target_pairs={{0,1},{1,2},{2,3},{3,0},{4,5},{5,6},{6,7},{7,4},{8,9},{9,10},{10,1... | collective-permute-start | bytes 491528 | tf_op jit(solution)/shard_map/ppermute | solution.py:434
  50.0 1.0 copy-start.4
  63.2 30.2 %collective-permute-start.8 = (bf16[64,1280]{1,0:T(8,128)(2,1)}, bf16[64,1280]{1,0:T(8,128)(2,1)S(1)}, u32[]{:S(2)}, u32[]{:S(2)}) collective-permute-start(bf16[64,1280]{1,0:T(8,128)(2,1)} %get-tuple-element.57), channel_id=1, source_target_pairs={{0,1},{1,2},{2,3},{3,0},{4,5},{5,6},{6,7},{7,4},{8,9},{9,10},{10,1... | collective-permute-start | bytes 491528 | tf_op jit(solution)/shard_map/ppermute | solution.py:434
  63.7 29.8 %collective-permute-start.9 = (bf16[64,1280]{1,0:T(8,128)(2,1)}, bf16[64,1280]{1,0:T(8,128)(2,1)S(1)}, u32[]{:S(2)}, u32[]{:S(2)}) collective-permute-start(bf16[64,1280]{1,0:T(8,128)(2,1)} %get-tuple-element.58), channel_id=1, source_target_pairs={{0,2},{1,3},{2,0},{3,1},{4,6},{5,7},{6,4},{7,5},{8,10},{9,11},{10,... | collective-permute-start | bytes 491528 | tf_op jit(solution)/shard_map/ppermute | solution.py:434
  67.3 26.1 %collective-permute-start.10 = (bf16[64,1280]{1,0:T(8,128)(2,1)}, bf16[64,1280]{1,0:T(8,128)(2,1)S(1)}, u32[]{:S(2)}, u32[]{:S(2)}) collective-permute-start(bf16[64,1280]{1,0:T(8,128)(2,1)} %get-tuple-element.59), channel_id=1, source_target_pairs={{0,3},{1,0},{2,1},{3,2},{4,7},{5,4},{6,5},{7,6},{8,11},{9,8},{10,9... | collective-permute-start | bytes 491528 | tf_op jit(solution)/shard_map/ppermute | solution.py:434
  69.0 0.7 copy-start.13
  69.6 1.0 copy-start.1
  84.5 9.0 %copy-start.3 = (bf16[64,1280]{1,0:T(8,128)(2,1)S(1)}, bf16[64,1280]{1,0:T(8,128)(2,1)}, u32[]{:S(2)}) copy-start(bf16[64,1280]{1,0:T(8,128)(2,1)} %get-tuple-element.56) | copy-start | bytes 491524
  84.5 46.7 %all-to-all-start.3 = ((bf16[32,128,128]{2,1,0:T(8,128)(2,1)}), bf16[32,128,128]{2,1,0:T(8,128)(2,1)S(1)}, u32[]{:S(2)}, u32[]{:S(2)}) async-start(bf16[32,128,128]{2,1,0:T(8,128)(2,1)} %get-tuple-element.74), calls=%async_computation.3 | async-start | bytes 2097152 | tf_op jit(solution)/shard_map/all_to_all | solution.py:511
  94.2 13.3 %copy-start.12 = (bf16[64,1280]{1,0:T(8,128)(2,1)S(1)}, bf16[64,1280]{1,0:T(8,128)(2,1)}, u32[]{:S(2)}) copy-start(bf16[64,1280]{1,0:T(8,128)(2,1)} %get-tuple-element.67) | copy-start | bytes 491524
  94.2 14.6 %copy-start.11 = (bf16[64,1280]{1,0:T(8,128)(2,1)S(1)}, bf16[64,1280]{1,0:T(8,128)(2,1)}, u32[]{:S(2)}) copy-start(bf16[64,1280]{1,0:T(8,128)(2,1)} %get-tuple-element.68) | copy-start | bytes 491524
  94.2 17.9 %copy-start.10 = (bf16[64,1280]{1,0:T(8,128)(2,1)S(1)}, bf16[64,1280]{1,0:T(8,128)(2,1)}, u32[]{:S(2)}) copy-start(bf16[64,1280]{1,0:T(8,128)(2,1)} %get-tuple-element.69) | copy-start | bytes 491524
  94.2 34.6 %copy-start.2 = (bf16[64,1280]{1,0:T(8,128)(2,1)S(1)}, bf16[64,1280]{1,0:T(8,128)(2,1)}, u32[]{:S(2)}) copy-start(bf16[64,1280]{1,0:T(8,128)(2,1)} %get-tuple-element.66) | copy-start | bytes 491524
  107.4 22.2 %collective-permute-start.11 = (bf16[32,128,128]{2,1,0:T(8,128)(2,1)}, bf16[32,128,128]{2,1,0:T(8,128)(2,1)S(1)}, u32[]{:S(2)}, u32[]{:S(2)}) collective-permute-start(bf16[32,128,128]{2,1,0:T(8,128)(2,1)} %get-tuple-element.65), channel_id=1, source_target_pairs={{0,128},{128,0},{1,129},{129,1},{2,130},{130,2},{3,131},{131,3},{4... | collective-permute-start | bytes 3145736 | tf_op jit(solution)/shard_map/ppermute | solution.py:525
  107.5 14.0 %collective-permute-start.12 = (bf16[64,1280]{1,0:T(8,128)(2,1)S(1)}, bf16[64,1280]{1,0:T(8,128)(2,1)S(1)}, u32[]{:S(2)}, u32[]{:S(2)}) collective-permute-start(bf16[64,1280]{1,0:T(8,128)(2,1)S(1)} %copy-done.12), channel_id=1, source_target_pairs={{0,1},{1,2},{2,3},{3,0},{4,5},{5,6},{6,7},{7,4},{8,9},{9,10},{10,1... | collective-permute-start | bytes 491528 | tf_op jit(solution)/shard_map/ppermute | solution.py:434
  108.8 15.2 %collective-permute-start.13 = (bf16[64,1280]{1,0:T(8,128)(2,1)S(1)}, bf16[64,1280]{1,0:T(8,128)(2,1)S(1)}, u32[]{:S(2)}, u32[]{:S(2)}) collective-permute-start(bf16[64,1280]{1,0:T(8,128)(2,1)S(1)} %copy-done.11), channel_id=1, source_target_pairs={{0,2},{1,3},{2,0},{3,1},{4,6},{5,7},{6,4},{7,5},{8,10},{9,11},{10,... | collective-permute-start | bytes 491528 | tf_op jit(solution)/shard_map/ppermute | solution.py:434
  112.1 16.8 %collective-permute-start.14 = (bf16[64,1280]{1,0:T(8,128)(2,1)S(1)}, bf16[64,1280]{1,0:T(8,128)(2,1)S(1)}, u32[]{:S(2)}, u32[]{:S(2)}) collective-permute-start(bf16[64,1280]{1,0:T(8,128)(2,1)S(1)} %copy-done.10), channel_id=1, source_target_pairs={{0,3},{1,0},{2,1},{3,2},{4,7},{5,4},{6,5},{7,6},{8,11},{9,8},{10,9... | collective-permute-start | bytes 491528 | tf_op jit(solution)/shard_map/ppermute | solution.py:434

commit v2 on v1

v2 whole, which is shorter than its diff:
```python
import math

import jax
import jax.numpy as jnp
from jax import lax
from jax.experimental import pallas as pl
from jax.experimental.pallas import tpu as pltpu
from jax.sharding import Mesh, PartitionSpec as P

HQ = 32
HK = 4
DH = 128
GROUP = HQ // HK
ROWS = 64
QROWS = GROUP * ROWS
HALF = 2048
NBLK = 32
KB = 512
PER = KB // ROWS
PACK = 2 * ROWS + 16
PLANE = 16
CTX = ("zl", "y", "x")
NEG = -1e30
SCALE = 1.0 / math.sqrt(DH)
EXP_SCALE = SCALE * math.log2(math.e)
MIB = 1 << 20
bf16 = jnp.bfloat16
f32 = jnp.float32
i32 = jnp.int32


def dot(a, b):
    return lax.dot_general(a, b, (((1,), (0,)), ((), ())), preferred_element_type=f32)


def dot_tn(a, b):
    return lax.dot_general(a, b, (((0,), (0,)), ((), ())), preferred_element_type=f32)


def dot_nt(a, b):
    return lax.dot_general(a, b, (((1,), (1,)), ((), ())), preferred_element_type=f32)


def stack_heads(ref):
    return jnp.concatenate([ref[:, h * DH : (h + 1) * DH] for h in range(GROUP)], axis=0)


def where_am_i():
    side = lax.axis_index("resp")
    place = (lax.axis_index("zl") * 4 + lax.axis_index("y")) * 4 + lax.axis_index("x")
    return side, place


def start_copies(pairs, sems):
    copies = [pltpu.make_async_copy(s, d, sems.at[n]) for n, (s, d) in enumerate(pairs)]
    for c in copies:
        c.start()
    return copies


def key_pairs(ref, first, row, kp, vp):
    level = lax.axis_index("zl")
    pairs = []
    for n, z in enumerate((level, 1 - level)):
        to = pl.ds(first + z * PLANE, PLANE)
        pairs.append((ref.at[:, n, row : row + 64, :], kp.at[to]))
        pairs.append((ref.at[:, n, row + 64 : row + 128, :], vp.at[to]))
    return pairs


def take(ref, first, rows):
    return ref[pl.ds(first, rows // ROWS), :, :].reshape(rows, DH)


def pick_start(doc, starts):
    low = jnp.where(doc >= 1, starts[0], 0)
    low = jnp.where(doc >= 2, starts[1], low)
    return jnp.where(doc >= 3, starts[2], low)


def key_positions(first, rows):
    return first + lax.broadcasted_iota(i32, (rows, QROWS), 0)


def lane_rows():
    return lax.broadcasted_iota(i32, (1, QROWS), 1) % ROWS


def head_lanes(row):
    return jnp.concatenate([row] * GROUP, axis=1)


def resp_range(resp_len, side, place):
    pos0 = place * ROWS
    live = resp_len[side]
    high = jnp.minimum(pos0 + lane_rows(), live - 1)
    blocks = jnp.minimum(pos0 + ROWS - 1, live - 1) // KB + 1
    return high, blocks


def pack_kernel(kp, vp, docs, kr, vr, out, ids, in_sems):
    copies = start_copies(
        [
            (docs, ids),
            (kp, out.at[0:64]),
            (vp, out.at[64:128]),
            (kr, out.at[PACK : PACK + 64]),
            (vr, out.at[PACK + 64 : PACK + 128]),
        ],
        in_sems,
    )
    copies[0].wait()
    row = jnp.concatenate([ids[...].astype(f32), jnp.full((1, DH - ROWS), 100.0, f32)], axis=1)
    out[128:144, :] = jnp.broadcast_to(row, (16, DH)).astype(bf16)
    for c in copies[1:]:
        c.wait()


def copies_kernel(own, other, out, both, in_sems, sems):
    for c in start_copies([(own, both.at[0]), (other, both.at[1])], in_sems):
        c.wait()
    for c in start_copies([(both, out.at[n]) for n in range(PLANE)], sems):
        c.wait()


def cotangent_kernel(*refs):
    pieces, out, sems = refs[:8], refs[8], refs[9]
    tp = lax.axis_index("tp")
    width = pieces[0].shape[1]
    pairs = []
    for n, ref in enumerate(pieces):
        cols = pl.ds(pl.multiple_of(lax.rem(tp + n // 2, 4) * width, width), width)
        pairs.append((ref, out.at[pl.ds((n % 2) * ROWS, ROWS), cols]))
    for c in start_copies(pairs, sems):
        c.wait()


def fwd_block(q_t, key, value, m_ref, l_ref, acc_ref, mask):
    z = dot(key, q_t) * EXP_SCALE
    if mask is not None:
        z = jnp.where(mask, z, NEG)
    old = m_ref[...]
    new = jnp.maximum(old, jnp.max(z, axis=0, keepdims=True))
    p = jnp.exp2(z - new)
    factor = jnp.exp2(old - new)
    m_ref[...] = new
    l_ref[...] = l_ref[...] * factor + jnp.sum(p, axis=0, keepdims=True)
    acc_ref[...] = acc_ref[...] * factor + dot_tn(value, p.astype(bf16))


def close_rows(m_ref, l_ref, acc_ref, att):
    total = l_ref[...]
    out = (acc_ref[...] / total).astype(bf16)
    rows = out.T
    for h in range(GROUP):
        att[:, h * DH : (h + 1) * DH] = rows[h * ROWS : (h + 1) * ROWS, :]
    return m_ref[...] + jnp.log2(total), out


def project(att, w_buf, tp, outs):
    all_att = att[...]
    width = outs[0].shape[1]
    for n, out in enumerate(outs):
        cols = pl.ds(pl.multiple_of(lax.rem(tp + n, 4) * width, width), width)
        res = dot(all_att, w_buf[:, cols]).astype(bf16)
        if isinstance(out, tuple):
            out[0][...] = res[0:ROWS]
            out[1][...] = res[ROWS : 2 * ROWS]
        else:
            out[...] = res


def row_deltas(d_t, out_t):
    return jnp.sum(d_t.astype(f32) * out_t.astype(f32), axis=0, keepdims=True)


def forward_kernel(
    doc_ids, resp_len, own, other, qp_in, qr_in, weight, cot_in,
    out0, out1, out2p, out2r, out3, d_out, stats, win,
    kp, vp, kr, vr, docs, qp, qr, w_buf, cot, att, m_ref, l_ref, acc_ref,
    q_sems, sems, d_sems, r_sems, w_sem, c_sem,
):
    side, place = where_am_i()
    tp = lax.axis_index("tp")
    level = lax.axis_index("zl")
    q_copies = start_copies([(qp_in, qp), (qr_in, qr)], q_sems)
    pairs = []
    for ref, first in ((own, side * NBLK), (other, (1 - side) * NBLK)):
        for n, z in enumerate((level, 1 - level)):
            pairs.append((ref.at[:, n, 128:144, :], docs.at[pl.ds(first + z * PLANE, PLANE)]))
    d_copies = start_copies(pairs, d_sems)
    copies = start_copies(
        key_pairs(own, side * NBLK, 0, kp, vp) + key_pairs(other, (1 - side) * NBLK, 0, kp, vp),
        sems,
    )
    r_copies = start_copies(key_pairs(own, 0, PACK, kr, vr), r_sems)
    w_copy = pltpu.make_async_copy(weight, w_buf, w_sem)
    w_copy.start()
    c_copy = pltpu.make_async_copy(cot_in, cot, c_sem)
    c_copy.start()
    for c in q_copies:
        c.wait()
    q_t = stack_heads(qp).T
    r_t = stack_heads(qr).T
    for c in d_copies:
        c.wait()
    all_docs = docs[...].astype(f32).reshape(2 * NBLK * 16, DH)
    starts = []
    for value in (1.0, 2.0, 3.0):
        starts.append(jnp.sum(jnp.where(all_docs < value, 1.0 / 16, 0.0)).astype(i32))
    for c in copies:
        c.wait()

    def begin():
        m_ref[...] = jnp.full((1, QROWS), NEG, f32)
        l_ref[...] = jnp.zeros((1, QROWS), f32)
        acc_ref[...] = jnp.zeros((DH, QROWS), f32)

    begin()
    block = side * NBLK + place
    pos0 = block * ROWS
    low = pick_start(head_lanes(docs[block].astype(f32)[0:1, 0:ROWS]), starts)
    high = pos0 + lane_rows()
    low0 = pick_start(doc_ids[0], starts)
    win[0] = low0

    @pl.loop(low0 // KB, pos0 // KB + 1)
    def _(j):
        pos = key_positions(j * KB, KB)
        fwd_block(
            q_t, take(kp, j * PER, KB), take(vp, j * PER, KB), m_ref, l_ref, acc_ref,
            (pos >= low) & (pos <= high),
        )

    stats[0:1, :], out_p = close_rows(m_ref, l_ref, acc_ref, att.at[0:ROWS, :])
    c_copy.wait()
    w_copy.wait()
    d_all = dot(w_buf[...], cot[...].T).astype(bf16)
    for n in range(2):
        for h in range(GROUP):
            d_out[n, :, h * ROWS : (h + 1) * ROWS] = d_all[
                h * DH : (h + 1) * DH, n * ROWS : (n + 1) * ROWS
            ]
    stats[2:3, :] = row_deltas(d_out[0], out_p)
    begin()
    for j in range(4096 // KB):
        fwd_block(r_t, take(kp, j * PER, KB), take(vp, j * PER, KB), m_ref, l_ref, acc_ref, None)
    high, used = resp_range(resp_len, side, place)
    for c in r_copies:
        c.wait()

    @pl.loop(0, used)
    def _(j):
        pos = key_positions(j * KB, KB)
        fwd_block(
            r_t, take(kr, j * PER, KB), take(vr, j * PER, KB), m_ref, l_ref, acc_ref, pos <= high
        )

    stats[1:2, :], out_r = close_rows(m_ref, l_ref, acc_ref, att.at[ROWS : 2 * ROWS, :])
    stats[3:4, :] = row_deltas(d_out[1], out_r)
    stats[4:5, :] = low.astype(f32)
    project(att, w_buf, tp, (out0, out1, (out2p, out2r), out3))


def bwd_block(q_t, q_rows, d_t, d_rows, key, value, log_total, delta, gq_ref, mask):
    z = dot(key, q_t) * EXP_SCALE
    if mask is not None:
        z = jnp.where(mask, z, NEG)
    p = jnp.exp2(z - log_total)
    g_value = dot(p.astype(bf16), d_rows)
    dp = dot(value, d_t)
    ds = (p * (dp - delta)).astype(bf16)
    g_key = dot(ds, q_rows)
    gq_ref[...] += dot_tn(key, ds)
    return g_key, g_value


def store_q(gq_ref, out):
    rows = (gq_ref[...] * SCALE).astype(bf16).T
    for h in range(GROUP):
        out[:, h * DH : (h + 1) * DH] = rows[h * ROWS : (h + 1) * ROWS, :]


def query_side(q, d_att, stats, side):
    q_rows = stack_heads(q)
    d_t = d_att[side]
    return (q_rows.T, q_rows, d_t, d_t.T, stats[side : side + 1, :], stats[2 + side : 3 + side, :])


def store_keys(out, j, row, g_key, g_value):
    level = j * PER // PLANE
    n = jnp.abs(level - lax.axis_index("zl"))
    blocks = pl.ds(j * PER - level * PLANE, PER)
    out[blocks, n, row : row + 64, :] = (g_key * SCALE).astype(bf16).reshape(PER, ROWS, DH)
    out[blocks, n, row + 64 : row + 128, :] = g_value.astype(bf16).reshape(PER, ROWS, DH)


def half_of_prompt(base, first, pos0, low, kp, vp, gk, gv, prompt, resp, gqp_ref, gqr_ref, out):
    for j in range(HALF // KB):
        at = slice(j * KB, (j + 1) * KB)
        gk[at, :], gv[at, :] = bwd_block(
            *resp[:4], take(kp, j * PER, KB), take(vp, j * PER, KB), *resp[4:], gqr_ref, None
        )
    high = pos0 + lane_rows()
    last = jnp.minimum(pos0 // KB - base, HALF // KB - 1)

    @pl.loop(jnp.maximum(first // KB - base, 0), last + 1)
    def _(j):
        at = pl.ds(pl.multiple_of(j * KB, KB), KB)
        pos = key_positions((base + j) * KB, KB)
        g_key, g_value = bwd_block(
            *prompt[:4], take(kp, j * PER, KB), take(vp, j * PER, KB), *prompt[4:], gqp_ref,
            (pos >= low) & (pos <= high),
        )
        gk[at, :] += g_key
        gv[at, :] += g_value

    for j in range(HALF // KB):
        at = slice(j * KB, (j + 1) * KB)
        store_keys(out, j, 0, gk[at, :], gv[at, :])


def bwd_other_kernel(
    win, other, qp_in, qr_in, d_in, stats_in,
    g_out, gqp_ref, gqr_ref,
    kp, vp, qp, qr, d_att, stats, gk, gv, sems,
):
    side, place = where_am_i()
    copies = start_copies(
        [(qr_in, qr), (qp_in, qp), (d_in, d_att), (stats_in, stats)]
        + key_pairs(other, 0, 0, kp, vp),
        sems,
    )
    gqp_ref[...] = jnp.zeros((DH, QROWS), f32)
    gqr_ref[...] = jnp.zeros((DH, QROWS), f32)
    for c in copies:
        c.wait()
    half_of_prompt(
        (1 - side) * (HALF // KB), win[0], (side * NBLK + place) * ROWS, stats[4:5, :].astype(i32),
        kp, vp, gk, gv, query_side(qp, d_att, stats, 0), query_side(qr, d_att, stats, 1),
        gqp_ref, gqr_ref, g_out,
    )


def bwd_own_kernel(
    win, resp_len, own, qp_in, qr_in, d_in, stats_in, gqp_in, gqr_in,
    gq_p, gq_r, g_out,
    kp, vp, kr, vr, qp, qr, d_att, stats, gk, gv, gqp_ref, gqr_ref, sems, r_sems,
):
    side, place = where_am_i()
    copies = start_copies(
        [(qr_in, qr), (qp_in, qp), (d_in, d_att), (stats_in, stats)]
        + [(gqp_in, gqp_ref), (gqr_in, gqr_ref)]
        + key_pairs(own, 0, 0, kp, vp),
        sems,
    )
    r_copies = start_copies(key_pairs(own, 0, PACK, kr, vr), r_sems)
    for c in copies:
        c.wait()
    resp = query_side(qr, d_att, stats, 1)
    half_of_prompt(
        side * (HALF // KB), win[0], (side * NBLK + place) * ROWS, stats[4:5, :].astype(i32),
        kp, vp, gk, gv, query_side(qp, d_att, stats, 0), resp, gqp_ref, gqr_ref, g_out,
    )
    store_q(gqp_ref, gq_p)
    for c in r_copies:
        c.wait()
    high, used = resp_range(resp_len, side, place)

    @pl.loop(0, used)
    def _(j):
        pos = key_positions(j * KB, KB)
        g_key, g_value = bwd_block(
            *resp[:4], take(kr, j * PER, KB), take(vr, j * PER, KB), *resp[4:], gqr_ref, pos <= high
        )
        store_keys(g_out, j, 128, g_key, g_value)

    @pl.loop(used, HALF // KB)
    def _(j):
        zero = jnp.zeros((KB, DH), f32)
        store_keys(g_out, j, 128, zero, zero)

    store_q(gqr_ref, gq_r)


def sum_kernel(parts, mine, other):
    for n, out in ((0, mine), (1, other)):
        total = parts[0, n].astype(f32)
        for m in range(1, PLANE):
            total = total + parts[m, n].astype(f32)
        out[...] = total.astype(out.dtype)


def last_kernel(mine, other, gk_p, gv_p, gk_r, gv_r):
    total = mine[...] + other[...].astype(f32)
    for n, out in enumerate((gk_p, gv_p, gk_r, gv_r)):
        out[...] = total[n * ROWS : (n + 1) * ROWS, :].astype(bf16)


VM = pl.BlockSpec(memory_space=pltpu.VMEM)
SM = pl.BlockSpec(memory_space=pltpu.SMEM)
HB = pl.BlockSpec(memory_space=pltpu.HBM)
ANY = pl.BlockSpec(memory_space=pl.ANY)


def shape(*dims, dtype=bf16):
    return jax.ShapeDtypeStruct(dims, dtype)


def call(kernel, name, in_specs, outs, scratch, args, gflop, out_specs=None, limit=58):
    return pl.pallas_call(
        kernel,
        out_shape=outs,
        in_specs=in_specs,
        out_specs=out_specs or (VM,) * len(outs),
        scratch_shapes=scratch,
        compiler_params=pltpu.CompilerParams(vmem_limit_bytes=limit * MIB),
        cost_estimate=pl.CostEstimate(
            flops=int(gflop * 1e9), bytes_accessed=4 * 10**6, transcendentals=10**6
        ),
        name=name,
    )(*args)


def state_scratch():
    return [pltpu.VMEM((1, QROWS), f32), pltpu.VMEM((1, QROWS), f32), pltpu.VMEM((DH, QROWS), f32)]


def key_scratch(blocks):
    return [pltpu.VMEM((blocks, ROWS, DH), bf16), pltpu.VMEM((blocks, ROWS, DH), bf16)]


def sems(n):
    return pltpu.SemaphoreType.DMA((n,))


SWAP = [(0, 1), (1, 0)]


def shift(x, by):
    return lax.ppermute(x, "tp", [(n, (n + by) % 4) for n in range(4)])


def add(*terms):
    total = terms[0].astype(f32)
    for t in terms[1:]:
        total = total + t.astype(f32)
    return total.astype(bf16)


def body(q_prompt, k_prompt, v_prompt, doc_ids, q_resp, k_resp, v_resp, resp_len, out_weight,
         grad_prompt, grad_resp):
    q_resp, k_resp, v_resp, grad_resp = q_resp[0], k_resp[0], v_resp[0], grad_resp[0]
    part = grad_prompt.shape[1]
    cols = GROUP * DH
    row_vm = pltpu.VMEM((ROWS, cols), bf16)
    weight_vm = pltpu.VMEM(out_weight.shape, bf16)
    stats_vm = pltpu.VMEM((8, QROWS), f32)

    left_p, left_r = shift(grad_prompt, 1), shift(grad_resp, 1)
    right_p, right_r = shift(grad_prompt, -1), shift(grad_resp, -1)
    (pack,) = call(
        pack_kernel, "pack_keys", [HB] * 5, (shape(PACK + 2 * ROWS, DH),),
        [pltpu.VMEM((1, ROWS), i32), sems(5)],
        (k_prompt, v_prompt, doc_ids.reshape(1, ROWS), k_resp, v_resp), 0.1,
    )
    pack_z = lax.ppermute(pack, "zl", SWAP)
    (packs,) = call(
        copies_kernel, "copy_packs", [ANY] * 2, (shape(PLANE, 2, PACK + 2 * ROWS, DH),),
        [pltpu.VMEM((2, PACK + 2 * ROWS, DH), bf16), sems(2), sems(PLANE)],
        (pack, pack_z), 0.1, limit=16,
        out_specs=(HB,),
    )
    own = lax.all_to_all(packs, ("y", "x"), 0, 0, tiled=True)
    far_p, far_r = shift(left_p, 1), shift(right_r, -1)
    (cot,) = call(
        cotangent_kernel, "join_cotangent", [ANY] * 8, (shape(2 * ROWS, 4 * part),), [sems(8)],
        (grad_prompt, grad_resp, right_p, right_r, far_p, far_r, left_p, left_r), 0.1,
        out_specs=(HB,), limit=16,
    )
    own, cot = lax.optimization_barrier((own, cot))
    other = lax.ppermute(own[:, :, :PACK], "resp", SWAP)

    o0, o1, o2p, o2r, o3, d_att, stats, win = call(
        forward_kernel, "forward", [SM] * 2 + [ANY] * 2 + [HB] * 3 + [ANY],
        (
            shape(2 * ROWS, part), shape(2 * ROWS, part), shape(ROWS, part), shape(ROWS, part),
            shape(2 * ROWS, part), shape(2, DH, QROWS), shape(8, QROWS, dtype=f32),
            shape(4, dtype=i32),
        ),
        key_scratch(2 * NBLK)
        + key_scratch(NBLK)
        + [
            pltpu.VMEM((2 * NBLK, 16, DH), bf16), row_vm, row_vm, weight_vm,
            pltpu.VMEM((2 * ROWS, 4 * part), bf16), pltpu.VMEM((2 * ROWS, cols), bf16),
        ]
        + state_scratch()
        + [sems(2), sems(8), sems(4), sems(4)] + [pltpu.SemaphoreType.DMA(())] * 2,
        (
            doc_ids, resp_len, own, other, q_prompt, q_resp, out_weight, cot,
        ), 8,
        out_specs=(VM,) * 7 + (SM,), limit=40,
    )
    half_scratch = key_scratch(NBLK)
    side_scratch = [
        row_vm, row_vm, pltpu.VMEM((2, DH, QROWS), bf16), stats_vm,
        pltpu.VMEM((HALF, DH), f32), pltpu.VMEM((HALF, DH), f32),
    ]
    acc = shape(DH, QROWS, dtype=f32)
    g_other, gqp_acc, gqr_acc = call(
        bwd_other_kernel, "backward_other_half", [SM, ANY] + [HB] * 4,
        (shape(PLANE, 2, 2 * ROWS, DH), acc, acc),
        half_scratch + side_scratch + [sems(8)],
        (win, other, q_prompt, q_resp, d_att, stats), 4, limit=30,
    )
    g_in = lax.ppermute(g_other, "resp", SWAP)
    gq_p, gq_r, g_mine = call(
        bwd_own_kernel, "backward_own_half", [SM, SM, ANY] + [HB] * 6,
        (shape(ROWS, cols),) * 2 + (shape(PLANE, 2, 4 * ROWS, DH),),
        half_scratch + half_scratch + side_scratch
        + [pltpu.VMEM((DH, QROWS), f32)] * 2 + [sems(10), sems(4)],
        (win, resp_len, own, q_prompt, q_resp, d_att, stats, gqp_acc, gqr_acc), 7, limit=30,
    )
    sends = g_mine.at[:, :, : 2 * ROWS].set(add(g_mine[:, :, : 2 * ROWS], g_in))
    sends, o2p, o2r = lax.optimization_barrier((sends, o2p, o2r))
    parts = lax.all_to_all(sends, ("y", "x"), 0, 0, tiled=True)
    f_p, f_r = shift(o2p, 1), shift(o2r, -1)
    n1 = add(o1, jnp.pad(f_p, ((0, ROWS), (0, 0))))
    n3 = add(o3, jnp.pad(f_r, ((ROWS, 0), (0, 0))))
    left_out, right_out = shift(n1, 1), shift(n3, -1)
    out = add(o0, left_out, right_out)
    mine, other = call(
        sum_kernel, "sum_parts", [VM],
        (shape(4 * ROWS, DH, dtype=f32), shape(4 * ROWS, DH)), [], (parts,), 0.1, limit=16,
    )
    other = lax.ppermute(other, "zl", SWAP)
    gk_p, gv_p, gk_r, gv_r = call(
        last_kernel, "last_sum", [VM] * 2, (shape(ROWS, DH),) * 4, [], (mine, other), 0.1, limit=16,
    )
    return (out[:ROWS], out[ROWS:][None], gq_p, gk_p, gv_p, gq_r[None], gk_r[None], gv_r[None])


def solution(mesh):
    fine = Mesh(mesh.devices.reshape(2, 2, 4, 4, 4), ("resp", "zl", "y", "x", "tp"))
    rows = P(("resp",) + CTX, "tp")
    resp_rows = P("resp", CTX, "tp")
    in_specs = (
        rows, rows, rows, P(("resp",) + CTX), resp_rows, resp_rows, resp_rows, P(),
        P("tp", None), rows, resp_rows,
    )
    out_specs = (rows, resp_rows, rows, rows, rows, resp_rows, resp_rows, resp_rows)
    return jax.shard_map(body, mesh=fine, in_specs=in_specs, out_specs=out_specs, check_vma=False)
```

time: 157 us -> 127 us (0.81); the launches traced: 156 us -> 127 us
  blocking collectives: 23.6 us -> 0 us
  waiting for transfers between devices: 28 us -> 46.2 us
  starting transfers between devices: 52 us -> 39.4 us
  Pallas kernels: 44.1 us -> 35 us
  other arithmetic: 3.1 us -> 0.72 us
    all_to_all x1 -> x0, blocking collectives: 23.6 us -> none  [body(): sums_p = lax.all_to_all(add(g_mine, g_in), CTX, 0, 0, tiled=True)]
    pallas_call x6 -> x8, Pallas kernels: 44.1 us -> 35 us  [call(): pl.pallas_call(kernel, out_shape=outs, in_specs=in_specs, out_specs=out_s...]
    ppermute x12 -> x10, waiting for transfers between devices: 25.3 us -> 32.2 us  [shift(): return lax.ppermute(x, 'tp', [(n, (n + by) % 4) for n in range(4)])]
    ppermute x12 -> x10, starting transfers between devices: 27 us -> 20.4 us  [shift(): return lax.ppermute(x, 'tp', [(n, (n + by) % 4) for n in range(4)])]
    ppermute x1 -> x2, waiting for transfers between devices: 0.01 us -> 6.34 us  [the longest x1 3.51 us: body(): other = lax.ppermute(other, 'zl', SWAP)]
    all_to_all x3 -> x2, starting transfers between devices: 22.9 us -> 16.7 us  [the longest x1 9.49 us: body(): parts = lax.all_to_all(sends, ('y', 'x'), 0, 0, tiled=True)]
    all_to_all x3 -> x2, waiting for transfers between devices: 0.01 us -> 5.02 us  [the longest x1 5.02 us: body(): parts = lax.all_to_all(sends, ('y', 'x'), 0, 0, tiled=True)]
    convert_element_type x3, other arithmetic: 3.1 us -> 0.22 us  [add(): return total.astype(bf16)]
  transfers between devices with their start and end apart: 18 -> 16, of which waited for: 7 -> 11; matrix products, arithmetic and copies ran while one was open for 2% -> 1% of each run, Pallas kernels for 25% -> 8%
where the time goes in v2:
time: 127 us
  waiting for transfers between devices  46.2 us (36%)
  starting transfers between devices  39.4 us (31%)
  Pallas kernels  35 us (28%)
  local copies, waits for them, and re-layouts  4.98 us (4%)
    pallas_call x8, Pallas kernels, call(): pl.pallas_call(kernel, out_shape=outs, in_specs=in_specs, out_specs=out_s...  35 us
    ppermute x10, waiting for transfers between devices, shift(): return lax.ppermute(x, 'tp', [(n, (n + by) % 4) for n in range(4)])  32.2 us
    ppermute x10, starting transfers between devices, shift(): return lax.ppermute(x, 'tp', [(n, (n + by) % 4) for n in range(4)])  20.4 us
    all_to_all x1, starting transfers between devices, body(): parts = lax.all_to_all(sends, ('y', 'x'), 0, 0, tiled=True)  9.49 us
    all_to_all x1, starting transfers between devices, body(): own = lax.all_to_all(packs, ('y', 'x'), 0, 0, tiled=True)  7.18 us
    all_to_all x1, waiting for transfers between devices, body(): parts = lax.all_to_all(sends, ('y', 'x'), 0, 0, tiled=True)  5.02 us
    unnamed x40, local copies, waits for them, and re-layouts  4.16 us
    ppermute x1, waiting for transfers between devices, body(): other = lax.ppermute(other, 'zl', SWAP)  3.51 us
  transfers between devices with their start and end apart: 16, of which 11 were waited for; matrix products, arithmetic and copies ran while one was open for 1% of the time, Pallas kernels for 8%

profile of v2, /device:TPU:32, one launch (start us, length us, event | category | flops | bytes accessed | tf_op | source)
XLA Modules:
  0.0 127.3 jit_solution(14699706727609944980)
XLA Ops:
  0.6 1.5 %pack_keys.1.own = bf16[272,128]{1,0:T(8,128)(2,1)} custom-call(bf16[64,128]{1,0:T(8,128)(2,1)} %kp.1, bf16[64,128]{1,0:T(8,128)(2,1)} %vp.1, s32[1,64]{1,0:T(1,128)} %bitcast.16, bf16[64,128]{1,0:T(8,128)(2,1)} %bitcast.17, bf16[64,128]{1,0:T(8,128)(2,1)} %bitcast.18), custom_call_target="tpu_custom_call" | custom-call | flops 100000000 | bytes 4000000 | tf_op jit(solution)/shard_map/pack_keys/pallas_call | solution.py:411
  2.1 1.9 %collective-permute-start = (bf16[272,128]{1,0:T(8,128)(2,1)}, bf16[272,128]{1,0:T(8,128)(2,1)S(1)}, u32[]{:S(2)}, u32[]{:S(2)}) collective-permute-start(bf16[272,128]{1,0:T(8,128)(2,1)} %pack_keys.1.own), channel_id=1, source_target_pairs={{0,64},{64,0},{1,65},{65,1},{2,66},{66,2},{3,67},{67,3},{4,68},{68... | collective-permute-start | bytes 208904 | tf_op jit(solution)/shard_map/ppermute | solution.py:467
  4.0 2.7 %collective-permute-done.other = bf16[272,128]{1,0:T(8,128)(2,1)S(1)} collective-permute-done((bf16[272,128]{1,0:T(8,128)(2,1)}, bf16[272,128]{1,0:T(8,128)(2,1)S(1)}, u32[]{:S(2)}, u32[]{:S(2)}) %collective-permute-start) | collective-permute-done | bytes 69664 | tf_op jit(solution)/shard_map/ppermute | solution.py:467
  6.7 0.9 copy-done.11
  7.6 1.7 %copy_packs.1 = bf16[16,2,272,128]{3,2,1,0:T(8,128)(2,1)} custom-call(bf16[272,128]{1,0:T(8,128)(2,1)S(1)} %copy-done.11, bf16[272,128]{1,0:T(8,128)(2,1)S(1)} %collective-permute-done.other), custom_call_target="tpu_custom_call" | custom-call | flops 100000000 | bytes 4000000 | tf_op jit(solution)/shard_map/copy_packs/pallas_call | solution.py:411
  9.3 0.0 copy-start.9
  9.3 0.0 copy-start.7
  9.3 7.2 %all-to-all-start = ((bf16[16,2,272,128]{3,2,1,0:T(8,128)(2,1)}), bf16[16,2,272,128]{3,2,1,0:T(8,128)(2,1)S(1)}, u32[]{:S(2)}, u32[]{:S(2)}) async-start(bf16[16,2,272,128]{3,2,1,0:T(8,128)(2,1)} %copy_packs.1), calls=%async_computation | async-start | bytes 4456448 | tf_op jit(solution)/shard_map/all_to_all | solution.py:474
  16.5 0.0 copy-start.18
  16.5 0.0 copy-start.19
  16.5 0.0 copy-done.9
  16.5 5.5 %collective-permute-start.2 = (bf16[64,1280]{1,0:T(8,128)(2,1)S(1)}, bf16[64,1280]{1,0:T(8,128)(2,1)S(1)}, u32[]{:S(2)}, u32[]{:S(2)}) collective-permute-start(bf16[64,1280]{1,0:T(8,128)(2,1)S(1)} %bitcast.10), channel_id=1, source_target_pairs={{0,3},{1,0},{2,1},{3,2},{4,7},{5,4},{6,5},{7,6},{8,11},{9,8},{10,9... | collective-permute-start | bytes 491528 | tf_op jit(solution)/shard_map/ppermute | solution.py:441
  22.0 0.0 collective-permute-start.3
  22.0 2.0 %collective-permute-start.6 = (bf16[64,1280]{1,0:T(8,128)(2,1)S(1)}, bf16[64,1280]{1,0:T(8,128)(2,1)S(1)}, u32[]{:S(2)}, u32[]{:S(2)}) collective-permute-start(bf16[64,1280]{1,0:T(8,128)(2,1)S(1)} %bitcast.11), channel_id=1, source_target_pairs={{0,1},{1,2},{2,3},{3,0},{4,5},{5,6},{6,7},{7,4},{8,9},{9,10},{10,1... | collective-permute-start | bytes 491528 | tf_op jit(solution)/shard_map/ppermute | solution.py:441
  24.0 2.2 %collective-permute-start.1 = (bf16[64,1280]{1,0:T(8,128)(2,1)S(1)}, bf16[64,1280]{1,0:T(8,128)(2,1)S(1)}, u32[]{:S(2)}, u32[]{:S(2)}) collective-permute-start(bf16[64,1280]{1,0:T(8,128)(2,1)S(1)} %copy-done.7), channel_id=1, source_target_pairs={{0,3},{1,0},{2,1},{3,2},{4,7},{5,4},{6,5},{7,6},{8,11},{9,8},{10,9... | collective-permute-start | bytes 491528 | tf_op jit(solution)/shard_map/ppermute | solution.py:441
  26.2 4.3 %collective-permute-done.2.refs_3_ = bf16[64,1280]{1,0:T(8,128)(2,1)S(1)} collective-permute-done((bf16[64,1280]{1,0:T(8,128)(2,1)S(1)}, bf16[64,1280]{1,0:T(8,128)(2,1)S(1)}, u32[]{:S(2)}, u32[]{:S(2)}) %collective-permute-start.2) | collective-permute-done | bytes 163872 | tf_op jit(solution)/shard_map/ppermute | solution.py:441
  30.4 4.7 %collective-permute-start.5 = (bf16[64,1280]{1,0:T(8,128)(2,1)S(1)}, bf16[64,1280]{1,0:T(8,128)(2,1)S(1)}, u32[]{:S(2)}, u32[]{:S(2)}) collective-permute-start(bf16[64,1280]{1,0:T(8,128)(2,1)S(1)} %collective-permute-done.2.refs_3_), channel_id=1, source_target_pairs={{0,3},{1,0},{2,1},{3,2},{4,7},{5,4},{6,5},{7,6},{8,11},{9,8},{10,9... | collective-permute-start | bytes 491528 | tf_op jit(solution)/shard_map/ppermute | solution.py:441
  35.1 3.2 %collective-permute-done.3.refs_6_ = bf16[64,1280]{1,0:T(8,128)(2,1)S(1)} collective-permute-done((bf16[64,1280]{1,0:T(8,128)(2,1)S(1)}, bf16[64,1280]{1,0:T(8,128)(2,1)S(1)}, u32[]{:S(2)}, u32[]{:S(2)}) %collective-permute-start.3) | collective-permute-done | bytes 163872 | tf_op jit(solution)/shard_map/ppermute | solution.py:441
  38.4 0.0 collective-permute-start.4
  38.4 3.5 %collective-permute-done.6.refs_7_ = bf16[64,1280]{1,0:T(8,128)(2,1)S(1)} collective-permute-done((bf16[64,1280]{1,0:T(8,128)(2,1)S(1)}, bf16[64,1280]{1,0:T(8,128)(2,1)S(1)}, u32[]{:S(2)}, u32[]{:S(2)}) %collective-permute-start.6) | collective-permute-done | bytes 163872 | tf_op jit(solution)/shard_map/ppermute | solution.py:441
  41.9 0.0 collective-permute-done.1.refs_2_
  41.9 0.0 collective-permute-done.5.refs_5_
  41.9 4.5 %collective-permute-done.4.refs_4_ = bf16[64,1280]{1,0:T(8,128)(2,1)S(1)} collective-permute-done((bf16[64,1280]{1,0:T(8,128)(2,1)S(1)}, bf16[64,1280]{1,0:T(8,128)(2,1)S(1)}, u32[]{:S(2)}, u32[]{:S(2)}) %collective-permute-start.4) | collective-permute-done | bytes 163872 | tf_op jit(solution)/shard_map/ppermute | solution.py:441
  46.4 0.9 copy-done.8
  47.3 0.9 copy-done.10
  48.3 0.3 join_cotangent.1.cot_in
  48.5 0.0 all-to-all-done.own
  48.6 0.0 copy-start.16
  48.6 0.0 copy-start.17
  48.6 0.1 slice.39
  48.7 0.1 collective-permute-start.7
  48.8 2.8 %collective-permute-done.7.other = bf16[16,2,144,128]{3,2,1,0:T(8,128)(2,1)S(1)} collective-permute-done((bf16[16,2,144,128]{3,2,1,0:T(8,128)(2,1)S(1)}, bf16[16,2,144,128]{3,2,1,0:T(8,128)(2,1)S(1)}, u32[]{:S(2)}, u32[]{:S(2)}) %collective-permute-start.7) | collective-permute-done | bytes 1179680 | tf_op jit(solution)/shard_map/ppermute | solution.py:482
  51.6 0.0 copy-done.16
  51.6 15.9 %forward.1 = (bf16[128,1280]{1,0:T(8,128)(2,1)S(1)}, bf16[128,1280]{1,0:T(8,128)(2,1)S(1)}, bf16[64,1280]{1,0:T(8,128)(2,1)S(1)}, bf16[64,1280]{1,0:T(8,128)(2,1...) custom-call(s32[64]{0:T(128)S(1)} %copy-done.18, ...), custom_call_target="tpu_custom_call" | custom-call | flops 8000000000 | bytes 4000000 | tf_op jit(solution)/shard_map/forward/pallas_call | solution.py:411
  67.5 0.0 copy-start.1
  67.5 0.0 copy-start.3
  67.5 0.0 copy-start.5
  67.5 0.0 copy-start.12
  67.5 0.0 copy-start.14
  67.5 4.4 %backward_other_half.1 = (bf16[16,2,128,128]{3,2,1,0:T(8,128)(2,1)S(1)}, f32[128,512]{1,0:T(8,128)S(1)}, f32[128,512]{1,0:T(8,128)S(1)}) custom-call(s32[4]{0:T(128)S(1)} %get-tuple-element.49.win, bf16[16,2,144,128]{3,2,1,0:T(8,128)(2,1)S(1)} %collective-permute-done.7.other, bf16[64,1024]{1,0:T(8,128)(2,1)S(1)} %copy-done.16, ...), custom_call_target="tpu_custom_call" | custom-call | flops 4000000000 | bytes 4000000 | tf_op jit(solution)/shard_map/backward_other_half/pallas_call | solution.py:411
  72.0 0.2 collective-permute-start.8
  72.2 10.4 %backward_own_half.1 = (bf16[64,1024]{1,0:T(8,128)(2,1)}, bf16[64,1024]{1,0:T(8,128)(2,1)}, bf16[16,2,256,128]{3,2,1,0:T(8,128)(2,1)S(1)}) custom-call(s32[4]{0:T(128)S(1)} %get-tuple-element.49.win, s32[2]{0:T(128)S(1)} %copy-done.19, bf16[16,2,272,128]{3,2,1,0:T(8,128)(2,1)S(1)} %all-to-all-done.own, bf16[64,1024]{1,0:T(8,128)(2,1)S(1)} %copy-done.16, ...), custom_call_target="tpu_custom_call" | custom-call | flops 7000000000 | bytes 4000000 | tf_op jit(solution)/shard_map/backward_own_half/pallas_call | solution.py:411
  82.6 0.0 collective-permute-done.8
  82.6 0.5 fusion
  83.2 1.4 %copy-done = bf16[16,2,256,128]{3,2,1,0:T(8,128)(2,1)} copy-done((bf16[16,2,256,128]{3,2,1,0:T(8,128)(2,1)}, bf16[16,2,256,128]{3,2,1,0:T(8,128)(2,1)S(1)}, u32[]{:S(2)}) %copy-start) | copy-done | bytes 2097176
  84.5 0.0 copy-start.2
  84.5 9.5 %all-to-all-start.1 = ((bf16[16,2,256,128]{3,2,1,0:T(8,128)(2,1)}), bf16[16,2,256,128]{3,2,1,0:T(8,128)(2,1)S(1)}, u32[]{:S(2)}, u32[]{:S(2)}) async-start(bf16[16,2,256,128]{3,2,1,0:T(8,128)(2,1)} %copy-done), calls=%async_computation.1 | async-start | bytes 4194304 | tf_op jit(solution)/shard_map/all_to_all | solution.py:526
  94.0 0.3 collective-permute-start.11
  94.3 2.7 %collective-permute-start.9 = (bf16[64,1280]{1,0:T(8,128)(2,1)S(1)}, bf16[64,1280]{1,0:T(8,128)(2,1)S(1)}, u32[]{:S(2)}, u32[]{:S(2)}) collective-permute-start(bf16[64,1280]{1,0:T(8,128)(2,1)S(1)} %copy-done.13), channel_id=1, source_target_pairs={{0,1},{1,2},{2,3},{3,0},{4,5},{5,6},{6,7},{7,4},{8,9},{9,10},{10,1... | collective-permute-start | bytes 491528 | tf_op jit(solution)/shard_map/ppermute | solution.py:441
  97.0 10.4 %collective-permute-done.11 = bf16[64,1280]{1,0:T(8,128)(2,1)S(1)} collective-permute-done((bf16[64,1280]{1,0:T(8,128)(2,1)S(1)}, bf16[64,1280]{1,0:T(8,128)(2,1)S(1)}, u32[]{:S(2)}, u32[]{:S(2)}) %collective-permute-start.11) | collective-permute-done | bytes 163872 | tf_op jit(solution)/shard_map/ppermute | solution.py:441
  107.4 0.0 copy-done.6
  107.5 0.1 collective-permute-start.12
  107.6 0.0 collective-permute-done.9
  107.6 3.0 %collective-permute-start.10 = (bf16[128,1280]{1,0:T(8,128)(2,1)S(1)}, bf16[128,1280]{1,0:T(8,128)(2,1)S(1)}, u32[]{:S(2)}, u32[]{:S(2)}) collective-permute-start(bf16[128,1280]{1,0:T(8,128)(2,1)S(1)} %add_convert_fusion.3), channel_id=1, source_target_pairs={{0,1},{1,2},{2,3},{3,0},{4,5},{5,6},{6,7},{7,4},{8,9},{9,10},{10,1... | collective-permute-start | bytes 983048 | tf_op jit(solution)/shard_map/ppermute | solution.py:441
  110.6 4.9 %collective-permute-done.12 = bf16[128,1280]{1,0:T(8,128)(2,1)S(1)} collective-permute-done((bf16[128,1280]{1,0:T(8,128)(2,1)S(1)}, bf16[128,1280]{1,0:T(8,128)(2,1)S(1)}, u32[]{:S(2)}, u32[]{:S(2)}) %collective-permute-start.12) | collective-permute-done | bytes 327712 | tf_op jit(solution)/shard_map/ppermute | solution.py:441
  115.5 1.4 %collective-permute-done.10 = bf16[128,1280]{1,0:T(8,128)(2,1)S(1)} collective-permute-done((bf16[128,1280]{1,0:T(8,128)(2,1)S(1)}, bf16[128,1280]{1,0:T(8,128)(2,1)S(1)}, u32[]{:S(2)}, u32[]{:S(2)}) %collective-permute-start.10) | collective-permute-done | bytes 327712 | tf_op jit(solution)/shard_map/ppermute | solution.py:441
  116.9 0.0 copy-done.2
  116.9 0.1 add_convert_fusion.1
  117.0 5.0 %all-to-all-done.1.parts = bf16[16,2,256,128]{3,2,1,0:T(8,128)(2,1)S(1)} async-done(((bf16[16,2,256,128]{3,2,1,0:T(8,128)(2,1)}), bf16[16,2,256,128]{3,2,1,0:T(8,128)(2,1)S(1)}, u32[]{:S(2)}, u32[]{:S(2)}) %all-to-all-start.1) | async-done | bytes 2097184 | tf_op jit(solution)/shard_map/all_to_all | solution.py:526
  122.0 0.3 sum_parts.1
  122.3 0.1 collective-permute-start.13
  122.4 0.7 slice_bitcast_fusion
  123.1 3.5 %collective-permute-done.13.other = bf16[256,128]{1,0:T(8,128)(2,1)S(1)} collective-permute-done((bf16[256,128]{1,0:T(8,128)(2,1)S(1)}, bf16[256,128]{1,0:T(8,128)(2,1)S(1)}, u32[]{:S(2)}, u32[]{:S(2)}) %collective-permute-start.13) | collective-permute-done | bytes 65568 | tf_op jit(solution)/shard_map/ppermute | solution.py:536
  126.7 0.6 last_sum.1
  (22 shorter events, 0.1 us)
Async XLA Ops:
  2.1 4.6 %collective-permute-start = (bf16[272,128]{1,0:T(8,128)(2,1)}, bf16[272,128]{1,0:T(8,128)(2,1)S(1)}, u32[]{:S(2)}, u32[]{:S(2)}) collective-permute-start(bf16[272,128]{1,0:T(8,128)(2,1)} %pack_keys.1.own), channel_id=1, source_target_pairs={{0,64},{64,0},{1,65},{65,1},{2,66},{66,2},{3,67},{67,3},{4,68},{68... | collective-permute-start | bytes 208904 | tf_op jit(solution)/shard_map/ppermute | solution.py:467
  6.7 0.9 copy-start.11
  9.3 7.2 %copy-start.9 = (bf16[1,64,1280]{2,1,0:T(8,128)(2,1)S(1)}, bf16[1,64,1280]{2,1,0:T(8,128)(2,1)}, u32[]{:S(2)}) copy-start(bf16[1,64,1280]{2,1,0:T(8,128)(2,1)} %param.23) | copy-start | bytes 491524
  9.3 12.7 %copy-start.7 = (bf16[64,1280]{1,0:T(8,128)(2,1)S(1)}, bf16[64,1280]{1,0:T(8,128)(2,1)}, u32[]{:S(2)}) copy-start(bf16[64,1280]{1,0:T(8,128)(2,1)} %refs_0_.1) | copy-start | bytes 491524
  9.3 39.2 %all-to-all-start = ((bf16[16,2,272,128]{3,2,1,0:T(8,128)(2,1)}), bf16[16,2,272,128]{3,2,1,0:T(8,128)(2,1)S(1)}, u32[]{:S(2)}, u32[]{:S(2)}) async-start(bf16[16,2,272,128]{3,2,1,0:T(8,128)(2,1)} %copy_packs.1), calls=%async_computation | async-start | bytes 4456448 | tf_op jit(solution)/shard_map/all_to_all | solution.py:474
  16.5 35.1 %copy-start.18 = (s32[64]{0:T(128)S(1)}, s32[64]{0:T(128)}, u32[]{:S(2)}) copy-start(s32[64]{0:T(128)} %doc_ids.1) | copy-start | bytes 772
  16.5 35.1 %copy-start.19 = (s32[2]{0:T(128)S(1)}, s32[2]{0:T(128)}, u32[]{:S(2)}) copy-start(s32[2]{0:T(128)} %resp_len.3) | copy-start | bytes 28
  16.5 13.9 %collective-permute-start.2 = (bf16[64,1280]{1,0:T(8,128)(2,1)S(1)}, bf16[64,1280]{1,0:T(8,128)(2,1)S(1)}, u32[]{:S(2)}, u32[]{:S(2)}) collective-permute-start(bf16[64,1280]{1,0:T(8,128)(2,1)S(1)} %bitcast.10), channel_id=1, source_target_pairs={{0,3},{1,0},{2,1},{3,2},{4,7},{5,4},{6,5},{7,6},{8,11},{9,8},{10,9... | collective-permute-start | bytes 491528 | tf_op jit(solution)/shard_map/ppermute | solution.py:441
  22.0 16.3 %collective-permute-start.3 = (bf16[64,1280]{1,0:T(8,128)(2,1)S(1)}, bf16[64,1280]{1,0:T(8,128)(2,1)S(1)}, u32[]{:S(2)}, u32[]{:S(2)}) collective-permute-start(bf16[64,1280]{1,0:T(8,128)(2,1)S(1)} %copy-done.7), channel_id=1, source_target_pairs={{0,1},{1,2},{2,3},{3,0},{4,5},{5,6},{6,7},{7,4},{8,9},{9,10},{10,1... | collective-permute-start | bytes 491528 | tf_op jit(solution)/shard_map/ppermute | solution.py:441
  22.0 19.9 %collective-permute-start.6 = (bf16[64,1280]{1,0:T(8,128)(2,1)S(1)}, bf16[64,1280]{1,0:T(8,128)(2,1)S(1)}, u32[]{:S(2)}, u32[]{:S(2)}) collective-permute-start(bf16[64,1280]{1,0:T(8,128)(2,1)S(1)} %bitcast.11), channel_id=1, source_target_pairs={{0,1},{1,2},{2,3},{3,0},{4,5},{5,6},{6,7},{7,4},{8,9},{9,10},{10,1... | collective-permute-start | bytes 491528 | tf_op jit(solution)/shard_map/ppermute | solution.py:441
  24.0 17.9 %collective-permute-start.1 = (bf16[64,1280]{1,0:T(8,128)(2,1)S(1)}, bf16[64,1280]{1,0:T(8,128)(2,1)S(1)}, u32[]{:S(2)}, u32[]{:S(2)}) collective-permute-start(bf16[64,1280]{1,0:T(8,128)(2,1)S(1)} %copy-done.7), channel_id=1, source_target_pairs={{0,3},{1,0},{2,1},{3,2},{4,7},{5,4},{6,5},{7,6},{8,11},{9,8},{10,9... | collective-permute-start | bytes 491528 | tf_op jit(solution)/shard_map/ppermute | solution.py:441
  30.4 11.4 %collective-permute-start.5 = (bf16[64,1280]{1,0:T(8,128)(2,1)S(1)}, bf16[64,1280]{1,0:T(8,128)(2,1)S(1)}, u32[]{:S(2)}, u32[]{:S(2)}) collective-permute-start(bf16[64,1280]{1,0:T(8,128)(2,1)S(1)} %collective-permute-done.2.refs_3_), channel_id=1, source_target_pairs={{0,3},{1,0},{2,1},{3,2},{4,7},{5,4},{6,5},{7,6},{8,11},{9,8},{10,9... | collective-permute-start | bytes 491528 | tf_op jit(solution)/shard_map/ppermute | solution.py:441
  38.4 8.1 %collective-permute-start.4 = (bf16[64,1280]{1,0:T(8,128)(2,1)S(1)}, bf16[64,1280]{1,0:T(8,128)(2,1)S(1)}, u32[]{:S(2)}, u32[]{:S(2)}) collective-permute-start(bf16[64,1280]{1,0:T(8,128)(2,1)S(1)} %collective-permute-done.3.refs_6_), channel_id=1, source_target_pairs={{0,1},{1,2},{2,3},{3,0},{4,5},{5,6},{6,7},{7,4},{8,9},{9,10},{10,1... | collective-permute-start | bytes 491528 | tf_op jit(solution)/shard_map/ppermute | solution.py:441
  46.4 0.9 copy-start.8
  47.3 0.9 copy-start.10
  48.6 3.1 %copy-start.16 = (bf16[64,1024]{1,0:T(8,128)(2,1)S(1)}, bf16[64,1024]{1,0:T(8,128)(2,1)}, u32[]{:S(2)}) copy-start(bf16[64,1024]{1,0:T(8,128)(2,1)} %qp_in.5) | copy-start | bytes 393220
  48.6 3.0 %copy-start.17 = (bf16[1,64,1024]{2,1,0:T(8,128)(2,1)S(1)}, bf16[1,64,1024]{2,1,0:T(8,128)(2,1)}, u32[]{:S(2)}) copy-start(bf16[1,64,1024]{2,1,0:T(8,128)(2,1)} %param.17) | copy-start | bytes 393220
  48.7 2.9 %collective-permute-start.7 = (bf16[16,2,144,128]{3,2,1,0:T(8,128)(2,1)S(1)}, bf16[16,2,144,128]{3,2,1,0:T(8,128)(2,1)S(1)}, u32[]{:S(2)}, u32[]{:S(2)}) collective-permute-start(bf16[16,2,144,128]{3,2,1,0:T(8,128)(2,1)S(1)} %slice.39), channel_id=1, source_target_pairs={{0,128},{128,0},{1,129},{129,1},{2,130},{130,2},{3,131},{131,3},{4... | collective-permute-start | bytes 3538952 | tf_op jit(solution)/shard_map/ppermute | solution.py:482
  67.5 4.5 %copy-start.1 = (bf16[128,1280]{1,0:T(8,128)(2,1)}, bf16[128,1280]{1,0:T(8,128)(2,1)S(1)}, u32[]{:S(2)}) copy-start(bf16[128,1280]{1,0:T(8,128)(2,1)S(1)} %get-tuple-element.47) | copy-start | bytes 983044
  67.5 4.5 %copy-start.3 = (bf16[128,1280]{1,0:T(8,128)(2,1)}, bf16[128,1280]{1,0:T(8,128)(2,1)S(1)}, u32[]{:S(2)}) copy-start(bf16[128,1280]{1,0:T(8,128)(2,1)S(1)} %get-tuple-element.48) | copy-start | bytes 983044
  67.5 4.5 %copy-start.5 = (bf16[128,1280]{1,0:T(8,128)(2,1)}, bf16[128,1280]{1,0:T(8,128)(2,1)S(1)}, u32[]{:S(2)}) copy-start(bf16[128,1280]{1,0:T(8,128)(2,1)S(1)} %get-tuple-element.59) | copy-start | bytes 983044
  67.5 4.5 %copy-start.12 = (bf16[64,1280]{1,0:T(8,128)(2,1)}, bf16[64,1280]{1,0:T(8,128)(2,1)S(1)}, u32[]{:S(2)}) copy-start(bf16[64,1280]{1,0:T(8,128)(2,1)S(1)} %get-tuple-element.58) | copy-start | bytes 491524
  67.5 4.5 %copy-start.14 = (bf16[64,1280]{1,0:T(8,128)(2,1)}, bf16[64,1280]{1,0:T(8,128)(2,1)S(1)}, u32[]{:S(2)}) copy-start(bf16[64,1280]{1,0:T(8,128)(2,1)S(1)} %get-tuple-element.60) | copy-start | bytes 491524
  72.0 10.6 %collective-permute-start.8 = (bf16[16,2,128,128]{3,2,1,0:T(8,128)(2,1)S(1)}, bf16[16,2,128,128]{3,2,1,0:T(8,128)(2,1)S(1)}, u32[]{:S(2)}, u32[]{:S(2)}) collective-permute-start(bf16[16,2,128,128]{3,2,1,0:T(8,128)(2,1)S(1)} %get-tuple-element.55), channel_id=1, source_target_pairs={{0,128},{128,0},{1,129},{129,1},{2,130},{130,2},{3,131},{131,3},{4... | collective-permute-start | bytes 3145736 | tf_op jit(solution)/shard_map/ppermute | solution.py:516
  83.1 1.4 %copy-start = (bf16[16,2,256,128]{3,2,1,0:T(8,128)(2,1)}, bf16[16,2,256,128]{3,2,1,0:T(8,128)(2,1)S(1)}, u32[]{:S(2)}) copy-start(bf16[16,2,256,128]{3,2,1,0:T(8,128)(2,1)S(1)} %fusion) | copy-start | bytes 6291460
  84.5 9.5 %copy-start.15 = (bf16[64,1280]{1,0:T(8,128)(2,1)S(1)}, bf16[64,1280]{1,0:T(8,128)(2,1)}, u32[]{:S(2)}) copy-start(bf16[64,1280]{1,0:T(8,128)(2,1)} %copy-done.14) | copy-start | bytes 491524
  84.5 9.8 %copy-start.13 = (bf16[64,1280]{1,0:T(8,128)(2,1)S(1)}, bf16[64,1280]{1,0:T(8,128)(2,1)}, u32[]{:S(2)}) copy-start(bf16[64,1280]{1,0:T(8,128)(2,1)} %copy-done.12) | copy-start | bytes 491524
  84.5 22.9 %copy-start.6 = (bf16[128,1280]{1,0:T(8,128)(2,1)S(1)}, bf16[128,1280]{1,0:T(8,128)(2,1)}, u32[]{:S(2)}) copy-start(bf16[128,1280]{1,0:T(8,128)(2,1)} %copy-done.5) | copy-start | bytes 983044
  84.5 23.0 %copy-start.4 = (bf16[128,1280]{1,0:T(8,128)(2,1)S(1)}, bf16[128,1280]{1,0:T(8,128)(2,1)}, u32[]{:S(2)}) copy-start(bf16[128,1280]{1,0:T(8,128)(2,1)} %copy-done.3) | copy-start | bytes 983044
  84.5 32.4 %copy-start.2 = (bf16[128,1280]{1,0:T(8,128)(2,1)S(1)}, bf16[128,1280]{1,0:T(8,128)(2,1)}, u32[]{:S(2)}) copy-start(bf16[128,1280]{1,0:T(8,128)(2,1)} %copy-done.1) | copy-start | bytes 983044
  84.5 37.5 %all-to-all-start.1 = ((bf16[16,2,256,128]{3,2,1,0:T(8,128)(2,1)}), bf16[16,2,256,128]{3,2,1,0:T(8,128)(2,1)S(1)}, u32[]{:S(2)}, u32[]{:S(2)}) async-start(bf16[16,2,256,128]{3,2,1,0:T(8,128)(2,1)} %copy-done), calls=%async_computation.1 | async-start | bytes 4194304 | tf_op jit(solution)/shard_map/all_to_all | solution.py:526
  94.0 13.4 %collective-permute-start.11 = (bf16[64,1280]{1,0:T(8,128)(2,1)S(1)}, bf16[64,1280]{1,0:T(8,128)(2,1)S(1)}, u32[]{:S(2)}, u32[]{:S(2)}) collective-permute-start(bf16[64,1280]{1,0:T(8,128)(2,1)S(1)} %copy-done.15), channel_id=1, source_target_pairs={{0,3},{1,0},{2,1},{3,2},{4,7},{5,4},{6,5},{7,6},{8,11},{9,8},{10,9... | collective-permute-start | bytes 491528 | tf_op jit(solution)/shard_map/ppermute | solution.py:441
  94.3 13.2 %collective-permute-start.9 = (bf16[64,1280]{1,0:T(8,128)(2,1)S(1)}, bf16[64,1280]{1,0:T(8,128)(2,1)S(1)}, u32[]{:S(2)}, u32[]{:S(2)}) collective-permute-start(bf16[64,1280]{1,0:T(8,128)(2,1)S(1)} %copy-done.13), channel_id=1, source_target_pairs={{0,1},{1,2},{2,3},{3,0},{4,5},{5,6},{6,7},{7,4},{8,9},{9,10},{10,1... | collective-permute-start | bytes 491528 | tf_op jit(solution)/shard_map/ppermute | solution.py:441
  107.5 8.1 %collective-permute-start.12 = (bf16[128,1280]{1,0:T(8,128)(2,1)S(1)}, bf16[128,1280]{1,0:T(8,128)(2,1)S(1)}, u32[]{:S(2)}, u32[]{:S(2)}) collective-permute-start(bf16[128,1280]{1,0:T(8,128)(2,1)S(1)} %add_convert_fusion.2), channel_id=1, source_target_pairs={{0,3},{1,0},{2,1},{3,2},{4,7},{5,4},{6,5},{7,6},{8,11},{9,8},{10,9... | collective-permute-start | bytes 983048 | tf_op jit(solution)/shard_map/ppermute | solution.py:441
  107.6 9.3 %collective-permute-start.10 = (bf16[128,1280]{1,0:T(8,128)(2,1)S(1)}, bf16[128,1280]{1,0:T(8,128)(2,1)S(1)}, u32[]{:S(2)}, u32[]{:S(2)}) collective-permute-start(bf16[128,1280]{1,0:T(8,128)(2,1)S(1)} %add_convert_fusion.3), channel_id=1, source_target_pairs={{0,1},{1,2},{2,3},{3,0},{4,5},{5,6},{6,7},{7,4},{8,9},{9,10},{10,1... | collective-permute-start | bytes 983048 | tf_op jit(solution)/shard_map/ppermute | solution.py:441
  122.3 4.4 %collective-permute-start.13 = (bf16[256,128]{1,0:T(8,128)(2,1)S(1)}, bf16[256,128]{1,0:T(8,128)(2,1)S(1)}, u32[]{:S(2)}, u32[]{:S(2)}) collective-permute-start(bf16[256,128]{1,0:T(8,128)(2,1)S(1)} %get-tuple-element.64), channel_id=1, source_target_pairs={{0,64},{64,0},{1,65},{65,1},{2,66},{66,2},{3,67},{67,3},{4,68},{68... | collective-permute-start | bytes 196616 | tf_op jit(solution)/shard_map/ppermute | solution.py:536

commit v3 on v2

--- a/solution.py
+++ b/solution.py
@@ -17,6 +17,9 @@
 NBLK = 32
 KB = 512
 PER = KB // ROWS
+WIN = 11
+WKEYS = WIN * ROWS
+LONG = 1024
 PACK = 2 * ROWS + 16
 PLANE = 16
 CTX = ("zl", "y", "x")
@@ -94,7 +97,7 @@
     pos0 = place * ROWS
     live = resp_len[side]
     high = jnp.minimum(pos0 + lane_rows(), live - 1)
-    blocks = jnp.minimum(pos0 + ROWS - 1, live - 1) // KB + 1
+    blocks = jnp.minimum(pos0 + ROWS - 1, live - 1) // LONG + 1
     return high, blocks
 
 
@@ -133,6 +136,28 @@
         pairs.append((ref, out.at[pl.ds((n % 2) * ROWS, ROWS), cols]))
     for c in start_copies(pairs, sems):
         c.wait()
+
+
+def window(first, last, end):
+    groups = jnp.maximum(last - first + WIN, 0) // WIN
+    return groups, lambda t: (jnp.minimum(first + t * WIN, end - WIN), first + t * WIN)
+
+
+def fwd_run(q_t, kp, vp, m_ref, l_ref, acc_ref):
+    blocks = 4096 // KB
+    m, l = m_ref[...], l_ref[...]
+    z = dot(take(kp, 0, KB), q_t) * EXP_SCALE
+    for j in range(blocks):
+        ahead = dot(take(kp, (j + 1) * PER, KB), q_t) * EXP_SCALE if j + 1 < blocks else None
+        new = jnp.maximum(m, jnp.max(z, axis=0, keepdims=True))
+        p = jnp.exp2(z - new)
+        factor = jnp.exp2(m - new)
+        m = new
+        l = l * factor + jnp.sum(p, axis=0, keepdims=True)
+        acc_ref[...] = acc_ref[...] * factor + dot_tn(take(vp, j * PER, KB), p.astype(bf16))
+        z = ahead
+    m_ref[...] = m
+    l_ref[...] = l
 
 
 def fwd_block(q_t, key, value, m_ref, l_ref, acc_ref, mask):
@@ -224,12 +249,15 @@
     low0 = pick_start(doc_ids[0], starts)
     win[0] = low0
 
-    @pl.loop(low0 // KB, pos0 // KB + 1)
-    def _(j):
-        pos = key_positions(j * KB, KB)
+    groups, group = window(low0 // ROWS, block, 2 * NBLK)
+
+    @pl.loop(0, groups)
+    def _(t):
+        at, new = group(t)
+        pos = key_positions(at * ROWS, WKEYS)
         fwd_block(
-            q_t, take(kp, j * PER, KB), take(vp, j * PER, KB), m_ref, l_ref, acc_ref,
-            (pos >= low) & (pos <= high),
+            q_t, take(kp, at, WKEYS), take(vp, at, WKEYS), m_ref, l_ref, acc_ref,
+            (pos >= jnp.maximum(low, new * ROWS)) & (pos <= high),
         )
 
     stats[0:1, :], out_p = close_rows(m_ref, l_ref, acc_ref, att.at[0:ROWS, :])
@@ -243,17 +271,17 @@
             ]
     stats[2:3, :] = row_deltas(d_out[0], out_p)
     begin()
-    for j in range(4096 // KB):
-        fwd_block(r_t, take(kp, j * PER, KB), take(vp, j * PER, KB), m_ref, l_ref, acc_ref, None)
+    fwd_run(r_t, kp, vp, m_ref, l_ref, acc_ref)
     high, used = resp_range(resp_len, side, place)
     for c in r_copies:
         c.wait()
 
     @pl.loop(0, used)
     def _(j):
-        pos = key_positions(j * KB, KB)
+        pos = key_positions(j * LONG, LONG)
+        at = j * (LONG // ROWS)
         fwd_block(
-            r_t, take(kr, j * PER, KB), take(vr, j * PER, KB), m_ref, l_ref, acc_ref, pos <= high
+            r_t, take(kr, at, LONG), take(vr, at, LONG), m_ref, l_ref, acc_ref, pos <= high
         )
 
     stats[1:2, :], out_r = close_rows(m_ref, l_ref, acc_ref, att.at[ROWS : 2 * ROWS, :])
@@ -262,19 +290,25 @@
     project(att, w_buf, tp, (out0, out1, (out2p, out2r), out3))
 
 
-def bwd_block(q_t, q_rows, d_t, d_rows, key, value, log_total, delta, gq_ref, mask):
-    z = dot(key, q_t) * EXP_SCALE
-    if mask is not None:
-        z = jnp.where(mask, z, NEG)
+def bwd_scores(side, key, value):
+    return dot(key, side[0]) * EXP_SCALE, dot(value, side[2])
+
+
+def bwd_finish(side, key, z, dp, gq_ref):
+    _, q_rows, _, d_rows, log_total, delta = side
     p = jnp.exp2(z - log_total)
     g_value = dot(p.astype(bf16), d_rows)
-    dp = dot(value, d_t)
     ds = (p * (dp - delta)).astype(bf16)
     g_key = dot(ds, q_rows)
     gq_ref[...] += dot_tn(key, ds)
     return g_key, g_value
 
 
+def bwd_block(side, key, value, gq_ref, mask):
+    z, dp = bwd_scores(side, key, value)
+    return bwd_finish(side, key, jnp.where(mask, z, NEG), dp, gq_ref)
+
+
 def store_q(gq_ref, out):
     rows = (gq_ref[...] * SCALE).astype(bf16).T
     for h in range(GROUP):
@@ -288,29 +322,38 @@
 
 
 def store_keys(out, j, row, g_key, g_value):
-    level = j * PER // PLANE
+    blocks = g_key.shape[0] // ROWS
+    level = j * blocks // PLANE
     n = jnp.abs(level - lax.axis_index("zl"))
-    blocks = pl.ds(j * PER - level * PLANE, PER)
-    out[blocks, n, row : row + 64, :] = (g_key * SCALE).astype(bf16).reshape(PER, ROWS, DH)
-    out[blocks, n, row + 64 : row + 128, :] = g_value.astype(bf16).reshape(PER, ROWS, DH)
-
-
-def half_of_prompt(base, first, pos0, low, kp, vp, gk, gv, prompt, resp, gqp_ref, gqr_ref, out):
-    for j in range(HALF // KB):
+    at = pl.ds(j * blocks - level * PLANE, blocks)
+    out[at, n, row : row + 64, :] = (g_key * SCALE).astype(bf16).reshape(blocks, ROWS, DH)
+    out[at, n, row + 64 : row + 128, :] = g_value.astype(bf16).reshape(blocks, ROWS, DH)
+
+
+def half_of_prompt(base, first, block, low, kp, vp, gk, gv, prompt, resp, gqp_ref, gqr_ref, out):
+    blocks = HALF // KB
+    z, dp = bwd_scores(resp, take(kp, 0, KB), take(vp, 0, KB))
+    for j in range(blocks):
         at = slice(j * KB, (j + 1) * KB)
-        gk[at, :], gv[at, :] = bwd_block(
-            *resp[:4], take(kp, j * PER, KB), take(vp, j * PER, KB), *resp[4:], gqr_ref, None
-        )
-    high = pos0 + lane_rows()
-    last = jnp.minimum(pos0 // KB - base, HALF // KB - 1)
-
-    @pl.loop(jnp.maximum(first // KB - base, 0), last + 1)
-    def _(j):
-        at = pl.ds(pl.multiple_of(j * KB, KB), KB)
-        pos = key_positions((base + j) * KB, KB)
+        if j + 1 < blocks:
+            ahead = bwd_scores(
+                resp, take(kp, (j + 1) * PER, KB), take(vp, (j + 1) * PER, KB)
+            )
+        gk[at, :], gv[at, :] = bwd_finish(resp, take(kp, j * PER, KB), z, dp, gqr_ref)
+        z, dp = ahead
+    high = block * ROWS + lane_rows()
+    groups, group = window(
+        jnp.maximum(first // ROWS - base, 0), jnp.minimum(block - base, NBLK - 1), NBLK
+    )
+
+    @pl.loop(0, groups)
+    def _(t):
+        here, new = group(t)
+        at = pl.ds(pl.multiple_of(here * ROWS, ROWS), WKEYS)
+        pos = key_positions((base + here) * ROWS, WKEYS)
         g_key, g_value = bwd_block(
-            *prompt[:4], take(kp, j * PER, KB), take(vp, j * PER, KB), *prompt[4:], gqp_ref,
-            (pos >= low) & (pos <= high),
+            prompt, take(kp, here, WKEYS), take(vp, here, WKEYS), gqp_ref,
+            (pos >= jnp.maximum(low, (base + new) * ROWS)) & (pos <= high),
         )
         gk[at, :] += g_key
         gv[at, :] += g_value
@@ -336,7 +379,7 @@
     for c in copies:
         c.wait()
     half_of_prompt(
-        (1 - side) * (HALF // KB), win[0], (side * NBLK + place) * ROWS, stats[4:5, :].astype(i32),
+        (1 - side) * NBLK, win[0], side * NBLK + place, stats[4:5, :].astype(i32),
         kp, vp, gk, gv, query_side(qp, d_att, stats, 0), query_side(qr, d_att, stats, 1),
         gqp_ref, gqr_ref, g_out,
     )
@@ -359,7 +402,7 @@
         c.wait()
     resp = query_side(qr, d_att, stats, 1)
     half_of_prompt(
-        side * (HALF // KB), win[0], (side * NBLK + place) * ROWS, stats[4:5, :].astype(i32),
+        side * NBLK, win[0], side * NBLK + place, stats[4:5, :].astype(i32),
         kp, vp, gk, gv, query_side(qp, d_att, stats, 0), resp, gqp_ref, gqr_ref, g_out,
     )
     store_q(gqp_ref, gq_p)
@@ -369,15 +412,16 @@
 
     @pl.loop(0, used)
     def _(j):
-        pos = key_positions(j * KB, KB)
+        pos = key_positions(j * LONG, LONG)
+        at = j * (LONG // ROWS)
         g_key, g_value = bwd_block(
-            *resp[:4], take(kr, j * PER, KB), take(vr, j * PER, KB), *resp[4:], gqr_ref, pos <= high
+            resp, take(kr, at, LONG), take(vr, at, LONG), gqr_ref, pos <= high
         )
         store_keys(g_out, j, 128, g_key, g_value)
 
-    @pl.loop(used, HALF // KB)
+    @pl.loop(used, HALF // LONG)
     def _(j):
-        zero = jnp.zeros((KB, DH), f32)
+        zero = jnp.zeros((LONG, DH), f32)
         store_keys(g_out, j, 128, zero, zero)
 
     store_q(gqr_ref, gq_r)

time: 127 us -> 127 us (level); the launches traced: 127 us -> 125 us
  Pallas kernels: 35 us -> 31 us
  waiting for transfers between devices: 46.2 us -> 49 us
    ppermute x10, waiting for transfers between devices: 32.2 us -> 36.5 us  [shift(): return lax.ppermute(x, 'tp', [(n, (n + by) % 4) for n in range(4)])]
    pallas_call x8, Pallas kernels: 35 us -> 31 us  [call(): pl.pallas_call(kernel, out_shape=outs, in_specs=in_specs, out_specs=out_s...]
    all_to_all x1, starting transfers between devices: 9.49 us -> 6.94 us  [body(): parts = lax.all_to_all(sends, ('y', 'x'), 0, 0, tiled=True)]
    ppermute x1, starting transfers between devices: 0.09 us -> 1.55 us  [body(): other = lax.ppermute(other, 'zl', SWAP)]
  transfers between devices with their start and end apart: 16 -> 16, of which waited for: 11 -> 12; matrix products, arithmetic and copies ran while one was open for 1% -> 1% of each run, Pallas kernels for 8% -> 7%
where the time goes in v3:
time: 127 us; the launch traced here: 125 us
  waiting for transfers between devices  49 us (39%)
  starting transfers between devices  38.5 us (30%)
  Pallas kernels  31 us (24%)
  local copies, waits for them, and re-layouts  4.98 us (4%)
    ppermute x10, waiting for transfers between devices, shift(): return lax.ppermute(x, 'tp', [(n, (n + by) % 4) for n in range(4)])  36.5 us
    pallas_call x8, Pallas kernels, call(): pl.pallas_call(kernel, out_shape=outs, in_specs=in_specs, out_specs=out_s...  31 us
    ppermute x10, starting transfers between devices, shift(): return lax.ppermute(x, 'tp', [(n, (n + by) % 4) for n in range(4)])  19.3 us
    all_to_all x1, starting transfers between devices, body(): own = lax.all_to_all(packs, ('y', 'x'), 0, 0, tiled=True)  7.18 us
    all_to_all x1, starting transfers between devices, body(): parts = lax.all_to_all(sends, ('y', 'x'), 0, 0, tiled=True)  6.94 us
    all_to_all x1, waiting for transfers between devices, body(): parts = lax.all_to_all(sends, ('y', 'x'), 0, 0, tiled=True)  4.72 us
    unnamed x40, local copies, waits for them, and re-layouts  4.16 us
    ppermute x1, waiting for transfers between devices, body(): other = lax.ppermute(own[:, :, :PACK], 'resp', SWAP)  2.83 us
  transfers between devices with their start and end apart: 16, of which 12 were waited for; matrix products, arithmetic and copies ran while one was open for 1% of the time, Pallas kernels for 7%

profile of v3, /device:TPU:32, one launch (start us, length us, event | category | flops | bytes accessed | tf_op | source)
XLA Modules:
  0.0 125.1 jit_solution(13367346851774028010)
XLA Ops:
  0.6 1.5 %pack_keys.1.own = bf16[272,128]{1,0:T(8,128)(2,1)} custom-call(bf16[64,128]{1,0:T(8,128)(2,1)} %kp.1, bf16[64,128]{1,0:T(8,128)(2,1)} %vp.1, s32[1,64]{1,0:T(1,128)} %bitcast.16, bf16[64,128]{1,0:T(8,128)(2,1)} %bitcast.17, bf16[64,128]{1,0:T(8,128)(2,1)} %bitcast.18), custom_call_target="tpu_custom_call" | custom-call | flops 100000000 | bytes 4000000 | tf_op jit(solution)/shard_map/pack_keys/pallas_call | solution.py:455
  2.1 1.9 %collective-permute-start = (bf16[272,128]{1,0:T(8,128)(2,1)}, bf16[272,128]{1,0:T(8,128)(2,1)S(1)}, u32[]{:S(2)}, u32[]{:S(2)}) collective-permute-start(bf16[272,128]{1,0:T(8,128)(2,1)} %pack_keys.1.own), channel_id=1, source_target_pairs={{0,64},{64,0},{1,65},{65,1},{2,66},{66,2},{3,67},{67,3},{4,68},{68... | collective-permute-start | bytes 208904 | tf_op jit(solution)/shard_map/ppermute | solution.py:511
  4.0 2.7 %collective-permute-done.other = bf16[272,128]{1,0:T(8,128)(2,1)S(1)} collective-permute-done((bf16[272,128]{1,0:T(8,128)(2,1)}, bf16[272,128]{1,0:T(8,128)(2,1)S(1)}, u32[]{:S(2)}, u32[]{:S(2)}) %collective-permute-start) | collective-permute-done | bytes 69664 | tf_op jit(solution)/shard_map/ppermute | solution.py:511
  6.7 0.9 copy-done.11
  7.6 1.7 %copy_packs.1 = bf16[16,2,272,128]{3,2,1,0:T(8,128)(2,1)} custom-call(bf16[272,128]{1,0:T(8,128)(2,1)S(1)} %copy-done.11, bf16[272,128]{1,0:T(8,128)(2,1)S(1)} %collective-permute-done.other), custom_call_target="tpu_custom_call" | custom-call | flops 100000000 | bytes 4000000 | tf_op jit(solution)/shard_map/copy_packs/pallas_call | solution.py:455
  9.3 0.0 copy-start.9
  9.3 0.0 copy-start.7
  9.3 7.2 %all-to-all-start = ((bf16[16,2,272,128]{3,2,1,0:T(8,128)(2,1)}), bf16[16,2,272,128]{3,2,1,0:T(8,128)(2,1)S(1)}, u32[]{:S(2)}, u32[]{:S(2)}) async-start(bf16[16,2,272,128]{3,2,1,0:T(8,128)(2,1)} %copy_packs.1), calls=%async_computation | async-start | bytes 4456448 | tf_op jit(solution)/shard_map/all_to_all | solution.py:518
  16.5 0.0 copy-start.18
  16.5 0.0 copy-start.19
  16.5 5.5 %collective-permute-start.2 = (bf16[64,1280]{1,0:T(8,128)(2,1)S(1)}, bf16[64,1280]{1,0:T(8,128)(2,1)S(1)}, u32[]{:S(2)}, u32[]{:S(2)}) collective-permute-start(bf16[64,1280]{1,0:T(8,128)(2,1)S(1)} %bitcast.10), channel_id=1, source_target_pairs={{0,3},{1,0},{2,1},{3,2},{4,7},{5,4},{6,5},{7,6},{8,11},{9,8},{10,9... | collective-permute-start | bytes 491528 | tf_op jit(solution)/shard_map/ppermute | solution.py:485
  22.0 0.0 collective-permute-start.3
  22.0 2.0 %collective-permute-start.6 = (bf16[64,1280]{1,0:T(8,128)(2,1)S(1)}, bf16[64,1280]{1,0:T(8,128)(2,1)S(1)}, u32[]{:S(2)}, u32[]{:S(2)}) collective-permute-start(bf16[64,1280]{1,0:T(8,128)(2,1)S(1)} %bitcast.11), channel_id=1, source_target_pairs={{0,1},{1,2},{2,3},{3,0},{4,5},{5,6},{6,7},{7,4},{8,9},{9,10},{10,1... | collective-permute-start | bytes 491528 | tf_op jit(solution)/shard_map/ppermute | solution.py:485
  24.0 2.2 %collective-permute-start.1 = (bf16[64,1280]{1,0:T(8,128)(2,1)S(1)}, bf16[64,1280]{1,0:T(8,128)(2,1)S(1)}, u32[]{:S(2)}, u32[]{:S(2)}) collective-permute-start(bf16[64,1280]{1,0:T(8,128)(2,1)S(1)} %copy-done.7), channel_id=1, source_target_pairs={{0,3},{1,0},{2,1},{3,2},{4,7},{5,4},{6,5},{7,6},{8,11},{9,8},{10,9... | collective-permute-start | bytes 491528 | tf_op jit(solution)/shard_map/ppermute | solution.py:485
  26.2 4.3 %collective-permute-done.2.refs_3_ = bf16[64,1280]{1,0:T(8,128)(2,1)S(1)} collective-permute-done((bf16[64,1280]{1,0:T(8,128)(2,1)S(1)}, bf16[64,1280]{1,0:T(8,128)(2,1)S(1)}, u32[]{:S(2)}, u32[]{:S(2)}) %collective-permute-start.2) | collective-permute-done | bytes 163872 | tf_op jit(solution)/shard_map/ppermute | solution.py:485
  30.4 4.7 %collective-permute-start.5 = (bf16[64,1280]{1,0:T(8,128)(2,1)S(1)}, bf16[64,1280]{1,0:T(8,128)(2,1)S(1)}, u32[]{:S(2)}, u32[]{:S(2)}) collective-permute-start(bf16[64,1280]{1,0:T(8,128)(2,1)S(1)} %collective-permute-done.2.refs_3_), channel_id=1, source_target_pairs={{0,3},{1,0},{2,1},{3,2},{4,7},{5,4},{6,5},{7,6},{8,11},{9,8},{10,9... | collective-permute-start | bytes 491528 | tf_op jit(solution)/shard_map/ppermute | solution.py:485
  35.1 3.2 %collective-permute-done.3.refs_6_ = bf16[64,1280]{1,0:T(8,128)(2,1)S(1)} collective-permute-done((bf16[64,1280]{1,0:T(8,128)(2,1)S(1)}, bf16[64,1280]{1,0:T(8,128)(2,1)S(1)}, u32[]{:S(2)}, u32[]{:S(2)}) %collective-permute-start.3) | collective-permute-done | bytes 163872 | tf_op jit(solution)/shard_map/ppermute | solution.py:485
  38.4 0.0 collective-permute-start.4
  38.4 3.5 %collective-permute-done.6.refs_7_ = bf16[64,1280]{1,0:T(8,128)(2,1)S(1)} collective-permute-done((bf16[64,1280]{1,0:T(8,128)(2,1)S(1)}, bf16[64,1280]{1,0:T(8,128)(2,1)S(1)}, u32[]{:S(2)}, u32[]{:S(2)}) %collective-permute-start.6) | collective-permute-done | bytes 163872 | tf_op jit(solution)/shard_map/ppermute | solution.py:485
  41.9 0.0 collective-permute-done.1.refs_2_
  41.9 0.0 collective-permute-done.5.refs_5_
  41.9 4.5 %collective-permute-done.4.refs_4_ = bf16[64,1280]{1,0:T(8,128)(2,1)S(1)} collective-permute-done((bf16[64,1280]{1,0:T(8,128)(2,1)S(1)}, bf16[64,1280]{1,0:T(8,128)(2,1)S(1)}, u32[]{:S(2)}, u32[]{:S(2)}) %collective-permute-start.4) | collective-permute-done | bytes 163872 | tf_op jit(solution)/shard_map/ppermute | solution.py:485
  46.4 0.9 copy-done.8
  47.3 0.9 copy-done.10
  48.3 0.3 join_cotangent.1.cot_in
  48.5 0.0 all-to-all-done.own
  48.6 0.0 copy-start.16
  48.6 0.0 copy-start.17
  48.6 0.1 slice.39
  48.7 0.1 collective-permute-start.7
  48.8 2.8 %collective-permute-done.7.other = bf16[16,2,144,128]{3,2,1,0:T(8,128)(2,1)S(1)} collective-permute-done((bf16[16,2,144,128]{3,2,1,0:T(8,128)(2,1)S(1)}, bf16[16,2,144,128]{3,2,1,0:T(8,128)(2,1)S(1)}, u32[]{:S(2)}, u32[]{:S(2)}) %collective-permute-start.7) | collective-permute-done | bytes 1179680 | tf_op jit(solution)/shard_map/ppermute | solution.py:526
  51.6 0.0 copy-done.16
  51.6 0.0 copy-done.17
  51.6 13.9 %forward.1 = (bf16[128,1280]{1,0:T(8,128)(2,1)S(1)}, bf16[128,1280]{1,0:T(8,128)(2,1)S(1)}, bf16[64,1280]{1,0:T(8,128)(2,1)S(1)}, bf16[64,1280]{1,0:T(8,128)(2,1...) custom-call(s32[64]{0:T(128)S(1)} %copy-done.18, ...), custom_call_target="tpu_custom_call" | custom-call | flops 8000000000 | bytes 4000000 | tf_op jit(solution)/shard_map/forward/pallas_call | solution.py:455
  65.5 0.0 copy-start.1
  65.6 0.0 copy-start.3
  65.6 0.0 copy-start.5
  65.6 0.0 copy-start.12
  65.6 0.0 copy-start.14
  65.6 3.9 %backward_other_half.1 = (bf16[16,2,128,128]{3,2,1,0:T(8,128)(2,1)S(1)}, f32[128,512]{1,0:T(8,128)S(1)}, f32[128,512]{1,0:T(8,128)S(1)}) custom-call(s32[4]{0:T(128)S(1)} %get-tuple-element.49.win, bf16[16,2,144,128]{3,2,1,0:T(8,128)(2,1)S(1)} %collective-permute-done.7.other, bf16[64,1024]{1,0:T(8,128)(2,1)S(1)} %copy-done.16, ...), custom_call_target="tpu_custom_call" | custom-call | flops 4000000000 | bytes 4000000 | tf_op jit(solution)/shard_map/backward_other_half/pallas_call | solution.py:455
  69.5 0.0 copy-done.1
  69.5 0.0 copy-done.3
  69.5 0.0 copy-done.5
  69.6 1.5 %collective-permute-start.8 = (bf16[16,2,128,128]{3,2,1,0:T(8,128)(2,1)S(1)}, bf16[16,2,128,128]{3,2,1,0:T(8,128)(2,1)S(1)}, u32[]{:S(2)}, u32[]{:S(2)}) collective-permute-start(bf16[16,2,128,128]{3,2,1,0:T(8,128)(2,1)S(1)} %get-tuple-element.55), channel_id=1, source_target_pairs={{0,128},{128,0},{1,129},{129,1},{2,130},{130,2},{3,131},{131,3},{4... | collective-permute-start | bytes 3145736 | tf_op jit(solution)/shard_map/ppermute | solution.py:560
  71.0 8.8 %backward_own_half.1 = (bf16[64,1024]{1,0:T(8,128)(2,1)}, bf16[64,1024]{1,0:T(8,128)(2,1)}, bf16[16,2,256,128]{3,2,1,0:T(8,128)(2,1)S(1)}) custom-call(s32[4]{0:T(128)S(1)} %get-tuple-element.49.win, s32[2]{0:T(128)S(1)} %copy-done.19, bf16[16,2,272,128]{3,2,1,0:T(8,128)(2,1)S(1)} %all-to-all-done.own, bf16[64,1024]{1,0:T(8,128)(2,1)S(1)} %copy-done.16, ...), custom_call_target="tpu_custom_call" | custom-call | flops 7000000000 | bytes 4000000 | tf_op jit(solution)/shard_map/backward_own_half/pallas_call | solution.py:455
  79.9 0.0 collective-permute-done.8
  79.9 0.5 fusion
  80.4 1.4 %copy-done = bf16[16,2,256,128]{3,2,1,0:T(8,128)(2,1)} copy-done((bf16[16,2,256,128]{3,2,1,0:T(8,128)(2,1)}, bf16[16,2,256,128]{3,2,1,0:T(8,128)(2,1)S(1)}, u32[]{:S(2)}) %copy-start) | copy-done | bytes 2097176
  81.8 6.9 %all-to-all-start.1 = ((bf16[16,2,256,128]{3,2,1,0:T(8,128)(2,1)}), bf16[16,2,256,128]{3,2,1,0:T(8,128)(2,1)S(1)}, u32[]{:S(2)}, u32[]{:S(2)}) async-start(bf16[16,2,256,128]{3,2,1,0:T(8,128)(2,1)} %copy-done), calls=%async_computation.1 | async-start | bytes 4194304 | tf_op jit(solution)/shard_map/all_to_all | solution.py:570
  88.7 1.4 %collective-permute-start.11 = (bf16[64,1280]{1,0:T(8,128)(2,1)S(1)}, bf16[64,1280]{1,0:T(8,128)(2,1)S(1)}, u32[]{:S(2)}, u32[]{:S(2)}) collective-permute-start(bf16[64,1280]{1,0:T(8,128)(2,1)S(1)} %copy-done.15), channel_id=1, source_target_pairs={{0,3},{1,0},{2,1},{3,2},{4,7},{5,4},{6,5},{7,6},{8,11},{9,8},{10,9... | collective-permute-start | bytes 491528 | tf_op jit(solution)/shard_map/ppermute | solution.py:485
  90.1 1.6 %collective-permute-start.9 = (bf16[64,1280]{1,0:T(8,128)(2,1)S(1)}, bf16[64,1280]{1,0:T(8,128)(2,1)S(1)}, u32[]{:S(2)}, u32[]{:S(2)}) collective-permute-start(bf16[64,1280]{1,0:T(8,128)(2,1)S(1)} %copy-done.13), channel_id=1, source_target_pairs={{0,1},{1,2},{2,3},{3,0},{4,5},{5,6},{6,7},{7,4},{8,9},{9,10},{10,1... | collective-permute-start | bytes 491528 | tf_op jit(solution)/shard_map/ppermute | solution.py:485
  91.7 5.5 %collective-permute-done.11 = bf16[64,1280]{1,0:T(8,128)(2,1)S(1)} collective-permute-done((bf16[64,1280]{1,0:T(8,128)(2,1)S(1)}, bf16[64,1280]{1,0:T(8,128)(2,1)S(1)}, u32[]{:S(2)}, u32[]{:S(2)}) %collective-permute-start.11) | collective-permute-done | bytes 163872 | tf_op jit(solution)/shard_map/ppermute | solution.py:485
  97.3 1.6 %collective-permute-start.12 = (bf16[128,1280]{1,0:T(8,128)(2,1)S(1)}, bf16[128,1280]{1,0:T(8,128)(2,1)S(1)}, u32[]{:S(2)}, u32[]{:S(2)}) collective-permute-start(bf16[128,1280]{1,0:T(8,128)(2,1)S(1)} %add_convert_fusion.2), channel_id=1, source_target_pairs={{0,3},{1,0},{2,1},{3,2},{4,7},{5,4},{6,5},{7,6},{8,11},{9,8},{10,9... | collective-permute-start | bytes 983048 | tf_op jit(solution)/shard_map/ppermute | solution.py:485
  98.9 1.1 collective-permute-done.9
  100.1 0.4 collective-permute-start.10
  100.5 13.0 %collective-permute-done.12 = bf16[128,1280]{1,0:T(8,128)(2,1)S(1)} collective-permute-done((bf16[128,1280]{1,0:T(8,128)(2,1)S(1)}, bf16[128,1280]{1,0:T(8,128)(2,1)S(1)}, u32[]{:S(2)}, u32[]{:S(2)}) %collective-permute-start.12) | collective-permute-done | bytes 327712 | tf_op jit(solution)/shard_map/ppermute | solution.py:485
  113.4 1.4 %collective-permute-done.10 = bf16[128,1280]{1,0:T(8,128)(2,1)S(1)} collective-permute-done((bf16[128,1280]{1,0:T(8,128)(2,1)S(1)}, bf16[128,1280]{1,0:T(8,128)(2,1)S(1)}, u32[]{:S(2)}, u32[]{:S(2)}) %collective-permute-start.10) | collective-permute-done | bytes 327712 | tf_op jit(solution)/shard_map/ppermute | solution.py:485
  114.8 0.1 add_convert_fusion.1
  114.9 4.7 %all-to-all-done.1.parts = bf16[16,2,256,128]{3,2,1,0:T(8,128)(2,1)S(1)} async-done(((bf16[16,2,256,128]{3,2,1,0:T(8,128)(2,1)}), bf16[16,2,256,128]{3,2,1,0:T(8,128)(2,1)S(1)}, u32[]{:S(2)}, u32[]{:S(2)}) %all-to-all-start.1) | async-done | bytes 2097184 | tf_op jit(solution)/shard_map/all_to_all | solution.py:570
  119.6 0.3 sum_parts.1
  119.9 1.6 %collective-permute-start.13 = (bf16[256,128]{1,0:T(8,128)(2,1)S(1)}, bf16[256,128]{1,0:T(8,128)(2,1)S(1)}, u32[]{:S(2)}, u32[]{:S(2)}) collective-permute-start(bf16[256,128]{1,0:T(8,128)(2,1)S(1)} %get-tuple-element.64), channel_id=1, source_target_pairs={{0,64},{64,0},{1,65},{65,1},{2,66},{66,2},{3,67},{67,3},{4,68},{68... | collective-permute-start | bytes 196616 | tf_op jit(solution)/shard_map/ppermute | solution.py:580
  121.4 0.7 slice_bitcast_fusion
  122.2 2.3 %collective-permute-done.13.other = bf16[256,128]{1,0:T(8,128)(2,1)S(1)} collective-permute-done((bf16[256,128]{1,0:T(8,128)(2,1)S(1)}, bf16[256,128]{1,0:T(8,128)(2,1)S(1)}, u32[]{:S(2)}, u32[]{:S(2)}) %collective-permute-start.13) | collective-permute-done | bytes 65568 | tf_op jit(solution)/shard_map/ppermute | solution.py:580
  124.5 0.6 last_sum.1
  (22 shorter events, 0.1 us)
Async XLA Ops:
  2.1 4.6 %collective-permute-start = (bf16[272,128]{1,0:T(8,128)(2,1)}, bf16[272,128]{1,0:T(8,128)(2,1)S(1)}, u32[]{:S(2)}, u32[]{:S(2)}) collective-permute-start(bf16[272,128]{1,0:T(8,128)(2,1)} %pack_keys.1.own), channel_id=1, source_target_pairs={{0,64},{64,0},{1,65},{65,1},{2,66},{66,2},{3,67},{67,3},{4,68},{68... | collective-permute-start | bytes 208904 | tf_op jit(solution)/shard_map/ppermute | solution.py:511
  6.7 0.9 copy-start.11
  9.3 7.2 %copy-start.9 = (bf16[1,64,1280]{2,1,0:T(8,128)(2,1)S(1)}, bf16[1,64,1280]{2,1,0:T(8,128)(2,1)}, u32[]{:S(2)}) copy-start(bf16[1,64,1280]{2,1,0:T(8,128)(2,1)} %param.23) | copy-start | bytes 491524
  9.3 12.7 %copy-start.7 = (bf16[64,1280]{1,0:T(8,128)(2,1)S(1)}, bf16[64,1280]{1,0:T(8,128)(2,1)}, u32[]{:S(2)}) copy-start(bf16[64,1280]{1,0:T(8,128)(2,1)} %refs_0_.1) | copy-start | bytes 491524
  9.3 39.2 %all-to-all-start = ((bf16[16,2,272,128]{3,2,1,0:T(8,128)(2,1)}), bf16[16,2,272,128]{3,2,1,0:T(8,128)(2,1)S(1)}, u32[]{:S(2)}, u32[]{:S(2)}) async-start(bf16[16,2,272,128]{3,2,1,0:T(8,128)(2,1)} %copy_packs.1), calls=%async_computation | async-start | bytes 4456448 | tf_op jit(solution)/shard_map/all_to_all | solution.py:518
  16.5 35.1 %copy-start.18 = (s32[64]{0:T(128)S(1)}, s32[64]{0:T(128)}, u32[]{:S(2)}) copy-start(s32[64]{0:T(128)} %doc_ids.1) | copy-start | bytes 772
  16.5 35.1 %copy-start.19 = (s32[2]{0:T(128)S(1)}, s32[2]{0:T(128)}, u32[]{:S(2)}) copy-start(s32[2]{0:T(128)} %resp_len.3) | copy-start | bytes 28
  16.5 13.9 %collective-permute-start.2 = (bf16[64,1280]{1,0:T(8,128)(2,1)S(1)}, bf16[64,1280]{1,0:T(8,128)(2,1)S(1)}, u32[]{:S(2)}, u32[]{:S(2)}) collective-permute-start(bf16[64,1280]{1,0:T(8,128)(2,1)S(1)} %bitcast.10), channel_id=1, source_target_pairs={{0,3},{1,0},{2,1},{3,2},{4,7},{5,4},{6,5},{7,6},{8,11},{9,8},{10,9... | collective-permute-start | bytes 491528 | tf_op jit(solution)/shard_map/ppermute | solution.py:485
  22.0 16.3 %collective-permute-start.3 = (bf16[64,1280]{1,0:T(8,128)(2,1)S(1)}, bf16[64,1280]{1,0:T(8,128)(2,1)S(1)}, u32[]{:S(2)}, u32[]{:S(2)}) collective-permute-start(bf16[64,1280]{1,0:T(8,128)(2,1)S(1)} %copy-done.7), channel_id=1, source_target_pairs={{0,1},{1,2},{2,3},{3,0},{4,5},{5,6},{6,7},{7,4},{8,9},{9,10},{10,1... | collective-permute-start | bytes 491528 | tf_op jit(solution)/shard_map/ppermute | solution.py:485
  22.0 19.9 %collective-permute-start.6 = (bf16[64,1280]{1,0:T(8,128)(2,1)S(1)}, bf16[64,1280]{1,0:T(8,128)(2,1)S(1)}, u32[]{:S(2)}, u32[]{:S(2)}) collective-permute-start(bf16[64,1280]{1,0:T(8,128)(2,1)S(1)} %bitcast.11), channel_id=1, source_target_pairs={{0,1},{1,2},{2,3},{3,0},{4,5},{5,6},{6,7},{7,4},{8,9},{9,10},{10,1... | collective-permute-start | bytes 491528 | tf_op jit(solution)/shard_map/ppermute | solution.py:485
  24.0 17.9 %collective-permute-start.1 = (bf16[64,1280]{1,0:T(8,128)(2,1)S(1)}, bf16[64,1280]{1,0:T(8,128)(2,1)S(1)}, u32[]{:S(2)}, u32[]{:S(2)}) collective-permute-start(bf16[64,1280]{1,0:T(8,128)(2,1)S(1)} %copy-done.7), channel_id=1, source_target_pairs={{0,3},{1,0},{2,1},{3,2},{4,7},{5,4},{6,5},{7,6},{8,11},{9,8},{10,9... | collective-permute-start | bytes 491528 | tf_op jit(solution)/shard_map/ppermute | solution.py:485
  30.4 11.4 %collective-permute-start.5 = (bf16[64,1280]{1,0:T(8,128)(2,1)S(1)}, bf16[64,1280]{1,0:T(8,128)(2,1)S(1)}, u32[]{:S(2)}, u32[]{:S(2)}) collective-permute-start(bf16[64,1280]{1,0:T(8,128)(2,1)S(1)} %collective-permute-done.2.refs_3_), channel_id=1, source_target_pairs={{0,3},{1,0},{2,1},{3,2},{4,7},{5,4},{6,5},{7,6},{8,11},{9,8},{10,9... | collective-permute-start | bytes 491528 | tf_op jit(solution)/shard_map/ppermute | solution.py:485
  38.4 8.1 %collective-permute-start.4 = (bf16[64,1280]{1,0:T(8,128)(2,1)S(1)}, bf16[64,1280]{1,0:T(8,128)(2,1)S(1)}, u32[]{:S(2)}, u32[]{:S(2)}) collective-permute-start(bf16[64,1280]{1,0:T(8,128)(2,1)S(1)} %collective-permute-done.3.refs_6_), channel_id=1, source_target_pairs={{0,1},{1,2},{2,3},{3,0},{4,5},{5,6},{6,7},{7,4},{8,9},{9,10},{10,1... | collective-permute-start | bytes 491528 | tf_op jit(solution)/shard_map/ppermute | solution.py:485
  46.4 0.9 copy-start.8
  47.3 0.9 copy-start.10
  48.6 3.1 %copy-start.16 = (bf16[64,1024]{1,0:T(8,128)(2,1)S(1)}, bf16[64,1024]{1,0:T(8,128)(2,1)}, u32[]{:S(2)}) copy-start(bf16[64,1024]{1,0:T(8,128)(2,1)} %qp_in.5) | copy-start | bytes 393220
  48.6 3.0 %copy-start.17 = (bf16[1,64,1024]{2,1,0:T(8,128)(2,1)S(1)}, bf16[1,64,1024]{2,1,0:T(8,128)(2,1)}, u32[]{:S(2)}) copy-start(bf16[1,64,1024]{2,1,0:T(8,128)(2,1)} %param.17) | copy-start | bytes 393220
  48.7 2.9 %collective-permute-start.7 = (bf16[16,2,144,128]{3,2,1,0:T(8,128)(2,1)S(1)}, bf16[16,2,144,128]{3,2,1,0:T(8,128)(2,1)S(1)}, u32[]{:S(2)}, u32[]{:S(2)}) collective-permute-start(bf16[16,2,144,128]{3,2,1,0:T(8,128)(2,1)S(1)} %slice.39), channel_id=1, source_target_pairs={{0,128},{128,0},{1,129},{129,1},{2,130},{130,2},{3,131},{131,3},{4... | collective-permute-start | bytes 3538952 | tf_op jit(solution)/shard_map/ppermute | solution.py:526
  65.5 4.0 %copy-start.1 = (bf16[128,1280]{1,0:T(8,128)(2,1)}, bf16[128,1280]{1,0:T(8,128)(2,1)S(1)}, u32[]{:S(2)}) copy-start(bf16[128,1280]{1,0:T(8,128)(2,1)S(1)} %get-tuple-element.47) | copy-start | bytes 983044
  65.6 4.0 %copy-start.3 = (bf16[128,1280]{1,0:T(8,128)(2,1)}, bf16[128,1280]{1,0:T(8,128)(2,1)S(1)}, u32[]{:S(2)}) copy-start(bf16[128,1280]{1,0:T(8,128)(2,1)S(1)} %get-tuple-element.48) | copy-start | bytes 983044
  65.6 4.0 %copy-start.5 = (bf16[128,1280]{1,0:T(8,128)(2,1)}, bf16[128,1280]{1,0:T(8,128)(2,1)S(1)}, u32[]{:S(2)}) copy-start(bf16[128,1280]{1,0:T(8,128)(2,1)S(1)} %get-tuple-element.59) | copy-start | bytes 983044
  65.6 4.0 %copy-start.12 = (bf16[64,1280]{1,0:T(8,128)(2,1)}, bf16[64,1280]{1,0:T(8,128)(2,1)S(1)}, u32[]{:S(2)}) copy-start(bf16[64,1280]{1,0:T(8,128)(2,1)S(1)} %get-tuple-element.58) | copy-start | bytes 491524
  65.6 4.0 %copy-start.14 = (bf16[64,1280]{1,0:T(8,128)(2,1)}, bf16[64,1280]{1,0:T(8,128)(2,1)S(1)}, u32[]{:S(2)}) copy-start(bf16[64,1280]{1,0:T(8,128)(2,1)S(1)} %get-tuple-element.60) | copy-start | bytes 491524
  69.6 10.3 %collective-permute-start.8 = (bf16[16,2,128,128]{3,2,1,0:T(8,128)(2,1)S(1)}, bf16[16,2,128,128]{3,2,1,0:T(8,128)(2,1)S(1)}, u32[]{:S(2)}, u32[]{:S(2)}) collective-permute-start(bf16[16,2,128,128]{3,2,1,0:T(8,128)(2,1)S(1)} %get-tuple-element.55), channel_id=1, source_target_pairs={{0,128},{128,0},{1,129},{129,1},{2,130},{130,2},{3,131},{131,3},{4... | collective-permute-start | bytes 3145736 | tf_op jit(solution)/shard_map/ppermute | solution.py:560
  80.4 1.4 %copy-start = (bf16[16,2,256,128]{3,2,1,0:T(8,128)(2,1)}, bf16[16,2,256,128]{3,2,1,0:T(8,128)(2,1)S(1)}, u32[]{:S(2)}) copy-start(bf16[16,2,256,128]{3,2,1,0:T(8,128)(2,1)S(1)} %fusion) | copy-start | bytes 6291460
  81.8 7.0 %copy-start.15 = (bf16[64,1280]{1,0:T(8,128)(2,1)S(1)}, bf16[64,1280]{1,0:T(8,128)(2,1)}, u32[]{:S(2)}) copy-start(bf16[64,1280]{1,0:T(8,128)(2,1)} %copy-done.14) | copy-start | bytes 491524
  81.8 8.4 %copy-start.13 = (bf16[64,1280]{1,0:T(8,128)(2,1)S(1)}, bf16[64,1280]{1,0:T(8,128)(2,1)}, u32[]{:S(2)}) copy-start(bf16[64,1280]{1,0:T(8,128)(2,1)} %copy-done.12) | copy-start | bytes 491524
  81.8 15.5 %copy-start.6 = (bf16[128,1280]{1,0:T(8,128)(2,1)S(1)}, bf16[128,1280]{1,0:T(8,128)(2,1)}, u32[]{:S(2)}) copy-start(bf16[128,1280]{1,0:T(8,128)(2,1)} %copy-done.5) | copy-start | bytes 983044
  81.8 18.3 %copy-start.4 = (bf16[128,1280]{1,0:T(8,128)(2,1)S(1)}, bf16[128,1280]{1,0:T(8,128)(2,1)}, u32[]{:S(2)}) copy-start(bf16[128,1280]{1,0:T(8,128)(2,1)} %copy-done.3) | copy-start | bytes 983044
  81.8 33.0 %copy-start.2 = (bf16[128,1280]{1,0:T(8,128)(2,1)S(1)}, bf16[128,1280]{1,0:T(8,128)(2,1)}, u32[]{:S(2)}) copy-start(bf16[128,1280]{1,0:T(8,128)(2,1)} %copy-done.1) | copy-start | bytes 983044
  81.8 37.8 %all-to-all-start.1 = ((bf16[16,2,256,128]{3,2,1,0:T(8,128)(2,1)}), bf16[16,2,256,128]{3,2,1,0:T(8,128)(2,1)S(1)}, u32[]{:S(2)}, u32[]{:S(2)}) async-start(bf16[16,2,256,128]{3,2,1,0:T(8,128)(2,1)} %copy-done), calls=%async_computation.1 | async-start | bytes 4194304 | tf_op jit(solution)/shard_map/all_to_all | solution.py:570
  88.7 8.5 %collective-permute-start.11 = (bf16[64,1280]{1,0:T(8,128)(2,1)S(1)}, bf16[64,1280]{1,0:T(8,128)(2,1)S(1)}, u32[]{:S(2)}, u32[]{:S(2)}) collective-permute-start(bf16[64,1280]{1,0:T(8,128)(2,1)S(1)} %copy-done.15), channel_id=1, source_target_pairs={{0,3},{1,0},{2,1},{3,2},{4,7},{5,4},{6,5},{7,6},{8,11},{9,8},{10,9... | collective-permute-start | bytes 491528 | tf_op jit(solution)/shard_map/ppermute | solution.py:485
  90.1 9.9 %collective-permute-start.9 = (bf16[64,1280]{1,0:T(8,128)(2,1)S(1)}, bf16[64,1280]{1,0:T(8,128)(2,1)S(1)}, u32[]{:S(2)}, u32[]{:S(2)}) collective-permute-start(bf16[64,1280]{1,0:T(8,128)(2,1)S(1)} %copy-done.13), channel_id=1, source_target_pairs={{0,1},{1,2},{2,3},{3,0},{4,5},{5,6},{6,7},{7,4},{8,9},{9,10},{10,1... | collective-permute-start | bytes 491528 | tf_op jit(solution)/shard_map/ppermute | solution.py:485
  97.3 16.1 %collective-permute-start.12 = (bf16[128,1280]{1,0:T(8,128)(2,1)S(1)}, bf16[128,1280]{1,0:T(8,128)(2,1)S(1)}, u32[]{:S(2)}, u32[]{:S(2)}) collective-permute-start(bf16[128,1280]{1,0:T(8,128)(2,1)S(1)} %add_convert_fusion.2), channel_id=1, source_target_pairs={{0,3},{1,0},{2,1},{3,2},{4,7},{5,4},{6,5},{7,6},{8,11},{9,8},{10,9... | collective-permute-start | bytes 983048 | tf_op jit(solution)/shard_map/ppermute | solution.py:485
  100.1 14.7 %collective-permute-start.10 = (bf16[128,1280]{1,0:T(8,128)(2,1)S(1)}, bf16[128,1280]{1,0:T(8,128)(2,1)S(1)}, u32[]{:S(2)}, u32[]{:S(2)}) collective-permute-start(bf16[128,1280]{1,0:T(8,128)(2,1)S(1)} %add_convert_fusion.3), channel_id=1, source_target_pairs={{0,1},{1,2},{2,3},{3,0},{4,5},{5,6},{6,7},{7,4},{8,9},{9,10},{10,1... | collective-permute-start | bytes 983048 | tf_op jit(solution)/shard_map/ppermute | solution.py:485
  119.9 4.6 %collective-permute-start.13 = (bf16[256,128]{1,0:T(8,128)(2,1)S(1)}, bf16[256,128]{1,0:T(8,128)(2,1)S(1)}, u32[]{:S(2)}, u32[]{:S(2)}) collective-permute-start(bf16[256,128]{1,0:T(8,128)(2,1)S(1)} %get-tuple-element.64), channel_id=1, source_target_pairs={{0,64},{64,0},{1,65},{65,1},{2,66},{66,2},{3,67},{67,3},{4,68},{68... | collective-permute-start | bytes 196616 | tf_op jit(solution)/shard_map/ppermute | solution.py:580

commit v4 on v3

--- a/solution.py
+++ b/solution.py
@@ -120,10 +120,20 @@
 
 
 def copies_kernel(own, other, out, both, in_sems, sems):
-    for c in start_copies([(own, both.at[0]), (other, both.at[1])], in_sems):
-        c.wait()
+    (copy,) = start_copies([(own, both.at[0])], in_sems)
+    both[1] = other[...]
+    copy.wait()
     for c in start_copies([(both, out.at[n]) for n in range(PLANE)], sems):
         c.wait()
+
+
+def query_kernel(qp_in, qr_in, rows, turned, qp, qr, sems):
+    copies = start_copies([(qp_in, qp), (qr_in, qr)], sems)
+    for n, (ref, c) in enumerate(zip((qp, qr), copies)):
+        c.wait()
+        stacked = stack_heads(ref)
+        rows[n] = stacked
+        turned[n] = stacked.T
 
 
 def cotangent_kernel(*refs):
@@ -200,15 +210,15 @@
 
 
 def forward_kernel(
-    doc_ids, resp_len, own, other, qp_in, qr_in, weight, cot_in,
-    out0, out1, out2p, out2r, out3, d_out, stats, win,
-    kp, vp, kr, vr, docs, qp, qr, w_buf, cot, att, m_ref, l_ref, acc_ref,
+    doc_ids, resp_len, own, other, turned_in, weight, cot_in,
+    out0, out1, out2p, out2r, out3, d_out, d_rows, stats, win,
+    kp, vp, kr, vr, docs, turned, w_buf, cot, att, m_ref, l_ref, acc_ref,
     q_sems, sems, d_sems, r_sems, w_sem, c_sem,
 ):
     side, place = where_am_i()
     tp = lax.axis_index("tp")
     level = lax.axis_index("zl")
-    q_copies = start_copies([(qp_in, qp), (qr_in, qr)], q_sems)
+    (q_copy,) = start_copies([(turned_in, turned)], q_sems)
     pairs = []
     for ref, first in ((own, side * NBLK), (other, (1 - side) * NBLK)):
         for n, z in enumerate((level, 1 - level)):
@@ -223,10 +233,9 @@
     w_copy.start()
     c_copy = pltpu.make_async_copy(cot_in, cot, c_sem)
     c_copy.start()
-    for c in q_copies:
-        c.wait()
-    q_t = stack_heads(qp).T
-    r_t = stack_heads(qr).T
+    q_copy.wait()
+    q_t = turned[0]
+    r_t = turned[1]
     for c in d_copies:
         c.wait()
     all_docs = docs[...].astype(f32).reshape(2 * NBLK * 16, DH)
@@ -269,6 +278,7 @@
             d_out[n, :, h * ROWS : (h + 1) * ROWS] = d_all[
                 h * DH : (h + 1) * DH, n * ROWS : (n + 1) * ROWS
             ]
+        d_rows[n] = d_out[n].T
     stats[2:3, :] = row_deltas(d_out[0], out_p)
     begin()
     fwd_run(r_t, kp, vp, m_ref, l_ref, acc_ref)
@@ -315,10 +325,11 @@
         out[:, h * DH : (h + 1) * DH] = rows[h * ROWS : (h + 1) * ROWS, :]
 
 
-def query_side(q, d_att, stats, side):
-    q_rows = stack_heads(q)
-    d_t = d_att[side]
-    return (q_rows.T, q_rows, d_t, d_t.T, stats[side : side + 1, :], stats[2 + side : 3 + side, :])
+def query_side(turned, rows, d_t, d_rows, stats, side):
+    return (
+        turned[side], rows[side], d_t[side], d_rows[side],
+        stats[side : side + 1, :], stats[2 + side : 3 + side, :],
+    )
 
 
 def store_keys(out, j, row, g_key, g_value):
@@ -364,13 +375,14 @@
 
 
 def bwd_other_kernel(
-    win, other, qp_in, qr_in, d_in, stats_in,
+    win, other, turned_in, rows_in, d_in, d_rows_in, stats_in,
     g_out, gqp_ref, gqr_ref,
-    kp, vp, qp, qr, d_att, stats, gk, gv, sems,
+    kp, vp, turned, rows, d_t, d_rows, stats, gk, gv, sems,
 ):
     side, place = where_am_i()
     copies = start_copies(
-        [(qr_in, qr), (qp_in, qp), (d_in, d_att), (stats_in, stats)]
+        [(turned_in, turned), (rows_in, rows), (d_in, d_t), (d_rows_in, d_rows)]
+        + [(stats_in, stats)]
         + key_pairs(other, 0, 0, kp, vp),
         sems,
     )
@@ -380,30 +392,31 @@
         c.wait()
     half_of_prompt(
         (1 - side) * NBLK, win[0], side * NBLK + place, stats[4:5, :].astype(i32),
-        kp, vp, gk, gv, query_side(qp, d_att, stats, 0), query_side(qr, d_att, stats, 1),
-        gqp_ref, gqr_ref, g_out,
+        kp, vp, gk, gv, query_side(turned, rows, d_t, d_rows, stats, 0),
+        query_side(turned, rows, d_t, d_rows, stats, 1), gqp_ref, gqr_ref, g_out,
     )
 
 
 def bwd_own_kernel(
-    win, resp_len, own, qp_in, qr_in, d_in, stats_in, gqp_in, gqr_in,
+    win, resp_len, own, turned_in, rows_in, d_in, d_rows_in, stats_in, gqp_in, gqr_in,
     gq_p, gq_r, g_out,
-    kp, vp, kr, vr, qp, qr, d_att, stats, gk, gv, gqp_ref, gqr_ref, sems, r_sems,
+    kp, vp, kr, vr, turned, rows, d_t, d_rows, stats, gk, gv, gqp_ref, gqr_ref, sems, r_sems,
 ):
     side, place = where_am_i()
     copies = start_copies(
-        [(qr_in, qr), (qp_in, qp), (d_in, d_att), (stats_in, stats)]
-        + [(gqp_in, gqp_ref), (gqr_in, gqr_ref)]
+        [(turned_in, turned), (rows_in, rows), (d_in, d_t), (d_rows_in, d_rows)]
+        + [(stats_in, stats), (gqp_in, gqp_ref), (gqr_in, gqr_ref)]
         + key_pairs(own, 0, 0, kp, vp),
         sems,
     )
     r_copies = start_copies(key_pairs(own, 0, PACK, kr, vr), r_sems)
     for c in copies:
         c.wait()
-    resp = query_side(qr, d_att, stats, 1)
+    resp = query_side(turned, rows, d_t, d_rows, stats, 1)
     half_of_prompt(
         side * NBLK, win[0], side * NBLK + place, stats[4:5, :].astype(i32),
-        kp, vp, gk, gv, query_side(qp, d_att, stats, 0), resp, gqp_ref, gqr_ref, g_out,
+        kp, vp, gk, gv, query_side(turned, rows, d_t, d_rows, stats, 0), resp,
+        gqp_ref, gqr_ref, g_out,
     )
     store_q(gqp_ref, gq_p)
     for c in r_copies:
@@ -510,60 +523,65 @@
     )
     pack_z = lax.ppermute(pack, "zl", SWAP)
     (packs,) = call(
-        copies_kernel, "copy_packs", [ANY] * 2, (shape(PLANE, 2, PACK + 2 * ROWS, DH),),
-        [pltpu.VMEM((2, PACK + 2 * ROWS, DH), bf16), sems(2), sems(PLANE)],
+        copies_kernel, "copy_packs", [ANY, VM], (shape(PLANE, 2, PACK + 2 * ROWS, DH),),
+        [pltpu.VMEM((2, PACK + 2 * ROWS, DH), bf16), sems(1), sems(PLANE)],
         (pack, pack_z), 0.1, limit=16,
         out_specs=(HB,),
     )
     own = lax.all_to_all(packs, ("y", "x"), 0, 0, tiled=True)
     far_p, far_r = shift(left_p, 1), shift(right_r, -1)
+    q_rows, q_turned = call(
+        query_kernel, "turn_queries", [HB] * 2, (shape(2, QROWS, DH), shape(2, DH, QROWS)),
+        [row_vm, row_vm, sems(2)], (q_prompt, q_resp), 0.1,
+    )
     (cot,) = call(
         cotangent_kernel, "join_cotangent", [ANY] * 8, (shape(2 * ROWS, 4 * part),), [sems(8)],
         (grad_prompt, grad_resp, right_p, right_r, far_p, far_r, left_p, left_r), 0.1,
         out_specs=(HB,), limit=16,
     )
-    own, cot = lax.optimization_barrier((own, cot))
+    own, cot, q_rows, q_turned = lax.optimization_barrier((own, cot, q_rows, q_turned))
     other = lax.ppermute(own[:, :, :PACK], "resp", SWAP)
 
-    o0, o1, o2p, o2r, o3, d_att, stats, win = call(
-        forward_kernel, "forward", [SM] * 2 + [ANY] * 2 + [HB] * 3 + [ANY],
+    o0, o1, o2p, o2r, o3, d_att, d_rows, stats, win = call(
+        forward_kernel, "forward", [SM] * 2 + [ANY] * 3 + [HB] + [ANY],
         (
             shape(2 * ROWS, part), shape(2 * ROWS, part), shape(ROWS, part), shape(ROWS, part),
-            shape(2 * ROWS, part), shape(2, DH, QROWS), shape(8, QROWS, dtype=f32),
-            shape(4, dtype=i32),
+            shape(2 * ROWS, part), shape(2, DH, QROWS), shape(2, QROWS, DH),
+            shape(8, QROWS, dtype=f32), shape(4, dtype=i32),
         ),
         key_scratch(2 * NBLK)
         + key_scratch(NBLK)
         + [
-            pltpu.VMEM((2 * NBLK, 16, DH), bf16), row_vm, row_vm, weight_vm,
+            pltpu.VMEM((2 * NBLK, 16, DH), bf16), pltpu.VMEM((2, DH, QROWS), bf16), weight_vm,
             pltpu.VMEM((2 * ROWS, 4 * part), bf16), pltpu.VMEM((2 * ROWS, cols), bf16),
         ]
         + state_scratch()
-        + [sems(2), sems(8), sems(4), sems(4)] + [pltpu.SemaphoreType.DMA(())] * 2,
+        + [sems(1), sems(8), sems(4), sems(4)] + [pltpu.SemaphoreType.DMA(())] * 2,
         (
-            doc_ids, resp_len, own, other, q_prompt, q_resp, out_weight, cot,
+            doc_ids, resp_len, own, other, q_turned, out_weight, cot,
         ), 8,
-        out_specs=(VM,) * 7 + (SM,), limit=40,
+        out_specs=(VM,) * 8 + (SM,), limit=40,
     )
     half_scratch = key_scratch(NBLK)
     side_scratch = [
-        row_vm, row_vm, pltpu.VMEM((2, DH, QROWS), bf16), stats_vm,
+        pltpu.VMEM((2, DH, QROWS), bf16), pltpu.VMEM((2, QROWS, DH), bf16),
+        pltpu.VMEM((2, DH, QROWS), bf16), pltpu.VMEM((2, QROWS, DH), bf16), stats_vm,
         pltpu.VMEM((HALF, DH), f32), pltpu.VMEM((HALF, DH), f32),
     ]
     acc = shape(DH, QROWS, dtype=f32)
     g_other, gqp_acc, gqr_acc = call(
-        bwd_other_kernel, "backward_other_half", [SM, ANY] + [HB] * 4,
+        bwd_other_kernel, "backward_other_half", [SM] + [ANY] * 6,
         (shape(PLANE, 2, 2 * ROWS, DH), acc, acc),
-        half_scratch + side_scratch + [sems(8)],
-        (win, other, q_prompt, q_resp, d_att, stats), 4, limit=30,
+        half_scratch + side_scratch + [sems(9)],
+        (win, other, q_turned, q_rows, d_att, d_rows, stats), 4, limit=30,
     )
     g_in = lax.ppermute(g_other, "resp", SWAP)
     gq_p, gq_r, g_mine = call(
-        bwd_own_kernel, "backward_own_half", [SM, SM, ANY] + [HB] * 6,
+        bwd_own_kernel, "backward_own_half", [SM, SM] + [ANY] * 8,
         (shape(ROWS, cols),) * 2 + (shape(PLANE, 2, 4 * ROWS, DH),),
         half_scratch + half_scratch + side_scratch
-        + [pltpu.VMEM((DH, QROWS), f32)] * 2 + [sems(10), sems(4)],
-        (win, resp_len, own, q_prompt, q_resp, d_att, stats, gqp_acc, gqr_acc), 7, limit=30,
+        + [pltpu.VMEM((DH, QROWS), f32)] * 2 + [sems(11), sems(4)],
+        (win, resp_len, own, q_turned, q_rows, d_att, d_rows, stats, gqp_acc, gqr_acc), 7, limit=30,
     )
     sends = g_mine.at[:, :, : 2 * ROWS].set(add(g_mine[:, :, : 2 * ROWS], g_in))
     sends, o2p, o2r = lax.optimization_barrier((sends, o2p, o2r))

time: 127 us -> 126 us (level)
  Pallas kernels: 31 us -> 34.2 us
  waiting for transfers between devices: 49 us -> 46.3 us
    ppermute x10, waiting for transfers between devices: 36.5 us -> 32.8 us  [shift(): return lax.ppermute(x, 'tp', [(n, (n + by) % 4) for n in range(4)])]
    pallas_call x8 -> x9, Pallas kernels: 31 us -> 34.2 us  [call(): pl.pallas_call(kernel, out_shape=outs, in_specs=in_specs, out_specs=out_s...]
    all_to_all x1, starting transfers between devices: 6.94 us -> 4.57 us  [body(): parts = lax.all_to_all(sends, ('y', 'x'), 0, 0, tiled=True)]
    ppermute x10, starting transfers between devices: 19.3 us -> 21.2 us  [shift(): return lax.ppermute(x, 'tp', [(n, (n + by) % 4) for n in range(4)])]
    ppermute x1, starting transfers between devices: 1.46 us -> 2.8 us  [body(): g_in = lax.ppermute(g_other, 'resp', SWAP)]
    ppermute x1, starting transfers between devices: 1.55 us -> 0.23 us  [body(): other = lax.ppermute(other, 'zl', SWAP)]
  transfers between devices with their start and end apart: 16 -> 16, of which waited for: 12 -> 11; matrix products, arithmetic and copies ran while one was open for 1% -> 1% of each run, Pallas kernels for 7% -> 10%
where the time goes in v4:
time: 126 us; the launch traced here: 125 us
  waiting for transfers between devices  46.3 us (37%)
  starting transfers between devices  38 us (30%)
  Pallas kernels  34.2 us (27%)
  local copies, waits for them, and re-layouts  4.96 us (4%)
    pallas_call x9, Pallas kernels, call(): pl.pallas_call(kernel, out_shape=outs, in_specs=in_specs, out_specs=out_s...  34.2 us
    ppermute x10, waiting for transfers between devices, shift(): return lax.ppermute(x, 'tp', [(n, (n + by) % 4) for n in range(4)])  32.8 us
    ppermute x10, starting transfers between devices, shift(): return lax.ppermute(x, 'tp', [(n, (n + by) % 4) for n in range(4)])  21.2 us
    all_to_all x1, starting transfers between devices, body(): own = lax.all_to_all(packs, ('y', 'x'), 0, 0, tiled=True)  7.18 us
    all_to_all x1, waiting for transfers between devices, body(): parts = lax.all_to_all(sends, ('y', 'x'), 0, 0, tiled=True)  4.58 us
    all_to_all x1, starting transfers between devices, body(): parts = lax.all_to_all(sends, ('y', 'x'), 0, 0, tiled=True)  4.57 us
    unnamed x40, local copies, waits for them, and re-layouts  4.14 us
    ppermute x1, waiting for transfers between devices, body(): other = lax.ppermute(other, 'zl', SWAP)  3.38 us
  transfers between devices with their start and end apart: 16, of which 11 were waited for; matrix products, arithmetic and copies ran while one was open for 1% of the time, Pallas kernels for 10%

profile of v4, /device:TPU:32, one launch (start us, length us, event | category | flops | bytes accessed | tf_op | source)
XLA Modules:
  0.0 125.1 jit_solution(7255810540875359230)
XLA Ops:
  0.6 1.5 %pack_keys.1.own = bf16[272,128]{1,0:T(8,128)(2,1)} custom-call(bf16[64,128]{1,0:T(8,128)(2,1)} %kp.1, bf16[64,128]{1,0:T(8,128)(2,1)} %vp.1, s32[1,64]{1,0:T(1,128)} %bitcast.13, bf16[64,128]{1,0:T(8,128)(2,1)} %bitcast.15, bf16[64,128]{1,0:T(8,128)(2,1)} %bitcast.16), custom_call_target="tpu_custom_call" | custom-call | flops 100000000 | bytes 4000000 | tf_op jit(solution)/shard_map/pack_keys/pallas_call | solution.py:468
  2.1 1.9 %collective-permute-start = (bf16[272,128]{1,0:T(8,128)(2,1)}, bf16[272,128]{1,0:T(8,128)(2,1)S(1)}, u32[]{:S(2)}, u32[]{:S(2)}) collective-permute-start(bf16[272,128]{1,0:T(8,128)(2,1)} %pack_keys.1.own), channel_id=1, source_target_pairs={{0,64},{64,0},{1,65},{65,1},{2,66},{66,2},{3,67},{67,3},{4,68},{68... | collective-permute-start | bytes 208904 | tf_op jit(solution)/shard_map/ppermute | solution.py:524
  4.0 2.7 %collective-permute-done.other = bf16[272,128]{1,0:T(8,128)(2,1)S(1)} collective-permute-done((bf16[272,128]{1,0:T(8,128)(2,1)}, bf16[272,128]{1,0:T(8,128)(2,1)S(1)}, u32[]{:S(2)}, u32[]{:S(2)}) %collective-permute-start) | collective-permute-done | bytes 69664 | tf_op jit(solution)/shard_map/ppermute | solution.py:524
  6.7 0.9 copy-done.11
  7.6 1.6 %copy_packs.1 = bf16[16,2,272,128]{3,2,1,0:T(8,128)(2,1)} custom-call(bf16[272,128]{1,0:T(8,128)(2,1)S(1)} %copy-done.11, bf16[272,128]{1,0:T(8,128)(2,1)S(1)} %collective-permute-done.other), custom_call_target="tpu_custom_call" | custom-call | flops 100000000 | bytes 4000000 | tf_op jit(solution)/shard_map/copy_packs/pallas_call | solution.py:468
  9.2 0.0 copy-start.9
  9.2 0.0 copy-start.7
  9.2 7.2 %all-to-all-start = ((bf16[16,2,272,128]{3,2,1,0:T(8,128)(2,1)}), bf16[16,2,272,128]{3,2,1,0:T(8,128)(2,1)S(1)}, u32[]{:S(2)}, u32[]{:S(2)}) async-start(bf16[16,2,272,128]{3,2,1,0:T(8,128)(2,1)} %copy_packs.1), calls=%async_computation | async-start | bytes 4456448 | tf_op jit(solution)/shard_map/all_to_all | solution.py:531
  16.4 0.0 copy-done.9
  16.4 5.5 %collective-permute-start.2 = (bf16[64,1280]{1,0:T(8,128)(2,1)S(1)}, bf16[64,1280]{1,0:T(8,128)(2,1)S(1)}, u32[]{:S(2)}, u32[]{:S(2)}) collective-permute-start(bf16[64,1280]{1,0:T(8,128)(2,1)S(1)} %bitcast.10), channel_id=1, source_target_pairs={{0,3},{1,0},{2,1},{3,2},{4,7},{5,4},{6,5},{7,6},{8,11},{9,8},{10,9... | collective-permute-start | bytes 491528 | tf_op jit(solution)/shard_map/ppermute | solution.py:498
  21.9 0.0 copy-done.7
  21.9 0.0 collective-permute-start.3
  21.9 2.0 %collective-permute-start.6 = (bf16[64,1280]{1,0:T(8,128)(2,1)S(1)}, bf16[64,1280]{1,0:T(8,128)(2,1)S(1)}, u32[]{:S(2)}, u32[]{:S(2)}) collective-permute-start(bf16[64,1280]{1,0:T(8,128)(2,1)S(1)} %bitcast.11), channel_id=1, source_target_pairs={{0,1},{1,2},{2,3},{3,0},{4,5},{5,6},{6,7},{7,4},{8,9},{9,10},{10,1... | collective-permute-start | bytes 491528 | tf_op jit(solution)/shard_map/ppermute | solution.py:498
  23.9 2.2 %collective-permute-start.1 = (bf16[64,1280]{1,0:T(8,128)(2,1)S(1)}, bf16[64,1280]{1,0:T(8,128)(2,1)S(1)}, u32[]{:S(2)}, u32[]{:S(2)}) collective-permute-start(bf16[64,1280]{1,0:T(8,128)(2,1)S(1)} %copy-done.7), channel_id=1, source_target_pairs={{0,3},{1,0},{2,1},{3,2},{4,7},{5,4},{6,5},{7,6},{8,11},{9,8},{10,9... | collective-permute-start | bytes 491528 | tf_op jit(solution)/shard_map/ppermute | solution.py:498
  26.1 4.3 %collective-permute-done.2.refs_3_ = bf16[64,1280]{1,0:T(8,128)(2,1)S(1)} collective-permute-done((bf16[64,1280]{1,0:T(8,128)(2,1)S(1)}, bf16[64,1280]{1,0:T(8,128)(2,1)S(1)}, u32[]{:S(2)}, u32[]{:S(2)}) %collective-permute-start.2) | collective-permute-done | bytes 163872 | tf_op jit(solution)/shard_map/ppermute | solution.py:498
  30.3 4.7 %collective-permute-start.5 = (bf16[64,1280]{1,0:T(8,128)(2,1)S(1)}, bf16[64,1280]{1,0:T(8,128)(2,1)S(1)}, u32[]{:S(2)}, u32[]{:S(2)}) collective-permute-start(bf16[64,1280]{1,0:T(8,128)(2,1)S(1)} %collective-permute-done.2.refs_3_), channel_id=1, source_target_pairs={{0,3},{1,0},{2,1},{3,2},{4,7},{5,4},{6,5},{7,6},{8,11},{9,8},{10,9... | collective-permute-start | bytes 491528 | tf_op jit(solution)/shard_map/ppermute | solution.py:498
  35.0 3.2 %collective-permute-done.3.refs_6_ = bf16[64,1280]{1,0:T(8,128)(2,1)S(1)} collective-permute-done((bf16[64,1280]{1,0:T(8,128)(2,1)S(1)}, bf16[64,1280]{1,0:T(8,128)(2,1)S(1)}, u32[]{:S(2)}, u32[]{:S(2)}) %collective-permute-start.3) | collective-permute-done | bytes 163872 | tf_op jit(solution)/shard_map/ppermute | solution.py:498
  38.2 0.0 collective-permute-start.4
  38.2 1.9 %turn_queries.1 = (bf16[2,512,128]{2,1,0:T(8,128)(2,1)}, bf16[2,128,512]{2,1,0:T(8,128)(2,1)}) custom-call(bf16[64,1024]{1,0:T(8,128)(2,1)} %qp_in.1, bf16[64,1024]{1,0:T(8,128)(2,1)} %bitcast.14), custom_call_target="tpu_custom_call" | custom-call | flops 100000000 | bytes 4000000 | tf_op jit(solution)/shard_map/turn_queries/pallas_call | solution.py:468
  40.1 1.6 %collective-permute-done.6.refs_7_ = bf16[64,1280]{1,0:T(8,128)(2,1)S(1)} collective-permute-done((bf16[64,1280]{1,0:T(8,128)(2,1)S(1)}, bf16[64,1280]{1,0:T(8,128)(2,1)S(1)}, u32[]{:S(2)}, u32[]{:S(2)}) %collective-permute-start.6) | collective-permute-done | bytes 163872 | tf_op jit(solution)/shard_map/ppermute | solution.py:498
  41.8 0.0 collective-permute-done.1.refs_2_
  41.8 0.0 collective-permute-done.5.refs_5_
  41.8 4.5 %collective-permute-done.4.refs_4_ = bf16[64,1280]{1,0:T(8,128)(2,1)S(1)} collective-permute-done((bf16[64,1280]{1,0:T(8,128)(2,1)S(1)}, bf16[64,1280]{1,0:T(8,128)(2,1)S(1)}, u32[]{:S(2)}, u32[]{:S(2)}) %collective-permute-start.4) | collective-permute-done | bytes 163872 | tf_op jit(solution)/shard_map/ppermute | solution.py:498
  46.3 0.9 copy-done.8
  47.2 0.9 copy-done.10
  48.1 0.3 join_cotangent.1.cot_in
  48.4 0.0 all-to-all-done.own
  48.4 0.0 copy-start.19
  48.4 0.1 slice.39
  48.5 0.0 copy-start.18
  48.5 0.1 collective-permute-start.7
  48.6 2.8 %collective-permute-done.7.other = bf16[16,2,144,128]{3,2,1,0:T(8,128)(2,1)S(1)} collective-permute-done((bf16[16,2,144,128]{3,2,1,0:T(8,128)(2,1)S(1)}, bf16[16,2,144,128]{3,2,1,0:T(8,128)(2,1)S(1)}, u32[]{:S(2)}, u32[]{:S(2)}) %collective-permute-start.7) | collective-permute-done | bytes 1179680 | tf_op jit(solution)/shard_map/ppermute | solution.py:543
  51.5 0.0 copy-done.16
  51.5 0.0 copy-done.17
  51.5 0.0 copy-done.19
  51.5 14.6 %forward.1 = (bf16[128,1280]{1,0:T(8,128)(2,1)S(1)}, bf16[128,1280]{1,0:T(8,128)(2,1)S(1)}, bf16[64,1280]{1,0:T(8,128)(2,1)S(1)}, bf16[64,1280]{1,0:T(8,128)(2,1...) custom-call(s32[64]{0:T(128)S(1)} %copy-done.16, ...), custom_call_target="tpu_custom_call" | custom-call | flops 8000000000 | bytes 4000000 | tf_op jit(solution)/shard_map/forward/pallas_call | solution.py:468
  66.1 0.0 copy-start.1
  66.1 0.0 copy-start.3
  66.1 0.0 copy-start.12
  66.2 0.0 copy-start.14
  66.2 0.0 copy-done.18
  66.2 3.7 %backward_other_half.1 = (bf16[16,2,128,128]{3,2,1,0:T(8,128)(2,1)S(1)}, f32[128,512]{1,0:T(8,128)S(1)}, f32[128,512]{1,0:T(8,128)S(1)}) custom-call(s32[4]{0:T(128)S(1)} %get-tuple-element.57.win, bf16[16,2,144,128]{3,2,1,0:T(8,128)(2,1)S(1)} %collective-permute-done.7.other, bf16[2,128,512]{2,1,0:T(8,128)(2,1)S(1)} %copy-done.19, ...), custom_call_target="tpu_custom_call" | custom-call | flops 4000000000 | bytes 4000000 | tf_op jit(solution)/shard_map/backward_other_half/pallas_call | solution.py:468
  69.9 2.8 %collective-permute-start.8 = (bf16[16,2,128,128]{3,2,1,0:T(8,128)(2,1)S(1)}, bf16[16,2,128,128]{3,2,1,0:T(8,128)(2,1)S(1)}, u32[]{:S(2)}, u32[]{:S(2)}) collective-permute-start(bf16[16,2,128,128]{3,2,1,0:T(8,128)(2,1)S(1)} %get-tuple-element.65), channel_id=1, source_target_pairs={{0,128},{128,0},{1,129},{129,1},{2,130},{130,2},{3,131},{131,3},{4... | collective-permute-start | bytes 3145736 | tf_op jit(solution)/shard_map/ppermute | solution.py:578
  72.7 9.8 %backward_own_half.1 = (bf16[64,1024]{1,0:T(8,128)(2,1)}, bf16[64,1024]{1,0:T(8,128)(2,1)}, bf16[16,2,256,128]{3,2,1,0:T(8,128)(2,1)S(1)}) custom-call(s32[4]{0:T(128)S(1)} %get-tuple-element.57.win, s32[2]{0:T(128)S(1)} %copy-done.17, bf16[16,2,272,128]{3,2,1,0:T(8,128)(2,1)S(1)} %all-to-all-done.own, bf16[2,128,512]{2,1,0:T(8,128)(2,1)S(1)} %copy-done.19, ...), custom_call_target="tpu_custom_call" | custom-call | flops 7000000000 | bytes 4000000 | tf_op jit(solution)/shard_map/backward_own_half/pallas_call | solution.py:468
  82.5 0.0 collective-permute-done.8
  82.5 0.5 fusion
  83.0 1.4 %copy-done = bf16[16,2,256,128]{3,2,1,0:T(8,128)(2,1)} copy-done((bf16[16,2,256,128]{3,2,1,0:T(8,128)(2,1)}, bf16[16,2,256,128]{3,2,1,0:T(8,128)(2,1)S(1)}, u32[]{:S(2)}) %copy-start) | copy-done | bytes 2097176
  84.4 0.0 copy-start.2
  84.4 4.6 %all-to-all-start.1 = ((bf16[16,2,256,128]{3,2,1,0:T(8,128)(2,1)}), bf16[16,2,256,128]{3,2,1,0:T(8,128)(2,1)S(1)}, u32[]{:S(2)}, u32[]{:S(2)}) async-start(bf16[16,2,256,128]{3,2,1,0:T(8,128)(2,1)} %copy-done), calls=%async_computation.1 | async-start | bytes 4194304 | tf_op jit(solution)/shard_map/all_to_all | solution.py:588
  89.0 3.8 %collective-permute-start.11 = (bf16[64,1280]{1,0:T(8,128)(2,1)S(1)}, bf16[64,1280]{1,0:T(8,128)(2,1)S(1)}, u32[]{:S(2)}, u32[]{:S(2)}) collective-permute-start(bf16[64,1280]{1,0:T(8,128)(2,1)S(1)} %copy-done.15), channel_id=1, source_target_pairs={{0,3},{1,0},{2,1},{3,2},{4,7},{5,4},{6,5},{7,6},{8,11},{9,8},{10,9... | collective-permute-start | bytes 491528 | tf_op jit(solution)/shard_map/ppermute | solution.py:498
  92.8 0.0 collective-permute-start.9
  92.8 6.1 %collective-permute-done.11 = bf16[64,1280]{1,0:T(8,128)(2,1)S(1)} collective-permute-done((bf16[64,1280]{1,0:T(8,128)(2,1)S(1)}, bf16[64,1280]{1,0:T(8,128)(2,1)S(1)}, u32[]{:S(2)}, u32[]{:S(2)}) %collective-permute-start.11) | collective-permute-done | bytes 163872 | tf_op jit(solution)/shard_map/ppermute | solution.py:498
  99.0 2.3 %collective-permute-start.12 = (bf16[128,1280]{1,0:T(8,128)(2,1)S(1)}, bf16[128,1280]{1,0:T(8,128)(2,1)S(1)}, u32[]{:S(2)}, u32[]{:S(2)}) collective-permute-start(bf16[128,1280]{1,0:T(8,128)(2,1)S(1)} %add_convert_fusion.2), channel_id=1, source_target_pairs={{0,3},{1,0},{2,1},{3,2},{4,7},{5,4},{6,5},{7,6},{8,11},{9,8},{10,9... | collective-permute-start | bytes 983048 | tf_op jit(solution)/shard_map/ppermute | solution.py:498
  101.3 0.0 collective-permute-done.9
  101.3 0.8 collective-permute-start.10
  102.1 11.7 %collective-permute-done.12 = bf16[128,1280]{1,0:T(8,128)(2,1)S(1)} collective-permute-done((bf16[128,1280]{1,0:T(8,128)(2,1)S(1)}, bf16[128,1280]{1,0:T(8,128)(2,1)S(1)}, u32[]{:S(2)}, u32[]{:S(2)}) %collective-permute-start.12) | collective-permute-done | bytes 327712 | tf_op jit(solution)/shard_map/ppermute | solution.py:498
  113.7 1.4 %collective-permute-done.10 = bf16[128,1280]{1,0:T(8,128)(2,1)S(1)} collective-permute-done((bf16[128,1280]{1,0:T(8,128)(2,1)S(1)}, bf16[128,1280]{1,0:T(8,128)(2,1)S(1)}, u32[]{:S(2)}, u32[]{:S(2)}) %collective-permute-start.10) | collective-permute-done | bytes 327712 | tf_op jit(solution)/shard_map/ppermute | solution.py:498
  115.1 0.1 add_convert_fusion.1
  115.2 4.6 %all-to-all-done.1.parts = bf16[16,2,256,128]{3,2,1,0:T(8,128)(2,1)S(1)} async-done(((bf16[16,2,256,128]{3,2,1,0:T(8,128)(2,1)}), bf16[16,2,256,128]{3,2,1,0:T(8,128)(2,1)S(1)}, u32[]{:S(2)}, u32[]{:S(2)}) %all-to-all-start.1) | async-done | bytes 2097184 | tf_op jit(solution)/shard_map/all_to_all | solution.py:588
  119.8 0.3 sum_parts.1
  120.1 0.2 collective-permute-start.13
  120.3 0.7 slice_bitcast_fusion
  121.1 3.4 %collective-permute-done.13.other = bf16[256,128]{1,0:T(8,128)(2,1)S(1)} collective-permute-done((bf16[256,128]{1,0:T(8,128)(2,1)S(1)}, bf16[256,128]{1,0:T(8,128)(2,1)S(1)}, u32[]{:S(2)}, u32[]{:S(2)}) %collective-permute-start.13) | collective-permute-done | bytes 65568 | tf_op jit(solution)/shard_map/ppermute | solution.py:598
  124.4 0.6 last_sum.1
  (23 shorter events, 0.1 us)
Async XLA Ops:
  2.1 4.6 %collective-permute-start = (bf16[272,128]{1,0:T(8,128)(2,1)}, bf16[272,128]{1,0:T(8,128)(2,1)S(1)}, u32[]{:S(2)}, u32[]{:S(2)}) collective-permute-start(bf16[272,128]{1,0:T(8,128)(2,1)} %pack_keys.1.own), channel_id=1, source_target_pairs={{0,64},{64,0},{1,65},{65,1},{2,66},{66,2},{3,67},{67,3},{4,68},{68... | collective-permute-start | bytes 208904 | tf_op jit(solution)/shard_map/ppermute | solution.py:524
  6.7 0.9 copy-start.11
  9.2 7.2 %copy-start.9 = (bf16[1,64,1280]{2,1,0:T(8,128)(2,1)S(1)}, bf16[1,64,1280]{2,1,0:T(8,128)(2,1)}, u32[]{:S(2)}) copy-start(bf16[1,64,1280]{2,1,0:T(8,128)(2,1)} %param.23) | copy-start | bytes 491524
  9.2 12.7 %copy-start.7 = (bf16[64,1280]{1,0:T(8,128)(2,1)S(1)}, bf16[64,1280]{1,0:T(8,128)(2,1)}, u32[]{:S(2)}) copy-start(bf16[64,1280]{1,0:T(8,128)(2,1)} %refs_0_.1) | copy-start | bytes 491524
  9.2 39.2 %all-to-all-start = ((bf16[16,2,272,128]{3,2,1,0:T(8,128)(2,1)}), bf16[16,2,272,128]{3,2,1,0:T(8,128)(2,1)S(1)}, u32[]{:S(2)}, u32[]{:S(2)}) async-start(bf16[16,2,272,128]{3,2,1,0:T(8,128)(2,1)} %copy_packs.1), calls=%async_computation | async-start | bytes 4456448 | tf_op jit(solution)/shard_map/all_to_all | solution.py:531
  16.4 13.9 %collective-permute-start.2 = (bf16[64,1280]{1,0:T(8,128)(2,1)S(1)}, bf16[64,1280]{1,0:T(8,128)(2,1)S(1)}, u32[]{:S(2)}, u32[]{:S(2)}) collective-permute-start(bf16[64,1280]{1,0:T(8,128)(2,1)S(1)} %bitcast.10), channel_id=1, source_target_pairs={{0,3},{1,0},{2,1},{3,2},{4,7},{5,4},{6,5},{7,6},{8,11},{9,8},{10,9... | collective-permute-start | bytes 491528 | tf_op jit(solution)/shard_map/ppermute | solution.py:498
  21.9 16.3 %collective-permute-start.3 = (bf16[64,1280]{1,0:T(8,128)(2,1)S(1)}, bf16[64,1280]{1,0:T(8,128)(2,1)S(1)}, u32[]{:S(2)}, u32[]{:S(2)}) collective-permute-start(bf16[64,1280]{1,0:T(8,128)(2,1)S(1)} %copy-done.7), channel_id=1, source_target_pairs={{0,1},{1,2},{2,3},{3,0},{4,5},{5,6},{6,7},{7,4},{8,9},{9,10},{10,1... | collective-permute-start | bytes 491528 | tf_op jit(solution)/shard_map/ppermute | solution.py:498
  21.9 19.9 %collective-permute-start.6 = (bf16[64,1280]{1,0:T(8,128)(2,1)S(1)}, bf16[64,1280]{1,0:T(8,128)(2,1)S(1)}, u32[]{:S(2)}, u32[]{:S(2)}) collective-permute-start(bf16[64,1280]{1,0:T(8,128)(2,1)S(1)} %bitcast.11), channel_id=1, source_target_pairs={{0,1},{1,2},{2,3},{3,0},{4,5},{5,6},{6,7},{7,4},{8,9},{9,10},{10,1... | collective-permute-start | bytes 491528 | tf_op jit(solution)/shard_map/ppermute | solution.py:498
  23.9 17.9 %collective-permute-start.1 = (bf16[64,1280]{1,0:T(8,128)(2,1)S(1)}, bf16[64,1280]{1,0:T(8,128)(2,1)S(1)}, u32[]{:S(2)}, u32[]{:S(2)}) collective-permute-start(bf16[64,1280]{1,0:T(8,128)(2,1)S(1)} %copy-done.7), channel_id=1, source_target_pairs={{0,3},{1,0},{2,1},{3,2},{4,7},{5,4},{6,5},{7,6},{8,11},{9,8},{10,9... | collective-permute-start | bytes 491528 | tf_op jit(solution)/shard_map/ppermute | solution.py:498
  30.3 11.4 %collective-permute-start.5 = (bf16[64,1280]{1,0:T(8,128)(2,1)S(1)}, bf16[64,1280]{1,0:T(8,128)(2,1)S(1)}, u32[]{:S(2)}, u32[]{:S(2)}) collective-permute-start(bf16[64,1280]{1,0:T(8,128)(2,1)S(1)} %collective-permute-done.2.refs_3_), channel_id=1, source_target_pairs={{0,3},{1,0},{2,1},{3,2},{4,7},{5,4},{6,5},{7,6},{8,11},{9,8},{10,9... | collective-permute-start | bytes 491528 | tf_op jit(solution)/shard_map/ppermute | solution.py:498
  38.2 8.1 %collective-permute-start.4 = (bf16[64,1280]{1,0:T(8,128)(2,1)S(1)}, bf16[64,1280]{1,0:T(8,128)(2,1)S(1)}, u32[]{:S(2)}, u32[]{:S(2)}) collective-permute-start(bf16[64,1280]{1,0:T(8,128)(2,1)S(1)} %collective-permute-done.3.refs_6_), channel_id=1, source_target_pairs={{0,1},{1,2},{2,3},{3,0},{4,5},{5,6},{6,7},{7,4},{8,9},{9,10},{10,1... | collective-permute-start | bytes 491528 | tf_op jit(solution)/shard_map/ppermute | solution.py:498
  38.2 13.2 %copy-start.16 = (s32[64]{0:T(128)S(1)}, s32[64]{0:T(128)}, u32[]{:S(2)}) copy-start(s32[64]{0:T(128)} %doc_ids.1) | copy-start | bytes 772
  38.2 13.2 %copy-start.17 = (s32[2]{0:T(128)S(1)}, s32[2]{0:T(128)}, u32[]{:S(2)}) copy-start(s32[2]{0:T(128)} %resp_len.3) | copy-start | bytes 28
  46.3 0.9 copy-start.8
  47.2 0.9 copy-start.10
  48.4 3.0 %copy-start.19 = (bf16[2,128,512]{2,1,0:T(8,128)(2,1)S(1)}, bf16[2,128,512]{2,1,0:T(8,128)(2,1)}, u32[]{:S(2)}) copy-start(bf16[2,128,512]{2,1,0:T(8,128)(2,1)} %get-tuple-element.53.turned_in) | copy-start | bytes 786436
  48.5 17.6 %copy-start.18 = (bf16[2,512,128]{2,1,0:T(8,128)(2,1)S(1)}, bf16[2,512,128]{2,1,0:T(8,128)(2,1)}, u32[]{:S(2)}) copy-start(bf16[2,512,128]{2,1,0:T(8,128)(2,1)} %get-tuple-element.58.rows_in) | copy-start | bytes 786436
  48.5 2.9 %collective-permute-start.7 = (bf16[16,2,144,128]{3,2,1,0:T(8,128)(2,1)S(1)}, bf16[16,2,144,128]{3,2,1,0:T(8,128)(2,1)S(1)}, u32[]{:S(2)}, u32[]{:S(2)}) collective-permute-start(bf16[16,2,144,128]{3,2,1,0:T(8,128)(2,1)S(1)} %slice.39), channel_id=1, source_target_pairs={{0,128},{128,0},{1,129},{129,1},{2,130},{130,2},{3,131},{131,3},{4... | collective-permute-start | bytes 3538952 | tf_op jit(solution)/shard_map/ppermute | solution.py:543
  66.1 3.7 %copy-start.1 = (bf16[128,1280]{1,0:T(8,128)(2,1)}, bf16[128,1280]{1,0:T(8,128)(2,1)S(1)}, u32[]{:S(2)}) copy-start(bf16[128,1280]{1,0:T(8,128)(2,1)S(1)} %get-tuple-element.55) | copy-start | bytes 983044
  66.1 3.7 %copy-start.3 = (bf16[128,1280]{1,0:T(8,128)(2,1)}, bf16[128,1280]{1,0:T(8,128)(2,1)S(1)}, u32[]{:S(2)}) copy-start(bf16[128,1280]{1,0:T(8,128)(2,1)S(1)} %get-tuple-element.56) | copy-start | bytes 983044
  66.1 3.7 %copy-start.5 = (bf16[128,1280]{1,0:T(8,128)(2,1)}, bf16[128,1280]{1,0:T(8,128)(2,1)S(1)}, u32[]{:S(2)}) copy-start(bf16[128,1280]{1,0:T(8,128)(2,1)S(1)} %get-tuple-element.69) | copy-start | bytes 983044
  66.1 3.7 %copy-start.12 = (bf16[64,1280]{1,0:T(8,128)(2,1)}, bf16[64,1280]{1,0:T(8,128)(2,1)S(1)}, u32[]{:S(2)}) copy-start(bf16[64,1280]{1,0:T(8,128)(2,1)S(1)} %get-tuple-element.68) | copy-start | bytes 491524
  66.2 3.7 %copy-start.14 = (bf16[64,1280]{1,0:T(8,128)(2,1)}, bf16[64,1280]{1,0:T(8,128)(2,1)S(1)}, u32[]{:S(2)}) copy-start(bf16[64,1280]{1,0:T(8,128)(2,1)S(1)} %get-tuple-element.70) | copy-start | bytes 491524
  69.9 12.6 %collective-permute-start.8 = (bf16[16,2,128,128]{3,2,1,0:T(8,128)(2,1)S(1)}, bf16[16,2,128,128]{3,2,1,0:T(8,128)(2,1)S(1)}, u32[]{:S(2)}, u32[]{:S(2)}) collective-permute-start(bf16[16,2,128,128]{3,2,1,0:T(8,128)(2,1)S(1)} %get-tuple-element.65), channel_id=1, source_target_pairs={{0,128},{128,0},{1,129},{129,1},{2,130},{130,2},{3,131},{131,3},{4... | collective-permute-start | bytes 3145736 | tf_op jit(solution)/shard_map/ppermute | solution.py:578
  83.0 1.4 %copy-start = (bf16[16,2,256,128]{3,2,1,0:T(8,128)(2,1)}, bf16[16,2,256,128]{3,2,1,0:T(8,128)(2,1)S(1)}, u32[]{:S(2)}) copy-start(bf16[16,2,256,128]{3,2,1,0:T(8,128)(2,1)S(1)} %fusion) | copy-start | bytes 6291460
  84.4 4.6 %copy-start.15 = (bf16[64,1280]{1,0:T(8,128)(2,1)S(1)}, bf16[64,1280]{1,0:T(8,128)(2,1)}, u32[]{:S(2)}) copy-start(bf16[64,1280]{1,0:T(8,128)(2,1)} %copy-done.14) | copy-start | bytes 491524
  84.4 8.4 %copy-start.13 = (bf16[64,1280]{1,0:T(8,128)(2,1)S(1)}, bf16[64,1280]{1,0:T(8,128)(2,1)}, u32[]{:S(2)}) copy-start(bf16[64,1280]{1,0:T(8,128)(2,1)} %copy-done.12) | copy-start | bytes 491524
  84.4 14.5 %copy-start.6 = (bf16[128,1280]{1,0:T(8,128)(2,1)S(1)}, bf16[128,1280]{1,0:T(8,128)(2,1)}, u32[]{:S(2)}) copy-start(bf16[128,1280]{1,0:T(8,128)(2,1)} %copy-done.5) | copy-start | bytes 983044
  84.4 16.9 %copy-start.4 = (bf16[128,1280]{1,0:T(8,128)(2,1)S(1)}, bf16[128,1280]{1,0:T(8,128)(2,1)}, u32[]{:S(2)}) copy-start(bf16[128,1280]{1,0:T(8,128)(2,1)} %copy-done.3) | copy-start | bytes 983044
  84.4 30.7 %copy-start.2 = (bf16[128,1280]{1,0:T(8,128)(2,1)S(1)}, bf16[128,1280]{1,0:T(8,128)(2,1)}, u32[]{:S(2)}) copy-start(bf16[128,1280]{1,0:T(8,128)(2,1)} %copy-done.1) | copy-start | bytes 983044
  84.4 35.4 %all-to-all-start.1 = ((bf16[16,2,256,128]{3,2,1,0:T(8,128)(2,1)}), bf16[16,2,256,128]{3,2,1,0:T(8,128)(2,1)S(1)}, u32[]{:S(2)}, u32[]{:S(2)}) async-start(bf16[16,2,256,128]{3,2,1,0:T(8,128)(2,1)} %copy-done), calls=%async_computation.1 | async-start | bytes 4194304 | tf_op jit(solution)/shard_map/all_to_all | solution.py:588
  89.0 9.9 %collective-permute-start.11 = (bf16[64,1280]{1,0:T(8,128)(2,1)S(1)}, bf16[64,1280]{1,0:T(8,128)(2,1)S(1)}, u32[]{:S(2)}, u32[]{:S(2)}) collective-permute-start(bf16[64,1280]{1,0:T(8,128)(2,1)S(1)} %copy-done.15), channel_id=1, source_target_pairs={{0,3},{1,0},{2,1},{3,2},{4,7},{5,4},{6,5},{7,6},{8,11},{9,8},{10,9... | collective-permute-start | bytes 491528 | tf_op jit(solution)/shard_map/ppermute | solution.py:498
  92.8 8.5 %collective-permute-start.9 = (bf16[64,1280]{1,0:T(8,128)(2,1)S(1)}, bf16[64,1280]{1,0:T(8,128)(2,1)S(1)}, u32[]{:S(2)}, u32[]{:S(2)}) collective-permute-start(bf16[64,1280]{1,0:T(8,128)(2,1)S(1)} %copy-done.13), channel_id=1, source_target_pairs={{0,1},{1,2},{2,3},{3,0},{4,5},{5,6},{6,7},{7,4},{8,9},{9,10},{10,1... | collective-permute-start | bytes 491528 | tf_op jit(solution)/shard_map/ppermute | solution.py:498
  99.0 14.8 %collective-permute-start.12 = (bf16[128,1280]{1,0:T(8,128)(2,1)S(1)}, bf16[128,1280]{1,0:T(8,128)(2,1)S(1)}, u32[]{:S(2)}, u32[]{:S(2)}) collective-permute-start(bf16[128,1280]{1,0:T(8,128)(2,1)S(1)} %add_convert_fusion.2), channel_id=1, source_target_pairs={{0,3},{1,0},{2,1},{3,2},{4,7},{5,4},{6,5},{7,6},{8,11},{9,8},{10,9... | collective-permute-start | bytes 983048 | tf_op jit(solution)/shard_map/ppermute | solution.py:498
  101.3 13.8 %collective-permute-start.10 = (bf16[128,1280]{1,0:T(8,128)(2,1)S(1)}, bf16[128,1280]{1,0:T(8,128)(2,1)S(1)}, u32[]{:S(2)}, u32[]{:S(2)}) collective-permute-start(bf16[128,1280]{1,0:T(8,128)(2,1)S(1)} %add_convert_fusion.3), channel_id=1, source_target_pairs={{0,1},{1,2},{2,3},{3,0},{4,5},{5,6},{6,7},{7,4},{8,9},{9,10},{10,1... | collective-permute-start | bytes 983048 | tf_op jit(solution)/shard_map/ppermute | solution.py:498
  120.1 4.4 %collective-permute-start.13 = (bf16[256,128]{1,0:T(8,128)(2,1)S(1)}, bf16[256,128]{1,0:T(8,128)(2,1)S(1)}, u32[]{:S(2)}, u32[]{:S(2)}) collective-permute-start(bf16[256,128]{1,0:T(8,128)(2,1)S(1)} %get-tuple-element.74), channel_id=1, source_target_pairs={{0,64},{64,0},{1,65},{65,1},{2,66},{66,2},{3,67},{67,3},{4,68},{68... | collective-permute-start | bytes 196616 | tf_op jit(solution)/shard_map/ppermute | solution.py:598
